TPU v7x, 1024 devices: a whole 4x8x16 slice. The times are simulated.
1024 devices in a mesh: comp: 32 (over z_hi, x, core), space: 32 (over z_lo, y).
Axes of the slice: x: 4, y: 8, z: 16 (z_hi: 4, z_lo: 4; z = z_hi * 4 + z_lo), core: 2. Of those that a mesh axis runs over, the one named last changes fastest.
Arguments:
- spectrum: float32 [288, 1024, 1024], P('comp', 'space'), may hold values from 0.01 to 1
- sea_mask: int32 [1024, 1024], P('space'), may hold values 0 or 1
- ice_flag: int32 [1024, 1024], P('space'), may hold values 0 or 1
- thickness: float32 [1024, 1024], P('space'), may hold values from 0.1 to 3
Outputs:
- updated: float32 [288, 1024, 1024], P('comp', 'space')
All inputs are finite; a program needn't handle non-finite values. No bound on the sum of `sea_mask` or of `ice_flag` on one device may be relied on, other than what follows from the above.
Results may differ from a plain program's by a relative error of at most 0.00002.
Values sent between devices are 32-bit elements; how exact they have to be, the bound alone decides.
No kernel may reach another device: no remote copies, remote signals or barrier semaphores. Data moves between devices by JAX's collectives and lax.ppermute only.
A program may use at most 32 MiB of HBM per device.

v0:
```python
import math

import jax
import jax.numpy as jnp
from jax import lax
from jax.sharding import PartitionSpec as P

ND = 36
NF = 8
PSTEPS = 4


courant_top = 0.65
mixing_rate = 0.5
whitecap_rate = 2.0
ice_rate = 0.3


def extended(cells, sides, width):
    for axis, dim in sides:
        count = lax.axis_size(axis)
        ends = count - 1
        head = lax.slice_in_dim(cells, 0, width, axis=dim)
        tail = lax.slice_in_dim(cells, cells.shape[dim] - width, cells.shape[dim], axis=dim)
        cells = jnp.concatenate(
            [
                lax.ppermute(tail, axis, [(i, (i + 1) % count) for i in range(ends)]),
                cells,
                lax.ppermute(head, axis, [((i + 1) % count, i) for i in range(ends)]),
            ],
            axis=dim,
        )
    return cells


def comp_tables(first, count):
    index = first + jnp.arange(count, dtype=jnp.int32)
    freq_index = index // ND
    dir_index = index % ND
    ratio = jnp.power(jnp.float32(1.1), freq_index.astype(jnp.float32))
    courant = courant_top / ratio
    theta = (dir_index.astype(jnp.float32) + 0.5) * (2.0 * math.pi / ND)
    return (courant * jnp.cos(theta), courant * jnp.sin(theta), ratio * ratio)


def upwind(framed, speed_x, speed_y):
    middle = framed[:, 1:-1, 1:-1]
    west = framed[:, 1:-1, :-2]
    east = framed[:, 1:-1, 2:]
    south = framed[:, :-2, 1:-1]
    north = framed[:, 2:, 1:-1]
    to_east = jnp.maximum(speed_x, 0.0)[:, None, None]
    to_west = jnp.maximum(-speed_x, 0.0)[:, None, None]
    to_north = jnp.maximum(speed_y, 0.0)[:, None, None]
    to_south = jnp.maximum(-speed_y, 0.0)[:, None, None]
    return (
        middle
        - to_east * (middle - west)
        - to_west * (middle - east)
        - to_north * (middle - south)
        - to_south * (middle - north)
    )


def shift_freq(values, offset):
    zeros = jnp.zeros((abs(offset),) + values.shape[1:], values.dtype)
    if offset > 0:
        return jnp.concatenate([values[offset:], zeros], axis=0)
    return jnp.concatenate([zeros, values[:offset]], axis=0)


def source_mix(points):
    shaped = points.reshape((NF, ND) + points.shape[1:])
    neighbours = shift_freq(jnp.roll(shaped, -3, axis=1), 2) + shift_freq(
        jnp.roll(shaped, 3, axis=1), 2
    )
    neighbours = (
        neighbours
        + shift_freq(jnp.roll(shaped, -1, axis=1), -2)
        + shift_freq(jnp.roll(shaped, 1, axis=1), -2)
    )
    mixed = shaped + mixing_rate * shaped * (0.25 * neighbours - shaped)
    energy = jnp.mean(mixed, axis=(0, 1))
    ratio = jnp.power(jnp.float32(1.1), jnp.arange(NF, dtype=jnp.int32).astype(jnp.float32))
    weight = (ratio * ratio).reshape((NF, 1) + (1,) * (points.ndim - 1))
    return (mixed / (1.0 + whitecap_rate * energy[None, None] * weight)).reshape(points.shape)


def body(spectrum, sea_mask, ice_flag, thickness):
    local_comps = spectrum.shape[0]
    first = lax.axis_index("comp") * local_comps
    speed_x, speed_y, freq_sq = comp_tables(first, local_comps)
    land = sea_mask.astype(jnp.float32)
    field = spectrum * land[None]
    for repeat in range(PSTEPS):
        edged = extended(field, (("space", 1),), 1)
        framed = jnp.pad(edged, ((0, 0), (0, 0), (1, 1)))
        field = upwind(framed, speed_x, speed_y) * land[None]
    points = lax.all_to_all(field, "comp", split_axis=1, concat_axis=0, tiled=True)
    mixed = source_mix(points)
    settled = lax.all_to_all(mixed, "comp", split_axis=0, concat_axis=1, tiled=True)
    ice_depth = ice_flag.astype(jnp.float32) * thickness
    return settled * jnp.exp(-ice_rate * ice_depth[None] * freq_sq[:, None, None])


def solution(mesh):
    in_specs = (P("comp", "space", None), P("space", None), P("space", None), P("space", None))
    out_specs = P("comp", "space", None)
    return jax.shard_map(body, mesh=mesh, in_specs=in_specs, out_specs=out_specs, check_vma=False)
```

profile of v0, /device:TPU:6, one launch (start us, length us, event | category | flops | bytes accessed | tf_op | source)
XLA Modules:
  0.0 255.6 jit_solution(4181972477178198981)
XLA Ops:
  0.0 0.9 convert_element_type.53
  0.9 2.0 copy_multiply_fusion
  3.0 3.5 %collective-permute-start = (f32[9,1,1024]{2,0,1:T(8,128)S(1)}, f32[9,1,1024]{2,0,1:T(8,128)S(1)}, u32[]{:S(2)}, u32[]{:S(2)}) collective-permute-start(f32[9,1,1024]{2,0,1:T(8,128)S(1)} %get-tuple-element.13), channel_id=1, source_target_pairs={{0,1},{1,2},{2,3},{3,4},{4,5},{5,6},{6,7},{7,8},{8,9},{9,10},{10,1... | collective-permute-start | bytes 110600 | tf_op jit(solution)/shard_map/ppermute | solution.py:27
  6.5 1.3 collective-permute-start.1
  7.8 0.1 negate_maximum_fusion
  7.8 0.1 broadcast_maximum_fusion
  7.9 0.5 collective-permute-done
  8.3 4.3 %collective-permute-done.1 = f32[9,1,1024]{2,0,1:T(8,128)S(1)} collective-permute-done((f32[9,1,1024]{2,0,1:T(8,128)S(1)}, f32[9,1,1024]{2,0,1:T(8,128)S(1)}, u32[]{:S(2)}, u32[]{:S(2)}) %collective-permute-start.1) | collective-permute-done | bytes 36896 | tf_op jit(solution)/shard_map/ppermute | solution.py:29
  12.6 0.7 select_maximum_fusion.6
  13.3 1.8 fusion.37
  15.1 3.5 %collective-permute-start.2 = (f32[9,1,1024]{2,0,1:T(8,128)S(1)}, f32[9,1,1024]{2,0,1:T(8,128)S(1)}, u32[]{:S(2)}, u32[]{:S(2)}) collective-permute-start(f32[9,1,1024]{2,0,1:T(8,128)S(1)} %get-tuple-element.11), channel_id=1, source_target_pairs={{0,1},{1,2},{2,3},{3,4},{4,5},{5,6},{6,7},{7,8},{8,9},{9,10},{10,1... | collective-permute-start | bytes 110600 | tf_op jit(solution)/shard_map/ppermute | solution.py:27
  18.6 1.3 collective-permute-start.3
  19.9 0.6 collective-permute-done.2
  20.5 4.6 %collective-permute-done.3 = f32[9,1,1024]{2,0,1:T(8,128)S(1)} collective-permute-done((f32[9,1,1024]{2,0,1:T(8,128)S(1)}, f32[9,1,1024]{2,0,1:T(8,128)S(1)}, u32[]{:S(2)}, u32[]{:S(2)}) %collective-permute-start.3) | collective-permute-done | bytes 36896 | tf_op jit(solution)/shard_map/ppermute | solution.py:29
  25.1 0.7 select_maximum_fusion.4
  25.8 1.8 fusion.26
  27.7 5.1 %collective-permute-start.4 = (f32[9,1,1024]{2,0,1:T(8,128)S(1)}, f32[9,1,1024]{2,0,1:T(8,128)S(1)}, u32[]{:S(2)}, u32[]{:S(2)}) collective-permute-start(f32[9,1,1024]{2,0,1:T(8,128)S(1)} %get-tuple-element.9), channel_id=1, source_target_pairs={{0,1},{1,2},{2,3},{3,4},{4,5},{5,6},{6,7},{7,8},{8,9},{9,10},{10,1... | collective-permute-start | bytes 110600 | tf_op jit(solution)/shard_map/ppermute | solution.py:27
  32.8 1.3 collective-permute-start.5
  34.1 0.6 collective-permute-done.4
  34.7 4.3 %collective-permute-done.5 = f32[9,1,1024]{2,0,1:T(8,128)S(1)} collective-permute-done((f32[9,1,1024]{2,0,1:T(8,128)S(1)}, f32[9,1,1024]{2,0,1:T(8,128)S(1)}, u32[]{:S(2)}, u32[]{:S(2)}) %collective-permute-start.5) | collective-permute-done | bytes 36896 | tf_op jit(solution)/shard_map/ppermute | solution.py:29
  39.0 0.7 select_maximum_fusion.2
  39.7 1.8 fusion.15
  41.5 3.9 %collective-permute-start.6 = (f32[9,1,1024]{2,0,1:T(8,128)S(1)}, f32[9,1,1024]{2,0,1:T(8,128)S(1)}, u32[]{:S(2)}, u32[]{:S(2)}) collective-permute-start(f32[9,1,1024]{2,0,1:T(8,128)S(1)} %get-tuple-element.7), channel_id=1, source_target_pairs={{0,1},{1,2},{2,3},{3,4},{4,5},{5,6},{6,7},{7,8},{8,9},{9,10},{10,1... | collective-permute-start | bytes 110600 | tf_op jit(solution)/shard_map/ppermute | solution.py:27
  45.4 1.3 collective-permute-start.7
  46.7 0.6 collective-permute-done.6
  47.3 4.3 %collective-permute-done.7 = f32[9,1,1024]{2,0,1:T(8,128)S(1)} collective-permute-done((f32[9,1,1024]{2,0,1:T(8,128)S(1)}, f32[9,1,1024]{2,0,1:T(8,128)S(1)}, u32[]{:S(2)}, u32[]{:S(2)}) %collective-permute-start.7) | collective-permute-done | bytes 36896 | tf_op jit(solution)/shard_map/ppermute | solution.py:29
  51.6 0.7 select_maximum_fusion
  52.3 2.7 %fusion.4 = f32[9,32,1024]{2,0,1:T(8,128)} fusion(f32[9,32,1024]{2,0,1:T(8,128)S(1)} %fusion.15, f32[9,1,1024]{2,0,1:T(8,128)S(1)} %collective-permute-done.7, f32[9,1,1024]{2,0,1:T(8,128)S(1)} %collective-permute-done.6, f32[9,34,1026]{2,0,1:T(8,128)S(1)} %select_maximum_fusion, f32[9]{0:T(128)S(1)} %get-tuple-element.23, f32[9]{0:T(128)S(1)} %get-tuple-element.25, ...), kind=kLoop, calls=%fused_computation.15 | loop fusion | flops 4423680 | bytes 4923536 | tf_op jit(solution)/shard_map/mul | solution.py:98
  55.0 21.8 %all-to-all-start = ((f32[9,32,1024]{2,0,1:T(8,128)}), f32[9,32,1024]{2,0,1:T(8,128)S(1)}, u32[]{:S(2)}, u32[]{:S(2)}) async-start(f32[9,32,1024]{2,0,1:T(8,128)} %fusion.4), calls=%async_computation | async-start | bytes 4194304 | tf_op jit(solution)/shard_map/all_to_all | solution.py:99
  76.9 61.7 %all-to-all-done = f32[9,32,1024]{2,0,1:T(8,128)S(1)} async-done(((f32[9,32,1024]{2,0,1:T(8,128)}), f32[9,32,1024]{2,0,1:T(8,128)S(1)}, u32[]{:S(2)}, u32[]{:S(2)}) %all-to-all-start) | async-done | bytes 1179680 | tf_op jit(solution)/shard_map/all_to_all | solution.py:99
  138.6 1.4 reshape.116
  140.0 1.2 fusion.59
  141.2 1.1 fusion.57
  142.4 4.5 %fusion.52 = (f32[1024]{0:T(1024)S(1)}, f32[8,36,1,1024]{3,2,1,0:T(1,128)S(1)}) fusion(f32[8,36,1,1024]{3,2,1,0:T(1,128)S(1)} %reshape.116, f32[8,35,1,1024]{3,2,1,0:T(1,128)S(1)} %get-tuple-element.20, f32[8,1,1,1024]{3,2,1,0:T(1,128)S(1)} %get-tuple-element.22, f32[8,1,1,1024]{3,2,1,0:T(1,128)S(1)} %get-tuple-element.21, ...), kind=kLoop, calls=%fused_computation.103 | loop fusion | flops 6781952 | bytes 7081984 | tf_op jit(solution)/shard_map/reduce_sum | solution.py:83
  146.9 0.1 multiply_add_fusion.1
  147.0 0.0 copy-start
  147.0 0.0 copy-start.1
  147.0 1.9 broadcast_divide_fusion
  148.9 44.7 %all-to-all-start.1 = ((f32[288,1,1024]{2,1,0:T(1,128)}), f32[288,1,1024]{2,1,0:T(1,128)S(1)}, u32[]{:S(2)}, u32[]{:S(2)}) async-start(f32[288,1,1024]{2,1,0:T(1,128)} %bitcast.2), calls=%async_computation.1 | async-start | bytes 2359296 | tf_op jit(solution)/shard_map/all_to_all | solution.py:101
  193.6 0.0 copy-done
  193.6 0.0 copy-done.1
  193.7 60.6 %all-to-all-done.1 = f32[288,1,1024]{2,1,0:T(1,128)S(1)} async-done(((f32[288,1,1024]{2,1,0:T(1,128)}), f32[288,1,1024]{2,1,0:T(1,128)S(1)}, u32[]{:S(2)}, u32[]{:S(2)}) %all-to-all-start.1) | async-done | bytes 1179680 | tf_op jit(solution)/shard_map/all_to_all | solution.py:101
  254.3 1.4 bitcast_multiply_fusion
  (10 shorter events, 0.1 us)
Async XLA Ops:
  3.0 5.4 %collective-permute-start = (f32[9,1,1024]{2,0,1:T(8,128)S(1)}, f32[9,1,1024]{2,0,1:T(8,128)S(1)}, u32[]{:S(2)}, u32[]{:S(2)}) collective-permute-start(f32[9,1,1024]{2,0,1:T(8,128)S(1)} %get-tuple-element.13), channel_id=1, source_target_pairs={{0,1},{1,2},{2,3},{3,4},{4,5},{5,6},{6,7},{7,8},{8,9},{9,10},{10,1... | collective-permute-start | bytes 110600 | tf_op jit(solution)/shard_map/ppermute | solution.py:27
  6.5 6.2 %collective-permute-start.1 = (f32[9,1,1024]{2,0,1:T(8,128)S(1)}, f32[9,1,1024]{2,0,1:T(8,128)S(1)}, u32[]{:S(2)}, u32[]{:S(2)}) collective-permute-start(f32[9,1,1024]{2,0,1:T(8,128)S(1)} %get-tuple-element.14), channel_id=1, source_target_pairs={{1,0},{2,1},{3,2},{4,3},{5,4},{6,5},{7,6},{8,7},{9,8},{10,9},{11,1... | collective-permute-start | bytes 110600 | tf_op jit(solution)/shard_map/ppermute | solution.py:29
  15.1 5.4 %collective-permute-start.2 = (f32[9,1,1024]{2,0,1:T(8,128)S(1)}, f32[9,1,1024]{2,0,1:T(8,128)S(1)}, u32[]{:S(2)}, u32[]{:S(2)}) collective-permute-start(f32[9,1,1024]{2,0,1:T(8,128)S(1)} %get-tuple-element.11), channel_id=1, source_target_pairs={{0,1},{1,2},{2,3},{3,4},{4,5},{5,6},{6,7},{7,8},{8,9},{9,10},{10,1... | collective-permute-start | bytes 110600 | tf_op jit(solution)/shard_map/ppermute | solution.py:27
  18.6 6.5 %collective-permute-start.3 = (f32[9,1,1024]{2,0,1:T(8,128)S(1)}, f32[9,1,1024]{2,0,1:T(8,128)S(1)}, u32[]{:S(2)}, u32[]{:S(2)}) collective-permute-start(f32[9,1,1024]{2,0,1:T(8,128)S(1)} %get-tuple-element.12), channel_id=1, source_target_pairs={{1,0},{2,1},{3,2},{4,3},{5,4},{6,5},{7,6},{8,7},{9,8},{10,9},{11,1... | collective-permute-start | bytes 110600 | tf_op jit(solution)/shard_map/ppermute | solution.py:29
  27.7 7.0 %collective-permute-start.4 = (f32[9,1,1024]{2,0,1:T(8,128)S(1)}, f32[9,1,1024]{2,0,1:T(8,128)S(1)}, u32[]{:S(2)}, u32[]{:S(2)}) collective-permute-start(f32[9,1,1024]{2,0,1:T(8,128)S(1)} %get-tuple-element.9), channel_id=1, source_target_pairs={{0,1},{1,2},{2,3},{3,4},{4,5},{5,6},{6,7},{7,8},{8,9},{9,10},{10,1... | collective-permute-start | bytes 110600 | tf_op jit(solution)/shard_map/ppermute | solution.py:27
  32.8 6.2 %collective-permute-start.5 = (f32[9,1,1024]{2,0,1:T(8,128)S(1)}, f32[9,1,1024]{2,0,1:T(8,128)S(1)}, u32[]{:S(2)}, u32[]{:S(2)}) collective-permute-start(f32[9,1,1024]{2,0,1:T(8,128)S(1)} %get-tuple-element.10), channel_id=1, source_target_pairs={{1,0},{2,1},{3,2},{4,3},{5,4},{6,5},{7,6},{8,7},{9,8},{10,9},{11,1... | collective-permute-start | bytes 110600 | tf_op jit(solution)/shard_map/ppermute | solution.py:29
  41.5 5.8 %collective-permute-start.6 = (f32[9,1,1024]{2,0,1:T(8,128)S(1)}, f32[9,1,1024]{2,0,1:T(8,128)S(1)}, u32[]{:S(2)}, u32[]{:S(2)}) collective-permute-start(f32[9,1,1024]{2,0,1:T(8,128)S(1)} %get-tuple-element.7), channel_id=1, source_target_pairs={{0,1},{1,2},{2,3},{3,4},{4,5},{5,6},{6,7},{7,8},{8,9},{9,10},{10,1... | collective-permute-start | bytes 110600 | tf_op jit(solution)/shard_map/ppermute | solution.py:27
  45.4 6.2 %collective-permute-start.7 = (f32[9,1,1024]{2,0,1:T(8,128)S(1)}, f32[9,1,1024]{2,0,1:T(8,128)S(1)}, u32[]{:S(2)}, u32[]{:S(2)}) collective-permute-start(f32[9,1,1024]{2,0,1:T(8,128)S(1)} %get-tuple-element.8), channel_id=1, source_target_pairs={{1,0},{2,1},{3,2},{4,3},{5,4},{6,5},{7,6},{8,7},{9,8},{10,9},{11,1... | collective-permute-start | bytes 110600 | tf_op jit(solution)/shard_map/ppermute | solution.py:29
  55.0 83.5 %all-to-all-start = ((f32[9,32,1024]{2,0,1:T(8,128)}), f32[9,32,1024]{2,0,1:T(8,128)S(1)}, u32[]{:S(2)}, u32[]{:S(2)}) async-start(f32[9,32,1024]{2,0,1:T(8,128)} %fusion.4), calls=%async_computation | async-start | bytes 4194304 | tf_op jit(solution)/shard_map/all_to_all | solution.py:99
  147.0 46.6 %copy-start = (f32[32,1024]{1,0:T(8,128)S(1)}, f32[32,1024]{1,0:T(8,128)}, u32[]{:S(2)}) copy-start(f32[32,1024]{1,0:T(8,128)} %param.7) | copy-start | bytes 393220
  147.0 46.6 %copy-start.1 = (s32[32,1024]{1,0:T(8,128)S(1)}, s32[32,1024]{1,0:T(8,128)}, u32[]{:S(2)}) copy-start(s32[32,1024]{1,0:T(8,128)} %param.6) | copy-start | bytes 393220
  148.9 105.4 %all-to-all-start.1 = ((f32[288,1,1024]{2,1,0:T(1,128)}), f32[288,1,1024]{2,1,0:T(1,128)S(1)}, u32[]{:S(2)}, u32[]{:S(2)}) async-start(f32[288,1,1024]{2,1,0:T(1,128)} %bitcast.2), calls=%async_computation.1 | async-start | bytes 2359296 | tf_op jit(solution)/shard_map/all_to_all | solution.py:101
where the time goes:
time: 256 us
  waiting for transfers between devices  142 us (55%)
  starting transfers between devices  87.8 us (34%)
  other arithmetic  21.9 us (9%)
  local copies, waits for them, and re-layouts  3.83 us (1%)
    all_to_all x1, waiting for transfers between devices, body(): lax.all_to_all(field, 'comp', split_axis=1, concat_axis=0, tiled=True)  61.7 us
    all_to_all x1, waiting for transfers between devices, body(): lax.all_to_all(mixed, 'comp', split_axis=0, concat_axis=1, tiled=True)  60.6 us
    all_to_all x1, starting transfers between devices, body(): lax.all_to_all(mixed, 'comp', split_axis=0, concat_axis=1, tiled=True)  44.7 us
    all_to_all x1, starting transfers between devices, body(): lax.all_to_all(field, 'comp', split_axis=1, concat_axis=0, tiled=True)  21.8 us
    ppermute x4, waiting for transfers between devices, extended(): lax.ppermute(head, axis, [((i + 1) % count, i) for i in range(ends)])  17.4 us
    ppermute x4, starting transfers between devices, extended(): lax.ppermute(tail, axis, [(i, (i + 1) % count) for i in range(ends)])  16 us
    mul x4, other arithmetic, body(): field = upwind(framed, speed_x, speed_y) * land[None]  8.08 us
    ppermute x4, starting transfers between devices, extended(): lax.ppermute(head, axis, [((i + 1) % count, i) for i in range(ends)])  5.17 us
  transfers between devices with their start and end apart: 10, of which 10 were waited for; matrix products, arithmetic and copies ran while one was open for 0% of the time, Pallas kernels for 0%

commit v1 on v0

v1 whole, which is shorter than its diff:
```python
import functools
import math

import jax
import jax.numpy as jnp
import numpy as np
from jax import lax
from jax.experimental import pallas as pl
from jax.experimental.pallas import tpu as pltpu
from jax.sharding import PartitionSpec as P

ND = 36
NF = 8
PSTEPS = 4
QUARTERS = 4
NQ = ND // QUARTERS
GROUP = 8
EDGE = 3

courant_top = 0.65
mixing_rate = 0.5
whitecap_rate = 2.0
ice_rate = 0.3

VMEM_BYTES = 40 * 1024 * 1024


def tables():
    rows = np.zeros((NF * QUARTERS, 2 * NQ + 2), np.float32)
    for p in range(NF * QUARTERS):
        ratio = 1.1 ** (p // QUARTERS)
        for i in range(NQ):
            theta = 2.0 * math.pi * ((p % QUARTERS) * NQ + i + 0.5) / ND
            rows[p, i] = abs(courant_top / ratio * math.cos(theta))
            rows[p, NQ + i] = abs(courant_top / ratio * math.sin(theta))
        rows[p, 2 * NQ] = ratio * ratio
    return rows


def quarter():
    return lax.rem(lax.axis_index("comp"), QUARTERS)


def edge_rows(first_ref, last_ref, first_mask, last_mask, out_ref):
    def write(field_ref, mask_ref, low):
        land = mask_ref[low : low + PSTEPS].astype(jnp.float32)
        for i in range(NQ):
            out_ref[PSTEPS * i : PSTEPS * (i + 1)] = field_ref[i, low : low + PSTEPS] * land
        out_ref[PSTEPS * NQ :] = land

    @pl.when(quarter() < 2)
    def _():
        write(last_ref, last_mask, 8 - PSTEPS)

    @pl.when(quarter() >= 2)
    def _():
        write(first_ref, first_mask, 0)


def propagate(table_ref, field_ref, mask_ref, halo_ref, a_ref, b_ref, lo_ref, hi_ref, land, ext):
    p = lax.axis_index("comp")
    q = lax.rem(p, QUARTERS)
    rows, cols = mask_ref.shape
    half = rows // 2
    high = rows + 8

    def run(eastward, northward):
        own = 8 if northward else 0
        halo = 8 - PSTEPS if northward else rows
        rest = 0 if northward else rows + PSTEPS
        zeros = jnp.zeros((8 - PSTEPS, cols), jnp.float32)
        land[own : own + rows] = mask_ref[...].astype(jnp.float32)
        land[halo : halo + PSTEPS] = halo_ref[PSTEPS * NQ :]
        land[rest : rest + 8 - PSTEPS] = zeros
        ext[rest : rest + 8 - PSTEPS] = zeros
        column = lax.broadcasted_iota(jnp.int32, (1, cols), 1)
        inner = (column != (0 if eastward else cols - 1)).astype(jnp.float32)

        def component(i, carry):
            ext[own : own + rows] = field_ref[i] * land[own : own + rows]
            for r in range(PSTEPS):
                ext[halo + r : halo + r + 1] = halo_ref[pl.ds(PSTEPS * i + r, 1)]
            ax = table_ref[p, i]
            ay = table_ref[p, NQ + i]
            stay = 1.0 - ax - ay
            side = inner * ax
            f = ext[...]
            for _ in range(PSTEPS):
                along = pltpu.roll(f, 1 if eastward else cols - 1, 1)
                across = pltpu.roll(f, 1 if northward else high - 1, 0)
                f = (stay * f + side * along + ay * across) * land[...]
            a_ref[i] = f[own : own + half]
            b_ref[i] = f[own + half : own + rows]

            @pl.when(i < EDGE)
            def _():
                lo_ref[i] = f[own : own + rows]

            @pl.when(i >= NQ - EDGE)
            def _():
                hi_ref[i - (NQ - EDGE)] = f[own : own + rows]

            return carry

        lax.fori_loop(0, NQ, component, 0)

    for k, (eastward, northward) in enumerate(
        ((True, True), (False, True), (False, False), (True, False))
    ):
        pl.when(q == k)(functools.partial(run, eastward, northward))


def at(low_ref, mid_ref, top_ref, i, rows, low_rows):
    if i < 0:
        return low_ref[i + EDGE, low_rows]
    if i >= NQ:
        return top_ref[i - NQ, low_rows]
    return mid_ref[i, rows]


def sums(a_ref, b_ref, low_ref, top_ref, s1_ref, s3_ref):
    half = a_ref.shape[1]
    for t in range(0, half, 8):
        rows = pl.ds(t, 8)
        a = lambda i: at(low_ref, a_ref, top_ref, i, rows, rows)
        b = lambda i: at(low_ref, b_ref, top_ref, i, rows, pl.ds(half + t, 8))
        for i in range(NQ):
            s1_ref[i, rows] = a(i - 1) + a(i + 1)
            s3_ref[i, rows] = b(i - 3) + b(i + 3)


def partial_energy(a_ref, b_ref, low_ref, top_ref, u_ref, d_ref, out_ref, prev_ref, next_ref):
    half, cols = a_ref.shape[1:]
    width = cols // GROUP
    for t in range(0, 2 * half, 8):
        mid, other, s = (a_ref, u_ref, t) if t < half else (b_ref, d_ref, t - half)
        e = lambda i: at(low_ref, mid, top_ref, i, pl.ds(s, 8), pl.ds(t, 8))
        total = jnp.zeros((8, cols), jnp.float32)
        for i in range(NQ):
            around = (e(i - 3) + e(i + 3)) + (e(i - 1) + e(i + 1))
            crossed = 0.25 * mixing_rate * other[i, pl.ds(s, 8)] * around
            total = total + (e(i) - mixing_rate * e(i) * e(i) + crossed)
        for g in range(GROUP):
            out_ref[g, t : t + 8] = total[:, g * width : (g + 1) * width]
    prev_ref[:EDGE] = u_ref[:EDGE]
    prev_ref[EDGE] = d_ref[0]
    next_ref[:EDGE] = u_ref[NQ - EDGE :]
    next_ref[EDGE] = d_ref[NQ - 1]


def finish(table_ref, a_ref, b_ref, u_ref, d_ref, low_ref, top_ref, s1_ref, s3_ref, energy_ref, ice_ref, thick_ref, out_ref):
    p = lax.axis_index("comp")
    fsq = table_ref[p, 2 * NQ]
    half = a_ref.shape[1]
    for t in range(0, 2 * half, 8):
        rows = pl.ds(t, 8)
        energy = jnp.concatenate([energy_ref[g, rows] for g in range(GROUP)], axis=1) * (1.0 / (ND * NF))
        depth = ice_ref[rows].astype(jnp.float32) * thick_ref[rows]
        factor = jnp.exp(-ice_rate * depth * fsq) / (1.0 + whitecap_rate * energy * fsq)
        for i in range(NQ):
            if t < half:
                e = a_ref[i, rows]
                u = lambda k: at(low_ref, u_ref, top_ref, k, rows, rows)
                near = s1_ref[i, rows] + (u(i - 3) + u(i + 3))
            else:
                s = pl.ds(t - half, 8)
                e = b_ref[i, s]
                d = lambda k: (
                    low_ref[EDGE, s] if k < 0 else top_ref[EDGE, s] if k >= NQ else d_ref[k, s]
                )
                near = s3_ref[i, s] + (d(i - 1) + d(i + 1))
            out_ref[i, rows] = (e + mixing_rate * e * (0.25 * near - e)) * factor


def in_vmem(count):
    return [pl.BlockSpec(memory_space=pltpu.VMEM)] * count


def in_smem():
    return [pl.BlockSpec(memory_space=pltpu.SMEM)]


def call(kernel, outs, table, count, scratch=()):
    shapes = [jax.ShapeDtypeStruct(s, jnp.float32) for s in outs]
    specs = in_vmem(len(outs))
    return pl.pallas_call(
        kernel,
        out_shape=shapes,
        in_specs=(in_smem() if table else []) + in_vmem(count),
        out_specs=specs,
        scratch_shapes=list(scratch),
        compiler_params=pltpu.CompilerParams(vmem_limit_bytes=VMEM_BYTES),
        name=kernel.__name__,
    )


def body(spectrum, sea_mask, ice_flag, thickness):
    comps, rows, cols = spectrum.shape
    half = rows // 2
    n_comp = lax.axis_size("comp")
    n_space = lax.axis_size("space")
    table = jnp.asarray(tables())

    def move(value, step):
        pairs = [(p, p + step) for p in range(n_comp) if 0 <= p + step < n_comp]
        return lax.ppermute(value, "comp", pairs)

    def turn(value, step):
        pairs = [(p, p // QUARTERS * QUARTERS + (p + step) % QUARTERS) for p in range(n_comp)]
        return lax.ppermute(value, "comp", pairs)

    message = pl.pallas_call(
        edge_rows,
        grid=(1,),
        out_shape=jax.ShapeDtypeStruct((PSTEPS * (comps + 1), cols), jnp.float32),
        in_specs=[
            pl.BlockSpec((comps, 8, cols), lambda g: (0, 0, 0)),
            pl.BlockSpec((comps, 8, cols), lambda g: (0, rows // 8 - 1, 0)),
            pl.BlockSpec((8, cols), lambda g: (0, 0)),
            pl.BlockSpec((8, cols), lambda g: (rows // 8 - 1, 0)),
        ],
        out_specs=pl.BlockSpec((PSTEPS * (comps + 1), cols), lambda g: (0, 0)),
        name="edge_rows",
    )(spectrum, spectrum, sea_mask, sea_mask)
    pairs = []
    for p in range(n_comp):
        step = 1 if p % QUARTERS < 2 else -1
        pairs += [
            (p * n_space + s, p * n_space + s + step) for s in range(n_space) if 0 <= s + step < n_space
        ]
    halo = lax.ppermute(message, ("comp", "space"), pairs)

    part = (comps, half, cols)
    edge = (EDGE, rows, cols)
    a, b, lo, hi = call(
        propagate,
        [part, part, edge, edge],
        True,
        3,
        [pltpu.VMEM((rows + 8, cols), jnp.float32), pltpu.VMEM((rows + 8, cols), jnp.float32)],
    )(table, spectrum, sea_mask, halo)

    u = move(a, -GROUP)
    d = move(b, GROUP)
    top = turn(lo, -1)
    low = turn(hi, 1)
    s1, s3 = call(sums, [part, part], False, 4)(a, b, low, top)
    s1 = move(s1, GROUP)
    s3 = move(s3, -GROUP)

    edges = (EDGE + 1, half, cols)
    share, to_prev, to_next = call(
        partial_energy, [(GROUP, rows, cols // GROUP), edges, edges], False, 6
    )(a, b, low, top, u, d)
    top_u = turn(to_prev, -1)
    low_u = turn(to_next, 1)

    near = [list(range(g, g + GROUP)) for g in range(0, n_comp, GROUP)]
    far = [list(range(g, n_comp, GROUP)) for g in range(GROUP)]

    def swap(value, groups):
        return lax.all_to_all(value, "comp", 0, 0, axis_index_groups=groups, tiled=True)

    share = jnp.sum(swap(share, near), axis=0)
    share = swap(jnp.broadcast_to(share[None], (n_comp // GROUP,) + share.shape), far)
    share = jnp.sum(share, axis=0)
    energy = swap(jnp.broadcast_to(share[None], (GROUP,) + share.shape), near)

    (out,) = call(finish, [(comps, rows, cols)], True, 11)(
        table, a, b, u, d, low_u, top_u, s1, s3, energy, ice_flag, thickness
    )
    return out


def solution(mesh):
    in_specs = (P("comp", "space", None), P("space", None), P("space", None), P("space", None))
    out_specs = P("comp", "space", None)
    return jax.shard_map(body, mesh=mesh, in_specs=in_specs, out_specs=out_specs, check_vma=False)
```

time: 256 us -> 178 us (0.70); the launches traced: 256 us -> 175 us
  waiting for transfers between devices: 142 us -> 86.9 us
  starting transfers between devices: 87.8 us -> 60.4 us
  other arithmetic: 21.9 us -> 2.96 us
  Pallas kernels: 0 us -> 9.85 us
  blocking collectives: 0 us -> 8.47 us
    all_to_all x2, waiting for transfers between devices: 122 us -> 11.7 us  [swap(): lax.all_to_all(value, 'comp', 0, 0, axis_index_groups=groups, tiled=True)]
    ppermute x8 -> x9, waiting for transfers between devices: 19.6 us -> 75.2 us  [the longest x4 62.5 us: move(): return lax.ppermute(value, 'comp', pairs)]
    all_to_all x2, starting transfers between devices: 66.6 us -> 22.9 us  [swap(): lax.all_to_all(value, 'comp', 0, 0, axis_index_groups=groups, tiled=True)]
    ppermute x8 -> x9, starting transfers between devices: 21.2 us -> 37.5 us  [the longest x4 25.1 us: move(): return lax.ppermute(value, 'comp', pairs)]
    mul x10 -> x0, other arithmetic: 11.5 us -> none  [the longest x4 8.08 us: body(): field = upwind(framed, speed_x, speed_y) * land[None]]
    pallas_call x0 -> x5, Pallas kernels: none -> 9.85 us  [the longest x1 4.04 us: body(): call(propagate, [part, part, edge, edge], True, 3, [pltpu.VMEM((rows + 8,...]
    all_to_all x0 -> x1, blocking collectives: none -> 8.47 us  [swap(): lax.all_to_all(value, 'comp', 0, 0, axis_index_groups=groups, tiled=True)]
    unnamed x4 -> x14, local copies, waits for them, and re-layouts: 0.01 us -> 3.21 us
  transfers between devices with their start and end apart: 10 -> 11, of which waited for: 10 -> 6; matrix products, arithmetic and copies ran while one was open for 0% -> 3% of each run, Pallas kernels for 0% -> 1%
where the time goes in v1:
time: 178 us; the launch traced here: 175 us
  waiting for transfers between devices  86.9 us (49%)
  starting transfers between devices  60.4 us (34%)
  Pallas kernels  9.85 us (6%)
  blocking collectives  8.47 us (5%)
  local copies, waits for them, and re-layouts  5.92 us (3%)
  other arithmetic  2.96 us (2%)
    ppermute x4, waiting for transfers between devices, move(): return lax.ppermute(value, 'comp', pairs)  62.5 us
    ppermute x4, starting transfers between devices, move(): return lax.ppermute(value, 'comp', pairs)  25.1 us
    all_to_all x2, starting transfers between devices, swap(): lax.all_to_all(value, 'comp', 0, 0, axis_index_groups=groups, tiled=True)  22.9 us
    all_to_all x2, waiting for transfers between devices, swap(): lax.all_to_all(value, 'comp', 0, 0, axis_index_groups=groups, tiled=True)  11.7 us
    ppermute x4, starting transfers between devices, turn(): return lax.ppermute(value, 'comp', pairs)  11.1 us
    all_to_all x1, blocking collectives, swap(): lax.all_to_all(value, 'comp', 0, 0, axis_index_groups=groups, tiled=True)  8.47 us
    ppermute x1, waiting for transfers between devices, body(): halo = lax.ppermute(message, ('comp', 'space'), pairs)  6.74 us
    ppermute x4, waiting for transfers between devices, turn(): return lax.ppermute(value, 'comp', pairs)  6 us
  transfers between devices with their start and end apart: 11, of which 6 were waited for; matrix products, arithmetic and copies ran while one was open for 3% of the time, Pallas kernels for 1%

profile of v1, /device:TPU:6, one launch (start us, length us, event | category | flops | bytes accessed | tf_op | source)
XLA Modules:
  0.0 174.6 jit_solution(12549258708111581920)
XLA Ops:
  0.0 0.0 copy-start.4
  0.0 0.0 copy-start.1
  0.0 0.0 copy-start
  0.0 1.9 %edge_rows.1 = f32[40,1024]{1,0:T(8,128)} custom-call(f32[9,32,1024]{2,1,0:T(8,128)} %field_ref.1, f32[9,32,1024]{2,1,0:T(8,128)} %field_ref.1, s32[32,1024]{1,0:T(8,128)} %mask_ref.1, s32[32,1024]{1,0:T(8,128)} %mask_ref.1), custom_call_target="tpu_custom_call" | custom-call | tf_op jit(solution)/shard_map/edge_rows/pallas_call | solution.py:212
  1.9 1.3 collective-permute-start
  3.2 6.7 %collective-permute-done.halo_ref = f32[40,1024]{1,0:T(8,128)S(1)} collective-permute-done((f32[40,1024]{1,0:T(8,128)}, f32[40,1024]{1,0:T(8,128)S(1)}, u32[]{:S(2)}, u32[]{:S(2)}) %collective-permute-start) | collective-permute-done | bytes 163872 | tf_op jit(solution)/shard_map/ppermute | solution.py:231
  9.9 0.0 copy-done.4
  9.9 0.0 copy-done.1
  9.9 0.0 copy-done
  9.9 4.0 %propagate.1 = (f32[9,16,1024]{2,1,0:T(8,128)S(1)}, f32[9,16,1024]{2,1,0:T(8,128)S(1)}, f32[3,32,1024]{2,1,0:T(8,128)S(1)}, f32[3,32,1024]{2,1,0:T(8,128)S(1)}) custom-call(f32[32,20]{1,0:T(8,128)S(1)} %copy-done.4, f32[9,32,1024]{2,1,0:T(8,128)S(1)} %copy-done, s32[32,1024]{1,0:T(8,128)S(1)} %copy-done.1, f32[40,1024]{1,0:T(8,128)S(1)} %collective-permute-done.halo_ref), custom_call_target="tpu_custom_call" | custom-call | tf_op jit(solution)/shard_map/propagate/pallas_call | solution.py:235
  14.0 1.3 collective-permute-start.1
  15.3 11.6 %collective-permute-start.2 = (f32[9,16,1024]{2,1,0:T(8,128)S(1)}, f32[9,16,1024]{2,1,0:T(8,128)S(1)}, u32[]{:S(2)}, u32[]{:S(2)}) collective-permute-start(f32[9,16,1024]{2,1,0:T(8,128)S(1)} %get-tuple-element.15.b_ref), channel_id=1, source_target_pairs={{0,256},{32,288},{64,320},{96,352},{128,384},{160,416},{192,448},{... | collective-permute-start | bytes 1769480 | tf_op jit(solution)/shard_map/ppermute | solution.py:206
  26.8 1.9 %collective-permute-start.3 = (f32[3,32,1024]{2,1,0:T(8,128)S(1)}, f32[3,32,1024]{2,1,0:T(8,128)S(1)}, u32[]{:S(2)}, u32[]{:S(2)}) collective-permute-start(f32[3,32,1024]{2,1,0:T(8,128)S(1)} %get-tuple-element.16), channel_id=1, source_target_pairs={{0,32},{32,64},{64,96},{96,0},{128,160},{160,192},{192,224},{224,1... | collective-permute-start | bytes 1179656 | tf_op jit(solution)/shard_map/ppermute | solution.py:210
  28.8 3.6 %collective-permute-start.4 = (f32[3,32,1024]{2,1,0:T(8,128)S(1)}, f32[3,32,1024]{2,1,0:T(8,128)S(1)}, u32[]{:S(2)}, u32[]{:S(2)}) collective-permute-start(f32[3,32,1024]{2,1,0:T(8,128)S(1)} %get-tuple-element.17), channel_id=1, source_target_pairs={{0,96},{32,0},{64,32},{96,64},{128,224},{160,128},{192,160},{224,1... | collective-permute-start | bytes 1179656 | tf_op jit(solution)/shard_map/ppermute | solution.py:210
  32.4 4.7 %collective-permute-done.3.low_ref = f32[3,32,1024]{2,1,0:T(8,128)S(1)} collective-permute-done((f32[3,32,1024]{2,1,0:T(8,128)S(1)}, f32[3,32,1024]{2,1,0:T(8,128)S(1)}, u32[]{:S(2)}, u32[]{:S(2)}) %collective-permute-start.3) | collective-permute-done | bytes 393248 | tf_op jit(solution)/shard_map/ppermute | solution.py:210
  37.1 1.3 collective-permute-done.4.top_ref
  38.4 1.1 sums.1
  39.5 10.9 %collective-permute-start.7 = (f32[9,16,1024]{2,1,0:T(8,128)}, f32[9,16,1024]{2,1,0:T(8,128)S(1)}, u32[]{:S(2)}, u32[]{:S(2)}) collective-permute-start(f32[9,16,1024]{2,1,0:T(8,128)} %get-tuple-element.20), channel_id=1, source_target_pairs={{0,256},{32,288},{64,320},{96,352},{128,384},{160,416},{192,448},{... | collective-permute-start | bytes 1769480 | tf_op jit(solution)/shard_map/ppermute | solution.py:206
  50.4 1.3 collective-permute-start.8
  51.7 62.5 %collective-permute-done.1.u_ref = f32[9,16,1024]{2,1,0:T(8,128)S(1)} collective-permute-done((f32[9,16,1024]{2,1,0:T(8,128)S(1)}, f32[9,16,1024]{2,1,0:T(8,128)S(1)}, u32[]{:S(2)}, u32[]{:S(2)}) %collective-permute-start.1) | collective-permute-done | bytes 589856 | tf_op jit(solution)/shard_map/ppermute | solution.py:206
  114.2 0.0 collective-permute-done.2.d_ref
  114.2 0.4 partial_energy.1
  114.6 0.0 copy-start.5
  114.6 0.7 copy-done.5
  115.3 0.0 copy-start.6
  115.3 0.7 copy-done.6
  116.0 8.5 %all_to_all.15 = f32[8,32,128]{2,1,0:T(8,128)} all-to-all(f32[8,32,128]{2,1,0:T(8,128)S(1)} %get-tuple-element.22), channel_id=1, replica_groups={{0,32,64,96,128,160,192,224},{256,288,320,352,384,416,448,480},{512,544..., dimensions={0} | all-to-all | bytes 262144 | tf_op jit(solution)/shard_map/all_to_all | solution.py:262
  124.5 1.5 reduce_sum.18
  126.0 1.3 broadcast_in_dim.4
  127.3 17.0 %all-to-all-start.1 = ((f32[4,32,128]{2,1,0:T(8,128)}), f32[4,32,128]{2,1,0:T(8,128)}, u32[]{:S(2)}, u32[]{:S(2)}) async-start(f32[4,32,128]{2,1,0:T(8,128)} %broadcast_in_dim.4), calls=%async_computation.1 | async-start | bytes 131072 | tf_op jit(solution)/shard_map/all_to_all | solution.py:262
  144.3 1.9 %collective-permute-start.5 = (f32[4,16,1024]{2,1,0:T(8,128)}, f32[4,16,1024]{2,1,0:T(8,128)}, u32[]{:S(2)}, u32[]{:S(2)}) collective-permute-start(f32[4,16,1024]{2,1,0:T(8,128)} %copy-done.6), channel_id=1, source_target_pairs={{0,32},{32,64},{64,96},{96,0},{128,160},{160,192},{192,224},{224,1... | collective-permute-start | bytes 786440 | tf_op jit(solution)/shard_map/ppermute | solution.py:210
  146.2 3.6 %collective-permute-start.6 = (f32[4,16,1024]{2,1,0:T(8,128)}, f32[4,16,1024]{2,1,0:T(8,128)}, u32[]{:S(2)}, u32[]{:S(2)}) collective-permute-start(f32[4,16,1024]{2,1,0:T(8,128)} %copy-done.5), channel_id=1, source_target_pairs={{0,96},{32,0},{64,32},{96,64},{128,224},{160,128},{192,160},{224,1... | collective-permute-start | bytes 786440 | tf_op jit(solution)/shard_map/ppermute | solution.py:210
  149.8 7.5 %all-to-all-done.1 = f32[4,32,128]{2,1,0:T(8,128)} async-done(((f32[4,32,128]{2,1,0:T(8,128)}), f32[4,32,128]{2,1,0:T(8,128)}, u32[]{:S(2)}, u32[]{:S(2)}) %all-to-all-start.1) | async-done | bytes 65568 | tf_op jit(solution)/shard_map/all_to_all | solution.py:262
  157.4 1.4 reduce_sum.19
  158.8 1.4 broadcast_in_dim.5
  160.2 6.0 %all-to-all-start.2 = ((f32[8,32,128]{2,1,0:T(8,128)}), f32[8,32,128]{2,1,0:T(8,128)}, u32[]{:S(2)}, u32[]{:S(2)}) async-start(f32[8,32,128]{2,1,0:T(8,128)} %broadcast_in_dim.5), calls=%async_computation.2 | async-start | bytes 262144 | tf_op jit(solution)/shard_map/all_to_all | solution.py:262
  166.2 0.0 collective-permute-done.5.low_ref
  166.2 0.0 collective-permute-done.6.top_ref
  166.2 0.0 collective-permute-done.7.s1_ref
  166.2 0.0 collective-permute-done.8.s3_ref
  166.2 4.1 %all-to-all-done.2.energy_ref = f32[8,32,128]{2,1,0:T(8,128)} async-done(((f32[8,32,128]{2,1,0:T(8,128)}), f32[8,32,128]{2,1,0:T(8,128)}, u32[]{:S(2)}, u32[]{:S(2)}) %all-to-all-start.2) | async-done | bytes 131104 | tf_op jit(solution)/shard_map/all_to_all | solution.py:262
  170.3 0.0 copy-start.2
  170.3 0.9 copy-done.2
  171.2 0.0 copy-start.3
  171.2 0.9 copy-done.3
  172.1 2.4 %finish.1 = f32[9,32,1024]{2,1,0:T(8,128)} custom-call(f32[32,20]{1,0:T(8,128)S(1)} %copy-done.4, f32[9,16,1024]{2,1,0:T(8,128)S(1)} %get-tuple-element.14.a_ref, f32[9,16,1024]{2,1,0:T(8,128)S(1)} %get-tuple-element.15.b_ref, f32[9,16,1024]{2,1,0:T(8,128)S(1)} %collective-permute-done.1.u_ref, f32[9,16,1024]{2,1,0:T(8,128)S(1)} %collective-permute-done.2.d_ref, ...), custom_call_target="tpu_custom_call" | custom-call | tf_op jit(solution)/shard_map/finish/pallas_call | solution.py:269
Async XLA Ops:
  0.0 9.9 %copy-start.4 = (f32[32,20]{1,0:T(8,128)S(1)}, f32[32,20]{1,0:T(8,128)}, u32[]{:S(2)}) copy-start(f32[32,20]{1,0:T(8,128)} %constant.4.clone.table_ref) | copy-start | bytes 7684
  0.0 9.9 %copy-start.1 = (s32[32,1024]{1,0:T(8,128)S(1)}, s32[32,1024]{1,0:T(8,128)}, u32[]{:S(2)}) copy-start(s32[32,1024]{1,0:T(8,128)} %mask_ref.1) | copy-start | bytes 393220
  0.0 9.9 %copy-start = (f32[9,32,1024]{2,1,0:T(8,128)S(1)}, f32[9,32,1024]{2,1,0:T(8,128)}, u32[]{:S(2)}) copy-start(f32[9,32,1024]{2,1,0:T(8,128)} %field_ref.1) | copy-start | bytes 3538948
  1.9 8.0 %collective-permute-start = (f32[40,1024]{1,0:T(8,128)}, f32[40,1024]{1,0:T(8,128)S(1)}, u32[]{:S(2)}, u32[]{:S(2)}) collective-permute-start(f32[40,1024]{1,0:T(8,128)} %edge_rows.1), channel_id=1, source_target_pairs={{0,1},{1,2},{2,3},{3,4},{4,5},{5,6},{6,7},{7,8},{8,9},{9,10},{10,1... | collective-permute-start | bytes 491528 | tf_op jit(solution)/shard_map/ppermute | solution.py:231
  14.0 100.2 %collective-permute-start.1 = (f32[9,16,1024]{2,1,0:T(8,128)S(1)}, f32[9,16,1024]{2,1,0:T(8,128)S(1)}, u32[]{:S(2)}, u32[]{:S(2)}) collective-permute-start(f32[9,16,1024]{2,1,0:T(8,128)S(1)} %get-tuple-element.14.a_ref), channel_id=1, source_target_pairs={{256,0},{288,32},{320,64},{352,96},{384,128},{416,160},{448,192},{... | collective-permute-start | bytes 1769480 | tf_op jit(solution)/shard_map/ppermute | solution.py:206
  15.3 98.9 %collective-permute-start.2 = (f32[9,16,1024]{2,1,0:T(8,128)S(1)}, f32[9,16,1024]{2,1,0:T(8,128)S(1)}, u32[]{:S(2)}, u32[]{:S(2)}) collective-permute-start(f32[9,16,1024]{2,1,0:T(8,128)S(1)} %get-tuple-element.15.b_ref), channel_id=1, source_target_pairs={{0,256},{32,288},{64,320},{96,352},{128,384},{160,416},{192,448},{... | collective-permute-start | bytes 1769480 | tf_op jit(solution)/shard_map/ppermute | solution.py:206
  26.8 10.3 %collective-permute-start.3 = (f32[3,32,1024]{2,1,0:T(8,128)S(1)}, f32[3,32,1024]{2,1,0:T(8,128)S(1)}, u32[]{:S(2)}, u32[]{:S(2)}) collective-permute-start(f32[3,32,1024]{2,1,0:T(8,128)S(1)} %get-tuple-element.16), channel_id=1, source_target_pairs={{0,32},{32,64},{64,96},{96,0},{128,160},{160,192},{192,224},{224,1... | collective-permute-start | bytes 1179656 | tf_op jit(solution)/shard_map/ppermute | solution.py:210
  28.8 9.6 %collective-permute-start.4 = (f32[3,32,1024]{2,1,0:T(8,128)S(1)}, f32[3,32,1024]{2,1,0:T(8,128)S(1)}, u32[]{:S(2)}, u32[]{:S(2)}) collective-permute-start(f32[3,32,1024]{2,1,0:T(8,128)S(1)} %get-tuple-element.17), channel_id=1, source_target_pairs={{0,96},{32,0},{64,32},{96,64},{128,224},{160,128},{192,160},{224,1... | collective-permute-start | bytes 1179656 | tf_op jit(solution)/shard_map/ppermute | solution.py:210
  39.5 126.7 %collective-permute-start.7 = (f32[9,16,1024]{2,1,0:T(8,128)}, f32[9,16,1024]{2,1,0:T(8,128)S(1)}, u32[]{:S(2)}, u32[]{:S(2)}) collective-permute-start(f32[9,16,1024]{2,1,0:T(8,128)} %get-tuple-element.20), channel_id=1, source_target_pairs={{0,256},{32,288},{64,320},{96,352},{128,384},{160,416},{192,448},{... | collective-permute-start | bytes 1769480 | tf_op jit(solution)/shard_map/ppermute | solution.py:206
  50.4 115.8 %collective-permute-start.8 = (f32[9,16,1024]{2,1,0:T(8,128)}, f32[9,16,1024]{2,1,0:T(8,128)S(1)}, u32[]{:S(2)}, u32[]{:S(2)}) collective-permute-start(f32[9,16,1024]{2,1,0:T(8,128)} %get-tuple-element.21), channel_id=1, source_target_pairs={{256,0},{288,32},{320,64},{352,96},{384,128},{416,160},{448,192},{... | collective-permute-start | bytes 1769480 | tf_op jit(solution)/shard_map/ppermute | solution.py:206
  114.6 0.7 copy-start.5
  115.3 0.7 copy-start.6
  127.3 30.1 %all-to-all-start.1 = ((f32[4,32,128]{2,1,0:T(8,128)}), f32[4,32,128]{2,1,0:T(8,128)}, u32[]{:S(2)}, u32[]{:S(2)}) async-start(f32[4,32,128]{2,1,0:T(8,128)} %broadcast_in_dim.4), calls=%async_computation.1 | async-start | bytes 131072 | tf_op jit(solution)/shard_map/all_to_all | solution.py:262
  144.3 21.9 %collective-permute-start.5 = (f32[4,16,1024]{2,1,0:T(8,128)}, f32[4,16,1024]{2,1,0:T(8,128)}, u32[]{:S(2)}, u32[]{:S(2)}) collective-permute-start(f32[4,16,1024]{2,1,0:T(8,128)} %copy-done.6), channel_id=1, source_target_pairs={{0,32},{32,64},{64,96},{96,0},{128,160},{160,192},{192,224},{224,1... | collective-permute-start | bytes 786440 | tf_op jit(solution)/shard_map/ppermute | solution.py:210
  146.2 20.0 %collective-permute-start.6 = (f32[4,16,1024]{2,1,0:T(8,128)}, f32[4,16,1024]{2,1,0:T(8,128)}, u32[]{:S(2)}, u32[]{:S(2)}) collective-permute-start(f32[4,16,1024]{2,1,0:T(8,128)} %copy-done.5), channel_id=1, source_target_pairs={{0,96},{32,0},{64,32},{96,64},{128,224},{160,128},{192,160},{224,1... | collective-permute-start | bytes 786440 | tf_op jit(solution)/shard_map/ppermute | solution.py:210
  160.2 10.1 %all-to-all-start.2 = ((f32[8,32,128]{2,1,0:T(8,128)}), f32[8,32,128]{2,1,0:T(8,128)}, u32[]{:S(2)}, u32[]{:S(2)}) async-start(f32[8,32,128]{2,1,0:T(8,128)} %broadcast_in_dim.5), calls=%async_computation.2 | async-start | bytes 262144 | tf_op jit(solution)/shard_map/all_to_all | solution.py:262
  170.3 0.9 copy-start.2
  171.2 0.9 copy-start.3

commit v2 on v1

--- a/solution.py
+++ b/solution.py
@@ -22,7 +22,7 @@
 whitecap_rate = 2.0
 ice_rate = 0.3
 
-VMEM_BYTES = 40 * 1024 * 1024
+VMEM_BYTES = 16 * 1024 * 1024
 
 
 def tables():
@@ -118,27 +118,27 @@
     return mid_ref[i, rows]
 
 
-def sums(a_ref, b_ref, low_ref, top_ref, s1_ref, s3_ref):
-    half = a_ref.shape[1]
-    for t in range(0, half, 8):
-        rows = pl.ds(t, 8)
-        a = lambda i: at(low_ref, a_ref, top_ref, i, rows, rows)
-        b = lambda i: at(low_ref, b_ref, top_ref, i, rows, pl.ds(half + t, 8))
-        for i in range(NQ):
-            s1_ref[i, rows] = a(i - 1) + a(i + 1)
-            s3_ref[i, rows] = b(i - 3) + b(i + 3)
-
-
-def partial_energy(a_ref, b_ref, low_ref, top_ref, u_ref, d_ref, out_ref, prev_ref, next_ref):
+def attenuation(table_ref, ice_ref, thick_ref, out_ref):
+    fsq = table_ref[lax.axis_index("comp"), 2 * NQ]
+    depth = ice_ref[...].astype(jnp.float32) * thick_ref[...]
+    out_ref[...] = jnp.exp(-ice_rate * depth * fsq)
+
+
+def half_way(a_ref, b_ref, low_ref, top_ref, u_ref, d_ref, s1_ref, s3_ref, out_ref, prev_ref, next_ref):
     half, cols = a_ref.shape[1:]
     width = cols // GROUP
     for t in range(0, 2 * half, 8):
-        mid, other, s = (a_ref, u_ref, t) if t < half else (b_ref, d_ref, t - half)
+        first = t < half
+        mid, other, s = (a_ref, u_ref, t) if first else (b_ref, d_ref, t - half)
         e = lambda i: at(low_ref, mid, top_ref, i, pl.ds(s, 8), pl.ds(t, 8))
         total = jnp.zeros((8, cols), jnp.float32)
         for i in range(NQ):
-            around = (e(i - 3) + e(i + 3)) + (e(i - 1) + e(i + 1))
-            crossed = 0.25 * mixing_rate * other[i, pl.ds(s, 8)] * around
+            near, far = e(i - 1) + e(i + 1), e(i - 3) + e(i + 3)
+            if first:
+                s1_ref[i, pl.ds(s, 8)] = near
+            else:
+                s3_ref[i, pl.ds(s, 8)] = far
+            crossed = 0.25 * mixing_rate * other[i, pl.ds(s, 8)] * (near + far)
             total = total + (e(i) - mixing_rate * e(i) * e(i) + crossed)
         for g in range(GROUP):
             out_ref[g, t : t + 8] = total[:, g * width : (g + 1) * width]
@@ -148,15 +148,22 @@
     next_ref[EDGE] = d_ref[NQ - 1]
 
 
-def finish(table_ref, a_ref, b_ref, u_ref, d_ref, low_ref, top_ref, s1_ref, s3_ref, energy_ref, ice_ref, thick_ref, out_ref):
+def total_to_all(parts_ref, out_ref):
+    total = parts_ref[0]
+    for k in range(1, parts_ref.shape[0]):
+        total = total + parts_ref[k]
+    for k in range(out_ref.shape[0]):
+        out_ref[k] = total
+
+
+def finish(table_ref, a_ref, b_ref, u_ref, d_ref, low_ref, top_ref, s1_ref, s3_ref, energy_ref, att_ref, out_ref):
     p = lax.axis_index("comp")
     fsq = table_ref[p, 2 * NQ]
     half = a_ref.shape[1]
     for t in range(0, 2 * half, 8):
         rows = pl.ds(t, 8)
         energy = jnp.concatenate([energy_ref[g, rows] for g in range(GROUP)], axis=1) * (1.0 / (ND * NF))
-        depth = ice_ref[rows].astype(jnp.float32) * thick_ref[rows]
-        factor = jnp.exp(-ice_rate * depth * fsq) / (1.0 + whitecap_rate * energy * fsq)
+        factor = att_ref[rows] / (1.0 + whitecap_rate * energy * fsq)
         for i in range(NQ):
             if t < half:
                 e = a_ref[i, rows]
@@ -244,14 +251,13 @@
     d = move(b, GROUP)
     top = turn(lo, -1)
     low = turn(hi, 1)
-    s1, s3 = call(sums, [part, part], False, 4)(a, b, low, top)
+    edges = (EDGE + 1, half, cols)
+    s1, s3, share, to_prev, to_next = call(
+        half_way, [part, part, (GROUP, rows, cols // GROUP), edges, edges], False, 6
+    )(a, b, low, top, u, d)
     s1 = move(s1, GROUP)
     s3 = move(s3, -GROUP)
-
-    edges = (EDGE + 1, half, cols)
-    share, to_prev, to_next = call(
-        partial_energy, [(GROUP, rows, cols // GROUP), edges, edges], False, 6
-    )(a, b, low, top, u, d)
+    (att,) = call(attenuation, [(rows, cols)], True, 2)(table, ice_flag, thickness)
     top_u = turn(to_prev, -1)
     low_u = turn(to_next, 1)
 
@@ -261,13 +267,14 @@
     def swap(value, groups):
         return lax.all_to_all(value, "comp", 0, 0, axis_index_groups=groups, tiled=True)
 
-    share = jnp.sum(swap(share, near), axis=0)
-    share = swap(jnp.broadcast_to(share[None], (n_comp // GROUP,) + share.shape), far)
-    share = jnp.sum(share, axis=0)
-    energy = swap(jnp.broadcast_to(share[None], (GROUP,) + share.shape), near)
-
-    (out,) = call(finish, [(comps, rows, cols)], True, 11)(
-        table, a, b, u, d, low_u, top_u, s1, s3, energy, ice_flag, thickness
+    def spread(value, copies):
+        return call(total_to_all, [(copies,) + value.shape[1:]], False, 1)(value)[0]
+
+    share = spread(swap(share, near), n_comp // GROUP)
+    energy = swap(spread(swap(share, far), GROUP), near)
+
+    (out,) = call(finish, [(comps, rows, cols)], True, 10)(
+        table, a, b, u, d, low_u, top_u, s1, s3, energy, att
     )
     return out
 

time: 178 us -> 184 us (1.034)
  starting transfers between devices: 60.4 us -> 96.9 us
  waiting for transfers between devices: 86.9 us -> 58.6 us
  other arithmetic: 2.96 us -> 0 us
    ppermute x4, starting transfers between devices: 25.1 us -> 64.8 us  [move(): return lax.ppermute(value, 'comp', pairs)]
    ppermute x4, waiting for transfers between devices: 62.5 us -> 37.5 us  [move(): return lax.ppermute(value, 'comp', pairs)]
    all_to_all x2, waiting for transfers between devices: 11.7 us -> 8.39 us  [swap(): lax.all_to_all(value, 'comp', 0, 0, axis_index_groups=groups, tiled=True)]
    all_to_all x2, starting transfers between devices: 22.9 us -> 19.7 us  [swap(): lax.all_to_all(value, 'comp', 0, 0, axis_index_groups=groups, tiled=True)]
    reduce_sum x2 -> x0, other arithmetic: 2.96 us -> none  [the longest x1 1.52 us: body(): share = jnp.sum(swap(share, near), axis=0)]
    broadcast_in_dim x2 -> x0, local copies, waits for them, and re-layouts: 2.72 us -> none  [the longest x1 1.38 us: body(): energy = swap(jnp.broadcast_to(share[None], (GROUP,) + share.shape), near)]
    unnamed x14 -> x22, local copies, waits for them, and re-layouts: 3.21 us -> 5.32 us
    pallas_call x3 -> x5, Pallas kernels: 3.95 us -> 5.45 us  [the longest x1 2.42 us: body(): call(finish, [(comps, rows, cols)], True, 10)]
  transfers between devices with their start and end apart: 11 -> 11, of which waited for: 6 -> 6; matrix products, arithmetic and copies ran while one was open for 3% -> 0% of each run, Pallas kernels for 1% -> 1%
where the time goes in v2:
time: 184 us; the launch traced here: 181 us
  starting transfers between devices  96.9 us (53%)
  waiting for transfers between devices  58.6 us (32%)
  Pallas kernels  11.4 us (6%)
  blocking collectives  8.38 us (5%)
  local copies, waits for them, and re-layouts  5.32 us (3%)
    ppermute x4, starting transfers between devices, move(): return lax.ppermute(value, 'comp', pairs)  64.8 us
    ppermute x4, waiting for transfers between devices, move(): return lax.ppermute(value, 'comp', pairs)  37.5 us
    all_to_all x2, starting transfers between devices, swap(): lax.all_to_all(value, 'comp', 0, 0, axis_index_groups=groups, tiled=True)  19.7 us
    ppermute x4, starting transfers between devices, turn(): return lax.ppermute(value, 'comp', pairs)  11.1 us
    all_to_all x2, waiting for transfers between devices, swap(): lax.all_to_all(value, 'comp', 0, 0, axis_index_groups=groups, tiled=True)  8.39 us
    all_to_all x1, blocking collectives, swap(): lax.all_to_all(value, 'comp', 0, 0, axis_index_groups=groups, tiled=True)  8.38 us
    ppermute x1, waiting for transfers between devices, body(): halo = lax.ppermute(message, ('comp', 'space'), pairs)  6.74 us
    ppermute x4, waiting for transfers between devices, turn(): return lax.ppermute(value, 'comp', pairs)  6 us
  transfers between devices with their start and end apart: 11, of which 6 were waited for; matrix products, arithmetic and copies ran while one was open for 0% of the time, Pallas kernels for 1%

profile of v2, /device:TPU:6, one launch (start us, length us, event | category | flops | bytes accessed | tf_op | source)
XLA Modules:
  0.0 180.7 jit_solution(12840199908895849510)
XLA Ops:
  0.0 0.0 copy-start.6
  0.0 0.0 copy-start.1
  0.0 0.0 copy-start
  0.0 1.9 %edge_rows.1 = f32[40,1024]{1,0:T(8,128)} custom-call(f32[9,32,1024]{2,1,0:T(8,128)} %field_ref.1, f32[9,32,1024]{2,1,0:T(8,128)} %field_ref.1, s32[32,1024]{1,0:T(8,128)} %mask_ref.1, s32[32,1024]{1,0:T(8,128)} %mask_ref.1), custom_call_target="tpu_custom_call" | custom-call | tf_op jit(solution)/shard_map/edge_rows/pallas_call | solution.py:219
  1.9 1.3 collective-permute-start
  3.2 6.7 %collective-permute-done.halo_ref = f32[40,1024]{1,0:T(8,128)S(1)} collective-permute-done((f32[40,1024]{1,0:T(8,128)}, f32[40,1024]{1,0:T(8,128)S(1)}, u32[]{:S(2)}, u32[]{:S(2)}) %collective-permute-start) | collective-permute-done | bytes 163872 | tf_op jit(solution)/shard_map/ppermute | solution.py:238
  9.9 0.0 copy-done.6
  9.9 0.0 copy-done.1
  9.9 0.0 copy-done
  9.9 4.0 %propagate.1 = (f32[9,16,1024]{2,1,0:T(8,128)S(1)}, f32[9,16,1024]{2,1,0:T(8,128)S(1)}, f32[3,32,1024]{2,1,0:T(8,128)S(1)}, f32[3,32,1024]{2,1,0:T(8,128)S(1)}) custom-call(f32[32,20]{1,0:T(8,128)S(1)} %copy-done.6, f32[9,32,1024]{2,1,0:T(8,128)S(1)} %copy-done, s32[32,1024]{1,0:T(8,128)S(1)} %copy-done.1, f32[40,1024]{1,0:T(8,128)S(1)} %collective-permute-done.halo_ref), custom_call_target="tpu_custom_call" | custom-call | tf_op jit(solution)/shard_map/propagate/pallas_call | solution.py:242
  14.0 1.3 collective-permute-start.1
  15.3 11.6 %collective-permute-start.2 = (f32[9,16,1024]{2,1,0:T(8,128)S(1)}, f32[9,16,1024]{2,1,0:T(8,128)S(1)}, u32[]{:S(2)}, u32[]{:S(2)}) collective-permute-start(f32[9,16,1024]{2,1,0:T(8,128)S(1)} %get-tuple-element.15.b_ref), channel_id=1, source_target_pairs={{0,256},{32,288},{64,320},{96,352},{128,384},{160,416},{192,448},{... | collective-permute-start | bytes 1769480 | tf_op jit(solution)/shard_map/ppermute | solution.py:213
  26.8 1.9 %collective-permute-start.3 = (f32[3,32,1024]{2,1,0:T(8,128)S(1)}, f32[3,32,1024]{2,1,0:T(8,128)S(1)}, u32[]{:S(2)}, u32[]{:S(2)}) collective-permute-start(f32[3,32,1024]{2,1,0:T(8,128)S(1)} %get-tuple-element.16), channel_id=1, source_target_pairs={{0,32},{32,64},{64,96},{96,0},{128,160},{160,192},{192,224},{224,1... | collective-permute-start | bytes 1179656 | tf_op jit(solution)/shard_map/ppermute | solution.py:217
  28.8 3.6 %collective-permute-start.4 = (f32[3,32,1024]{2,1,0:T(8,128)S(1)}, f32[3,32,1024]{2,1,0:T(8,128)S(1)}, u32[]{:S(2)}, u32[]{:S(2)}) collective-permute-start(f32[3,32,1024]{2,1,0:T(8,128)S(1)} %get-tuple-element.17), channel_id=1, source_target_pairs={{0,96},{32,0},{64,32},{96,64},{128,224},{160,128},{192,160},{224,1... | collective-permute-start | bytes 1179656 | tf_op jit(solution)/shard_map/ppermute | solution.py:217
  32.4 4.7 %collective-permute-done.3.low_ref = f32[3,32,1024]{2,1,0:T(8,128)S(1)} collective-permute-done((f32[3,32,1024]{2,1,0:T(8,128)S(1)}, f32[3,32,1024]{2,1,0:T(8,128)S(1)}, u32[]{:S(2)}, u32[]{:S(2)}) %collective-permute-start.3) | collective-permute-done | bytes 393248 | tf_op jit(solution)/shard_map/ppermute | solution.py:217
  37.1 1.3 collective-permute-done.4.top_ref
  38.4 37.5 %collective-permute-done.1.u_ref = f32[9,16,1024]{2,1,0:T(8,128)S(1)} collective-permute-done((f32[9,16,1024]{2,1,0:T(8,128)S(1)}, f32[9,16,1024]{2,1,0:T(8,128)S(1)}, u32[]{:S(2)}, u32[]{:S(2)}) %collective-permute-start.1) | collective-permute-done | bytes 589856 | tf_op jit(solution)/shard_map/ppermute | solution.py:213
  75.9 0.0 collective-permute-done.2.d_ref
  75.9 1.3 half_way.1
  77.2 0.0 copy-start.10
  77.2 0.7 copy-done.10
  77.9 0.0 copy-start.9
  77.9 50.6 %collective-permute-start.7 = (f32[9,16,1024]{2,1,0:T(8,128)}, f32[9,16,1024]{2,1,0:T(8,128)S(1)}, u32[]{:S(2)}, u32[]{:S(2)}) collective-permute-start(f32[9,16,1024]{2,1,0:T(8,128)} %get-tuple-element.20), channel_id=1, source_target_pairs={{0,256},{32,288},{64,320},{96,352},{128,384},{160,416},{192,448},{... | collective-permute-start | bytes 1769480 | tf_op jit(solution)/shard_map/ppermute | solution.py:213
  128.5 1.3 collective-permute-start.8
  129.8 8.4 %all_to_all.15.parts_ref = f32[8,32,128]{2,1,0:T(8,128)S(1)} all-to-all(f32[8,32,128]{2,1,0:T(8,128)S(1)} %get-tuple-element.22), channel_id=1, replica_groups={{0,32,64,96,128,160,192,224},{256,288,320,352,384,416,448,480},{512,544..., dimensions={0} | all-to-all | bytes 262144 | tf_op jit(solution)/shard_map/all_to_all | solution.py:268
  138.2 0.0 copy-done.9
  138.2 0.0 copy-start.5
  138.2 0.6 copy-done.5
  138.9 13.8 %all-to-all-start.1 = ((f32[4,32,128]{2,1,0:T(8,128)}), f32[4,32,128]{2,1,0:T(8,128)}, u32[]{:S(2)}, u32[]{:S(2)}) async-start(f32[4,32,128]{2,1,0:T(8,128)} %copy-done.5), calls=%async_computation.1 | async-start | bytes 131072 | tf_op jit(solution)/shard_map/all_to_all | solution.py:268
  152.6 1.9 %collective-permute-start.5 = (f32[4,16,1024]{2,1,0:T(8,128)}, f32[4,16,1024]{2,1,0:T(8,128)}, u32[]{:S(2)}, u32[]{:S(2)}) collective-permute-start(f32[4,16,1024]{2,1,0:T(8,128)} %copy-done.10), channel_id=1, source_target_pairs={{0,32},{32,64},{64,96},{96,0},{128,160},{160,192},{192,224},{224,1... | collective-permute-start | bytes 786440 | tf_op jit(solution)/shard_map/ppermute | solution.py:217
  154.6 3.6 %collective-permute-start.6 = (f32[4,16,1024]{2,1,0:T(8,128)}, f32[4,16,1024]{2,1,0:T(8,128)}, u32[]{:S(2)}, u32[]{:S(2)}) collective-permute-start(f32[4,16,1024]{2,1,0:T(8,128)} %copy-done.9), channel_id=1, source_target_pairs={{0,96},{32,0},{64,32},{96,64},{128,224},{160,128},{192,160},{224,1... | collective-permute-start | bytes 786440 | tf_op jit(solution)/shard_map/ppermute | solution.py:217
  158.2 7.5 %all-to-all-done.1.parts_ref = f32[4,32,128]{2,1,0:T(8,128)} async-done(((f32[4,32,128]{2,1,0:T(8,128)}), f32[4,32,128]{2,1,0:T(8,128)}, u32[]{:S(2)}, u32[]{:S(2)}) %all-to-all-start.1) | async-done | bytes 65568 | tf_op jit(solution)/shard_map/all_to_all | solution.py:268
  165.8 0.9 total_to_all.3
  166.6 0.0 copy-start.4
  166.6 0.6 copy-done.4
  167.3 6.0 %all-to-all-start.2 = ((f32[8,32,128]{2,1,0:T(8,128)}), f32[8,32,128]{2,1,0:T(8,128)}, u32[]{:S(2)}, u32[]{:S(2)}) async-start(f32[8,32,128]{2,1,0:T(8,128)} %copy-done.4), calls=%async_computation.2 | async-start | bytes 262144 | tf_op jit(solution)/shard_map/all_to_all | solution.py:268
  173.2 0.9 copy-done.7
  174.1 0.9 copy-done.8
  175.0 0.8 attenuation.1.att_ref
  175.9 0.0 copy-start.2
  175.9 0.6 copy-done.2
  176.5 0.0 collective-permute-done.5.low_ref
  176.5 0.0 collective-permute-done.6.top_ref
  176.5 0.8 all-to-all-done.2.energy_ref
  177.4 0.0 collective-permute-done.7.s1_ref
  177.4 0.0 collective-permute-done.8.s3_ref
  177.4 0.9 copy-done.3
  178.3 2.4 %finish.1 = f32[9,32,1024]{2,1,0:T(8,128)} custom-call(f32[32,20]{1,0:T(8,128)S(1)} %copy-done.6, f32[9,16,1024]{2,1,0:T(8,128)S(1)} %get-tuple-element.14.a_ref, f32[9,16,1024]{2,1,0:T(8,128)S(1)} %get-tuple-element.15.b_ref, f32[9,16,1024]{2,1,0:T(8,128)S(1)} %collective-permute-done.1.u_ref, f32[9,16,1024]{2,1,0:T(8,128)S(1)} %collective-permute-done.2.d_ref, ...), custom_call_target="tpu_custom_call" | custom-call | tf_op jit(solution)/shard_map/finish/pallas_call | solution.py:276
  (4 shorter events, 0.0 us)
Async XLA Ops:
  0.0 9.9 %copy-start.6 = (f32[32,20]{1,0:T(8,128)S(1)}, f32[32,20]{1,0:T(8,128)}, u32[]{:S(2)}) copy-start(f32[32,20]{1,0:T(8,128)} %constant.2.clone.table_ref) | copy-start | bytes 7684
  0.0 9.9 %copy-start.1 = (s32[32,1024]{1,0:T(8,128)S(1)}, s32[32,1024]{1,0:T(8,128)}, u32[]{:S(2)}) copy-start(s32[32,1024]{1,0:T(8,128)} %mask_ref.1) | copy-start | bytes 393220
  0.0 9.9 %copy-start = (f32[9,32,1024]{2,1,0:T(8,128)S(1)}, f32[9,32,1024]{2,1,0:T(8,128)}, u32[]{:S(2)}) copy-start(f32[9,32,1024]{2,1,0:T(8,128)} %field_ref.1) | copy-start | bytes 3538948
  1.9 8.0 %collective-permute-start = (f32[40,1024]{1,0:T(8,128)}, f32[40,1024]{1,0:T(8,128)S(1)}, u32[]{:S(2)}, u32[]{:S(2)}) collective-permute-start(f32[40,1024]{1,0:T(8,128)} %edge_rows.1), channel_id=1, source_target_pairs={{0,1},{1,2},{2,3},{3,4},{4,5},{5,6},{6,7},{7,8},{8,9},{9,10},{10,1... | collective-permute-start | bytes 491528 | tf_op jit(solution)/shard_map/ppermute | solution.py:238
  14.0 61.9 %collective-permute-start.1 = (f32[9,16,1024]{2,1,0:T(8,128)S(1)}, f32[9,16,1024]{2,1,0:T(8,128)S(1)}, u32[]{:S(2)}, u32[]{:S(2)}) collective-permute-start(f32[9,16,1024]{2,1,0:T(8,128)S(1)} %get-tuple-element.14.a_ref), channel_id=1, source_target_pairs={{256,0},{288,32},{320,64},{352,96},{384,128},{416,160},{448,192},{... | collective-permute-start | bytes 1769480 | tf_op jit(solution)/shard_map/ppermute | solution.py:213
  15.3 60.6 %collective-permute-start.2 = (f32[9,16,1024]{2,1,0:T(8,128)S(1)}, f32[9,16,1024]{2,1,0:T(8,128)S(1)}, u32[]{:S(2)}, u32[]{:S(2)}) collective-permute-start(f32[9,16,1024]{2,1,0:T(8,128)S(1)} %get-tuple-element.15.b_ref), channel_id=1, source_target_pairs={{0,256},{32,288},{64,320},{96,352},{128,384},{160,416},{192,448},{... | collective-permute-start | bytes 1769480 | tf_op jit(solution)/shard_map/ppermute | solution.py:213
  26.8 10.3 %collective-permute-start.3 = (f32[3,32,1024]{2,1,0:T(8,128)S(1)}, f32[3,32,1024]{2,1,0:T(8,128)S(1)}, u32[]{:S(2)}, u32[]{:S(2)}) collective-permute-start(f32[3,32,1024]{2,1,0:T(8,128)S(1)} %get-tuple-element.16), channel_id=1, source_target_pairs={{0,32},{32,64},{64,96},{96,0},{128,160},{160,192},{192,224},{224,1... | collective-permute-start | bytes 1179656 | tf_op jit(solution)/shard_map/ppermute | solution.py:217
  28.8 9.6 %collective-permute-start.4 = (f32[3,32,1024]{2,1,0:T(8,128)S(1)}, f32[3,32,1024]{2,1,0:T(8,128)S(1)}, u32[]{:S(2)}, u32[]{:S(2)}) collective-permute-start(f32[3,32,1024]{2,1,0:T(8,128)S(1)} %get-tuple-element.17), channel_id=1, source_target_pairs={{0,96},{32,0},{64,32},{96,64},{128,224},{160,128},{192,160},{224,1... | collective-permute-start | bytes 1179656 | tf_op jit(solution)/shard_map/ppermute | solution.py:217
  77.2 0.7 copy-start.10
  77.9 60.3 %copy-start.9 = (f32[4,16,1024]{2,1,0:T(8,128)}, f32[4,16,1024]{2,1,0:T(8,128)S(1)}, u32[]{:S(2)}) copy-start(f32[4,16,1024]{2,1,0:T(8,128)S(1)} %get-tuple-element.19) | copy-start | bytes 786436
  77.9 99.4 %collective-permute-start.7 = (f32[9,16,1024]{2,1,0:T(8,128)}, f32[9,16,1024]{2,1,0:T(8,128)S(1)}, u32[]{:S(2)}, u32[]{:S(2)}) collective-permute-start(f32[9,16,1024]{2,1,0:T(8,128)} %get-tuple-element.20), channel_id=1, source_target_pairs={{0,256},{32,288},{64,320},{96,352},{128,384},{160,416},{192,448},{... | collective-permute-start | bytes 1769480 | tf_op jit(solution)/shard_map/ppermute | solution.py:213
  128.5 48.8 %collective-permute-start.8 = (f32[9,16,1024]{2,1,0:T(8,128)}, f32[9,16,1024]{2,1,0:T(8,128)S(1)}, u32[]{:S(2)}, u32[]{:S(2)}) collective-permute-start(f32[9,16,1024]{2,1,0:T(8,128)} %get-tuple-element.21), channel_id=1, source_target_pairs={{256,0},{288,32},{320,64},{352,96},{384,128},{416,160},{448,192},{... | collective-permute-start | bytes 1769480 | tf_op jit(solution)/shard_map/ppermute | solution.py:213
  138.2 0.6 copy-start.5
  138.9 26.9 %all-to-all-start.1 = ((f32[4,32,128]{2,1,0:T(8,128)}), f32[4,32,128]{2,1,0:T(8,128)}, u32[]{:S(2)}, u32[]{:S(2)}) async-start(f32[4,32,128]{2,1,0:T(8,128)} %copy-done.5), calls=%async_computation.1 | async-start | bytes 131072 | tf_op jit(solution)/shard_map/all_to_all | solution.py:268
  152.6 23.9 %collective-permute-start.5 = (f32[4,16,1024]{2,1,0:T(8,128)}, f32[4,16,1024]{2,1,0:T(8,128)}, u32[]{:S(2)}, u32[]{:S(2)}) collective-permute-start(f32[4,16,1024]{2,1,0:T(8,128)} %copy-done.10), channel_id=1, source_target_pairs={{0,32},{32,64},{64,96},{96,0},{128,160},{160,192},{192,224},{224,1... | collective-permute-start | bytes 786440 | tf_op jit(solution)/shard_map/ppermute | solution.py:217
  154.6 22.0 %collective-permute-start.6 = (f32[4,16,1024]{2,1,0:T(8,128)}, f32[4,16,1024]{2,1,0:T(8,128)}, u32[]{:S(2)}, u32[]{:S(2)}) collective-permute-start(f32[4,16,1024]{2,1,0:T(8,128)} %copy-done.9), channel_id=1, source_target_pairs={{0,96},{32,0},{64,32},{96,64},{128,224},{160,128},{192,160},{224,1... | collective-permute-start | bytes 786440 | tf_op jit(solution)/shard_map/ppermute | solution.py:217
  166.6 0.7 copy-start.4
  167.3 10.1 %all-to-all-start.2 = ((f32[8,32,128]{2,1,0:T(8,128)}), f32[8,32,128]{2,1,0:T(8,128)}, u32[]{:S(2)}, u32[]{:S(2)}) async-start(f32[8,32,128]{2,1,0:T(8,128)} %copy-done.4), calls=%async_computation.2 | async-start | bytes 262144 | tf_op jit(solution)/shard_map/all_to_all | solution.py:268
  173.2 0.9 copy-start.7
  174.1 0.9 copy-start.8
  175.9 0.6 copy-start.2
  177.4 0.9 copy-start.3

commit v3 on v2

--- a/solution.py
+++ b/solution.py
@@ -16,13 +16,14 @@
 NQ = ND // QUARTERS
 GROUP = 8
 EDGE = 3
+Z_LOW = 4
 
 courant_top = 0.65
 mixing_rate = 0.5
 whitecap_rate = 2.0
 ice_rate = 0.3
 
-VMEM_BYTES = 16 * 1024 * 1024
+VMEM_BYTES = 12 * 1024 * 1024
 
 
 def tables():
@@ -41,6 +42,22 @@
     return lax.rem(lax.axis_index("comp"), QUARTERS)
 
 
+def climbs(space, count):
+    return 2 * space < count
+
+
+def by_direction(kernel):
+    here = climbs(lax.axis_index("space"), lax.axis_size("space"))
+    pl.when(here)(lambda: kernel(True))
+    pl.when(jnp.logical_not(here))(lambda: kernel(False))
+
+
+def by_place(kernel):
+    place = lax.axis_index("space") * Z_LOW // lax.axis_size("space")
+    for k in range(Z_LOW):
+        pl.when(place == k)(functools.partial(kernel, k))
+
+
 def edge_rows(first_ref, last_ref, first_mask, last_mask, out_ref):
     def write(field_ref, mask_ref, low):
         land = mask_ref[low : low + PSTEPS].astype(jnp.float32)
@@ -57,11 +74,10 @@
         write(first_ref, first_mask, 0)
 
 
-def propagate(table_ref, field_ref, mask_ref, halo_ref, a_ref, b_ref, lo_ref, hi_ref, land, ext):
+def propagate(table_ref, field_ref, mask_ref, halo_ref, out_ref, lo_ref, hi_ref, land, ext):
     p = lax.axis_index("comp")
     q = lax.rem(p, QUARTERS)
     rows, cols = mask_ref.shape
-    half = rows // 2
     high = rows + 8
 
     def run(eastward, northward):
@@ -89,8 +105,7 @@
                 along = pltpu.roll(f, 1 if eastward else cols - 1, 1)
                 across = pltpu.roll(f, 1 if northward else high - 1, 0)
                 f = (stay * f + side * along + ay * across) * land[...]
-            a_ref[i] = f[own : own + half]
-            b_ref[i] = f[own + half : own + rows]
+            out_ref[i] = f[own : own + rows]
 
             @pl.when(i < EDGE)
             def _():
@@ -110,42 +125,45 @@
         pl.when(q == k)(functools.partial(run, eastward, northward))
 
 
-def at(low_ref, mid_ref, top_ref, i, rows, low_rows):
+def at(low_ref, mid_ref, top_ref, i, rows):
     if i < 0:
-        return low_ref[i + EDGE, low_rows]
+        return low_ref[i + EDGE, rows]
     if i >= NQ:
-        return top_ref[i - NQ, low_rows]
+        return top_ref[i - NQ, rows]
     return mid_ref[i, rows]
 
 
-def attenuation(table_ref, ice_ref, thick_ref, out_ref):
+def sums(table_ref, e_ref, low_ref, top_ref, ice_ref, thick_ref, out_ref, att_ref):
     fsq = table_ref[lax.axis_index("comp"), 2 * NQ]
     depth = ice_ref[...].astype(jnp.float32) * thick_ref[...]
-    out_ref[...] = jnp.exp(-ice_rate * depth * fsq)
-
-
-def half_way(a_ref, b_ref, low_ref, top_ref, u_ref, d_ref, s1_ref, s3_ref, out_ref, prev_ref, next_ref):
-    half, cols = a_ref.shape[1:]
+    att_ref[...] = jnp.exp(-ice_rate * depth * fsq)
+
+    def write(climbed):
+        step = 3 if climbed else 1
+        for t in range(0, e_ref.shape[1], 8):
+            rows = pl.ds(t, 8)
+            e = lambda i: at(low_ref, e_ref, top_ref, i, rows)
+            for i in range(NQ):
+                out_ref[i, rows] = e(i - step) + e(i + step)
+
+    by_direction(write)
+
+
+def half_way(e_ref, low_ref, top_ref, r_ref, share_ref, prev_ref, next_ref):
+    rows, cols = e_ref.shape[1:]
     width = cols // GROUP
-    for t in range(0, 2 * half, 8):
-        first = t < half
-        mid, other, s = (a_ref, u_ref, t) if first else (b_ref, d_ref, t - half)
-        e = lambda i: at(low_ref, mid, top_ref, i, pl.ds(s, 8), pl.ds(t, 8))
+    for t in range(0, rows, 8):
+        there = pl.ds(t, 8)
+        e = lambda i: at(low_ref, e_ref, top_ref, i, there)
         total = jnp.zeros((8, cols), jnp.float32)
         for i in range(NQ):
-            near, far = e(i - 1) + e(i + 1), e(i - 3) + e(i + 3)
-            if first:
-                s1_ref[i, pl.ds(s, 8)] = near
-            else:
-                s3_ref[i, pl.ds(s, 8)] = far
-            crossed = 0.25 * mixing_rate * other[i, pl.ds(s, 8)] * (near + far)
+            around = (e(i - 1) + e(i + 1)) + (e(i - 3) + e(i + 3))
+            crossed = 0.25 * mixing_rate * r_ref[i, there] * around
             total = total + (e(i) - mixing_rate * e(i) * e(i) + crossed)
         for g in range(GROUP):
-            out_ref[g, t : t + 8] = total[:, g * width : (g + 1) * width]
-    prev_ref[:EDGE] = u_ref[:EDGE]
-    prev_ref[EDGE] = d_ref[0]
-    next_ref[:EDGE] = u_ref[NQ - EDGE :]
-    next_ref[EDGE] = d_ref[NQ - 1]
+            share_ref[g, there] = total[:, g * width : (g + 1) * width]
+    prev_ref[...] = r_ref[:EDGE]
+    next_ref[...] = r_ref[NQ - EDGE :]
 
 
 def total_to_all(parts_ref, out_ref):
@@ -156,27 +174,24 @@
         out_ref[k] = total
 
 
-def finish(table_ref, a_ref, b_ref, u_ref, d_ref, low_ref, top_ref, s1_ref, s3_ref, energy_ref, att_ref, out_ref):
-    p = lax.axis_index("comp")
-    fsq = table_ref[p, 2 * NQ]
-    half = a_ref.shape[1]
-    for t in range(0, 2 * half, 8):
-        rows = pl.ds(t, 8)
-        energy = jnp.concatenate([energy_ref[g, rows] for g in range(GROUP)], axis=1) * (1.0 / (ND * NF))
-        factor = att_ref[rows] / (1.0 + whitecap_rate * energy * fsq)
-        for i in range(NQ):
-            if t < half:
-                e = a_ref[i, rows]
-                u = lambda k: at(low_ref, u_ref, top_ref, k, rows, rows)
-                near = s1_ref[i, rows] + (u(i - 3) + u(i + 3))
-            else:
-                s = pl.ds(t - half, 8)
-                e = b_ref[i, s]
-                d = lambda k: (
-                    low_ref[EDGE, s] if k < 0 else top_ref[EDGE, s] if k >= NQ else d_ref[k, s]
-                )
-                near = s3_ref[i, s] + (d(i - 1) + d(i + 1))
-            out_ref[i, rows] = (e + mixing_rate * e * (0.25 * near - e)) * factor
+def finish(
+    table_ref, e_ref, r_ref, low_ref, top_ref, inner_ref, outer_ref, energy_ref, att_ref, told_ref, out_ref
+):
+    fsq = table_ref[lax.axis_index("comp"), 2 * NQ]
+
+    def write(climbed, s_ref):
+        step = 1 if climbed else 3
+        for t in range(0, e_ref.shape[1], 8):
+            rows = pl.ds(t, 8)
+            energy = jnp.concatenate([energy_ref[g, rows] for g in range(GROUP)], axis=1) * (1.0 / (ND * NF))
+            factor = att_ref[rows] / (1.0 + whitecap_rate * energy * fsq)
+            raw = lambda i: at(low_ref, r_ref, top_ref, i, rows)
+            for i in range(NQ):
+                e = e_ref[i, rows]
+                around = s_ref[i, rows] + (raw(i - step) + raw(i + step))
+                out_ref[i, rows] = (e + mixing_rate * e * (0.25 * around - e)) * factor
+
+    by_place(lambda k: write(k < 2, outer_ref if k in (0, 3) else inner_ref))
 
 
 def in_vmem(count):
@@ -197,20 +212,40 @@
         out_specs=specs,
         scratch_shapes=list(scratch),
         compiler_params=pltpu.CompilerParams(vmem_limit_bytes=VMEM_BYTES),
+        cost_estimate=pl.CostEstimate(flops=1024, bytes_accessed=1024, transcendentals=0),
         name=kernel.__name__,
     )
 
 
 def body(spectrum, sea_mask, ice_flag, thickness):
     comps, rows, cols = spectrum.shape
-    half = rows // 2
     n_comp = lax.axis_size("comp")
     n_space = lax.axis_size("space")
     table = jnp.asarray(tables())
 
-    def move(value, step):
-        pairs = [(p, p + step) for p in range(n_comp) if 0 <= p + step < n_comp]
-        return lax.ppermute(value, "comp", pairs)
+    def place(s):
+        return s * Z_LOW // n_space
+
+    def move(value, first, places):
+        pairs = []
+        for p in range(n_comp):
+            for s in range(n_space):
+                to = p + (GROUP if climbs(s, n_space) == first else -GROUP)
+                if 0 <= to < n_comp and place(s) in places:
+                    pairs.append((p * n_space + s, to * n_space + s))
+        return lax.ppermute(value, ("comp", "space"), pairs)
+
+    def tell(value):
+        pairs = []
+        for p in range(n_comp):
+            for s in range(n_space):
+                step = n_space // Z_LOW * (1 if place(s) == 2 else -1)
+                if place(s) in (1, 2):
+                    pairs.append((p * n_space + s, p * n_space + s + step))
+        return lax.ppermute(value, ("comp", "space"), pairs)
+
+    def after(value, *others):
+        return lax.optimization_barrier((value, *others))[0]
 
     def turn(value, step):
         pairs = [(p, p // QUARTERS * QUARTERS + (p + step) % QUARTERS) for p in range(n_comp)]
@@ -237,30 +272,22 @@
         ]
     halo = lax.ppermute(message, ("comp", "space"), pairs)
 
-    part = (comps, half, cols)
+    whole = (comps, rows, cols)
     edge = (EDGE, rows, cols)
-    a, b, lo, hi = call(
-        propagate,
-        [part, part, edge, edge],
-        True,
-        3,
-        [pltpu.VMEM((rows + 8, cols), jnp.float32), pltpu.VMEM((rows + 8, cols), jnp.float32)],
-    )(table, spectrum, sea_mask, halo)
-
-    u = move(a, -GROUP)
-    d = move(b, GROUP)
+    scratch = pltpu.VMEM((rows + 8, cols), jnp.float32)
+    e, lo, hi = call(propagate, [whole, edge, edge], True, 3, [scratch, scratch])(
+        table, spectrum, sea_mask, halo
+    )
+    received = move(e, True, (0, 1, 2, 3))
     top = turn(lo, -1)
     low = turn(hi, 1)
-    edges = (EDGE + 1, half, cols)
-    s1, s3, share, to_prev, to_next = call(
-        half_way, [part, part, (GROUP, rows, cols // GROUP), edges, edges], False, 6
-    )(a, b, low, top, u, d)
-    s1 = move(s1, GROUP)
-    s3 = move(s3, -GROUP)
-    (att,) = call(attenuation, [(rows, cols)], True, 2)(table, ice_flag, thickness)
-    top_u = turn(to_prev, -1)
-    low_u = turn(to_next, 1)
-
+    out, att = call(sums, [whole, (rows, cols)], True, 5)(table, e, low, top, ice_flag, thickness)
+    out, received = lax.optimization_barrier((out, received))
+    inner = move(out, False, (1, 2))
+
+    share, to_prev, to_next = call(half_way, [(GROUP, rows, cols // GROUP), edge, edge], False, 4)(
+        e, low, top, received
+    )
     near = [list(range(g, g + GROUP)) for g in range(0, n_comp, GROUP)]
     far = [list(range(g, n_comp, GROUP)) for g in range(GROUP)]
 
@@ -270,13 +297,20 @@
     def spread(value, copies):
         return call(total_to_all, [(copies,) + value.shape[1:]], False, 1)(value)[0]
 
-    share = spread(swap(share, near), n_comp // GROUP)
-    energy = swap(spread(swap(share, far), GROUP), near)
-
-    (out,) = call(finish, [(comps, rows, cols)], True, 10)(
-        table, a, b, u, d, low_u, top_u, s1, s3, energy, att
+    share = swap(share, near)
+    top = turn(after(to_prev, share), -1)
+    low = turn(after(to_next, share), 1)
+    share = swap(spread(share, n_comp // GROUP), far)
+    share, inner = lax.optimization_barrier((share, inner))
+    told = tell(share[0])
+    out, share, told = lax.optimization_barrier((out, share, told))
+    outer = move(out, False, (0, 3))
+    energy = swap(spread(share, GROUP), near)
+
+    (updated,) = call(finish, [whole], True, 9)(
+        table, e, received, low, top, inner, outer, energy, att, told
     )
-    return out
+    return updated
 
 
 def solution(mesh):

time: 184 us -> 166 us (0.902)
  blocking collectives: 8.38 us -> 74.2 us
  starting transfers between devices: 96.9 us -> 32.2 us
  waiting for transfers between devices: 58.6 us -> 41.9 us
    all_to_all x1 -> x2, blocking collectives: 8.38 us -> 74.2 us  [swap(): lax.all_to_all(value, 'comp', 0, 0, axis_index_groups=groups, tiled=True)]
    ppermute x4, starting transfers between devices: 64.8 us -> 14.3 us  [the longest x3 13 us: move(): return lax.ppermute(value, ('comp', 'space'), pairs)]
    all_to_all x2 -> x1, starting transfers between devices: 19.7 us -> 5.41 us  [swap(): lax.all_to_all(value, 'comp', 0, 0, axis_index_groups=groups, tiled=True)]
    ppermute x4, waiting for transfers between devices: 37.5 us -> 25 us  [the longest x3 20.7 us: move(): return lax.ppermute(value, ('comp', 'space'), pairs)]
    all_to_all x2 -> x1, waiting for transfers between devices: 8.39 us -> 3.22 us  [swap(): lax.all_to_all(value, 'comp', 0, 0, axis_index_groups=groups, tiled=True)]
    unnamed x22 -> x20, local copies, waits for them, and re-layouts: 5.32 us -> 3.53 us
  transfers between devices with their start and end apart: 11 -> 10, of which waited for: 6 -> 8; matrix products, arithmetic and copies ran while one was open for 0% -> 0% of each run, Pallas kernels for 1% -> 2%
where the time goes in v3:
time: 166 us; the launch traced here: 164 us
  blocking collectives  74.2 us (45%)
  waiting for transfers between devices  41.9 us (25%)
  starting transfers between devices  32.2 us (19%)
  Pallas kernels  12 us (7%)
  local copies, waits for them, and re-layouts  3.53 us (2%)
    all_to_all x2, blocking collectives, swap(): lax.all_to_all(value, 'comp', 0, 0, axis_index_groups=groups, tiled=True)  74.2 us
    ppermute x3, waiting for transfers between devices, move(): return lax.ppermute(value, ('comp', 'space'), pairs)  20.7 us
    ppermute x3, starting transfers between devices, move(): return lax.ppermute(value, ('comp', 'space'), pairs)  13 us
    ppermute x4, starting transfers between devices, turn(): return lax.ppermute(value, 'comp', pairs)  11.1 us
    ppermute x4, waiting for transfers between devices, turn(): return lax.ppermute(value, 'comp', pairs)  6.95 us
    ppermute x1, waiting for transfers between devices, body(): halo = lax.ppermute(message, ('comp', 'space'), pairs)  6.74 us
    all_to_all x1, starting transfers between devices, swap(): lax.all_to_all(value, 'comp', 0, 0, axis_index_groups=groups, tiled=True)  5.41 us
    ppermute x1, waiting for transfers between devices, tell(): return lax.ppermute(value, ('comp', 'space'), pairs)  4.33 us
  transfers between devices with their start and end apart: 10, of which 8 were waited for; matrix products, arithmetic and copies ran while one was open for 0% of the time, Pallas kernels for 2%

profile of v3, /device:TPU:6, one launch (start us, length us, event | category | flops | bytes accessed | tf_op | source)
XLA Modules:
  0.0 164.0 jit_solution(13489727649549990596)
XLA Ops:
  0.0 0.0 copy-start.3
  0.0 0.0 copy-start
  0.0 0.0 copy-start.1
  0.0 1.9 %edge_rows.1 = f32[40,1024]{1,0:T(8,128)} custom-call(f32[9,32,1024]{2,1,0:T(8,128)} %field_ref.1, f32[9,32,1024]{2,1,0:T(8,128)} %field_ref.1, s32[32,1024]{1,0:T(8,128)} %mask_ref.1, s32[32,1024]{1,0:T(8,128)} %mask_ref.1), custom_call_target="tpu_custom_call" | custom-call | tf_op jit(solution)/shard_map/edge_rows/pallas_call | solution.py:254
  1.9 0.0 copy-start.4
  1.9 0.0 copy-start.5
  1.9 1.4 collective-permute-start
  3.3 6.7 %collective-permute-done.halo_ref = f32[40,1024]{1,0:T(8,128)S(1)} collective-permute-done((f32[40,1024]{1,0:T(8,128)}, f32[40,1024]{1,0:T(8,128)S(1)}, u32[]{:S(2)}, u32[]{:S(2)}) %collective-permute-start) | collective-permute-done | bytes 163872 | tf_op jit(solution)/shard_map/ppermute | solution.py:273
  10.0 0.0 copy-done.3
  10.0 0.0 copy-done
  10.0 0.0 copy-done.1
  10.0 4.0 %propagate.1 = (f32[9,32,1024]{2,1,0:T(8,128)S(1)}, f32[3,32,1024]{2,1,0:T(8,128)S(1)}, f32[3,32,1024]{2,1,0:T(8,128)S(1)}) custom-call(f32[32,20]{1,0:T(8,128)S(1)} %copy-done.3, f32[9,32,1024]{2,1,0:T(8,128)S(1)} %copy-done, s32[32,1024]{1,0:T(8,128)S(1)} %copy-done.1, f32[40,1024]{1,0:T(8,128)S(1)} %collective-permute-done.halo_ref), custom_call_target="tpu_custom_call" | custom-call | flops 1024 | bytes 1024 | tf_op jit(solution)/shard_map/propagate/pallas_call | solution.py:278
  14.1 11.0 %collective-permute-start.3 = (f32[9,32,1024]{2,1,0:T(8,128)S(1)}, f32[9,32,1024]{2,1,0:T(8,128)S(1)}, u32[]{:S(2)}, u32[]{:S(2)}) collective-permute-start(f32[9,32,1024]{2,1,0:T(8,128)S(1)} %get-tuple-element.22.e_ref), channel_id=1, source_target_pairs={{0,256},{1,257},{2,258},{3,259},{4,260},{5,261},{6,262},{7,263},{8... | collective-permute-start | bytes 3538952 | tf_op jit(solution)/shard_map/ppermute | solution.py:236
  25.1 1.9 %collective-permute-start.1 = (f32[3,32,1024]{2,1,0:T(8,128)S(1)}, f32[3,32,1024]{2,1,0:T(8,128)S(1)}, u32[]{:S(2)}, u32[]{:S(2)}) collective-permute-start(f32[3,32,1024]{2,1,0:T(8,128)S(1)} %get-tuple-element.23), channel_id=1, source_target_pairs={{0,32},{32,64},{64,96},{96,0},{128,160},{160,192},{192,224},{224,1... | collective-permute-start | bytes 1179656 | tf_op jit(solution)/shard_map/ppermute | solution.py:252
  27.0 3.6 %collective-permute-start.2 = (f32[3,32,1024]{2,1,0:T(8,128)S(1)}, f32[3,32,1024]{2,1,0:T(8,128)S(1)}, u32[]{:S(2)}, u32[]{:S(2)}) collective-permute-start(f32[3,32,1024]{2,1,0:T(8,128)S(1)} %get-tuple-element.24), channel_id=1, source_target_pairs={{0,96},{32,0},{64,32},{96,64},{128,224},{160,128},{192,160},{224,1... | collective-permute-start | bytes 1179656 | tf_op jit(solution)/shard_map/ppermute | solution.py:252
  30.7 4.7 %collective-permute-done.1.low_ref = f32[3,32,1024]{2,1,0:T(8,128)S(1)} collective-permute-done((f32[3,32,1024]{2,1,0:T(8,128)S(1)}, f32[3,32,1024]{2,1,0:T(8,128)S(1)}, u32[]{:S(2)}, u32[]{:S(2)}) %collective-permute-start.1) | collective-permute-done | bytes 393248 | tf_op jit(solution)/shard_map/ppermute | solution.py:252
  35.4 1.3 collective-permute-done.2.top_ref
  36.7 0.0 copy-done.4
  36.7 0.0 copy-done.5
  36.7 2.0 %sums.1 = (f32[9,32,1024]{2,1,0:T(8,128)}, f32[32,1024]{1,0:T(8,128)S(1)}) custom-call(f32[32,20]{1,0:T(8,128)S(1)} %copy-done.3, f32[9,32,1024]{2,1,0:T(8,128)S(1)} %get-tuple-element.22.e_ref, f32[3,32,1024]{2,1,0:T(8,128)S(1)} %collective-permute-done.1.low_ref, f32[3,32,1024]{2,1,0:T(8,128)S(1)} %collective-permute-done.2.top_ref, ...), custom_call_target="tpu_custom_call" | custom-call | flops 1024 | bytes 1024 | tf_op jit(solution)/shard_map/sums/pallas_call | solution.py:284
  38.6 0.0 copy-start.6
  38.6 0.6 copy-done.6
  39.3 10.8 %collective-permute-done.3.r_ref = f32[9,32,1024]{2,1,0:T(8,128)S(1)} collective-permute-done((f32[9,32,1024]{2,1,0:T(8,128)S(1)}, f32[9,32,1024]{2,1,0:T(8,128)S(1)}, u32[]{:S(2)}, u32[]{:S(2)}) %collective-permute-start.3) | collective-permute-done | bytes 1179680 | tf_op jit(solution)/shard_map/ppermute | solution.py:236
  50.1 0.7 collective-permute-start.6
  50.8 1.3 half_way.1
  52.1 8.4 %all_to_all.15.parts_ref = f32[8,32,128]{2,1,0:T(8,128)S(1)} all-to-all(f32[8,32,128]{2,1,0:T(8,128)S(1)} %get-tuple-element.28), channel_id=1, replica_groups={{0,32,64,96,128,160,192,224},{256,288,320,352,384,416,448,480},{512,544..., dimensions={0} | all-to-all | bytes 262144 | tf_op jit(solution)/shard_map/all_to_all | solution.py:295
  60.4 65.8 %all_to_all.16.parts_ref = f32[4,32,128]{2,1,0:T(8,128)S(1)} all-to-all(f32[4,32,128]{2,1,0:T(8,128)S(1)} %total_to_all.2), channel_id=1, replica_groups={{0,256,512,768},{32,288,544,800},{64,320,576,832},{96,352,608,864},{128..., dimensions={0} | all-to-all | bytes 131072 | tf_op jit(solution)/shard_map/all_to_all | solution.py:295
  126.2 0.0 collective-permute-done.6.inner_ref
  126.3 1.3 collective-permute-start.7
  127.5 4.3 %collective-permute-done.7.told_ref = f32[32,128]{1,0:T(8,128)S(1)} collective-permute-done((f32[32,128]{1,0:T(8,128)S(1)}, f32[32,128]{1,0:T(8,128)S(1)}, u32[]{:S(2)}, u32[]{:S(2)}) %collective-permute-start.7) | collective-permute-done | bytes 16416 | tf_op jit(solution)/shard_map/ppermute | solution.py:245
  131.9 0.0 copy-start.8
  131.9 0.6 copy-done.8
  132.5 1.3 collective-permute-start.8
  133.8 1.9 %collective-permute-start.4 = (f32[3,32,1024]{2,1,0:T(8,128)}, f32[3,32,1024]{2,1,0:T(8,128)}, u32[]{:S(2)}, u32[]{:S(2)}) collective-permute-start(f32[3,32,1024]{2,1,0:T(8,128)} %get-tuple-element.29), channel_id=1, source_target_pairs={{0,32},{32,64},{64,96},{96,0},{128,160},{160,192},{192,224},{224,1... | collective-permute-start | bytes 1179656 | tf_op jit(solution)/shard_map/ppermute | solution.py:252
  135.7 3.6 %collective-permute-start.5 = (f32[3,32,1024]{2,1,0:T(8,128)}, f32[3,32,1024]{2,1,0:T(8,128)}, u32[]{:S(2)}, u32[]{:S(2)}) collective-permute-start(f32[3,32,1024]{2,1,0:T(8,128)} %get-tuple-element.31), channel_id=1, source_target_pairs={{0,96},{32,0},{64,32},{96,64},{128,224},{160,128},{192,160},{224,1... | collective-permute-start | bytes 1179656 | tf_op jit(solution)/shard_map/ppermute | solution.py:252
  139.4 0.0 copy-start.2
  139.4 0.6 copy-done.2
  140.0 5.4 %all-to-all-start.2 = ((f32[8,32,128]{2,1,0:T(8,128)}), f32[8,32,128]{2,1,0:T(8,128)}, u32[]{:S(2)}, u32[]{:S(2)}) async-start(f32[8,32,128]{2,1,0:T(8,128)} %copy-done.2), calls=%async_computation.2 | async-start | bytes 262144 | tf_op jit(solution)/shard_map/all_to_all | solution.py:295
  145.4 0.0 collective-permute-done.4.low_ref
  145.4 1.0 collective-permute-done.5.top_ref
  146.4 3.2 %all-to-all-done.2.energy_ref = f32[8,32,128]{2,1,0:T(8,128)} async-done(((f32[8,32,128]{2,1,0:T(8,128)}), f32[8,32,128]{2,1,0:T(8,128)}, u32[]{:S(2)}, u32[]{:S(2)}) %all-to-all-start.2) | async-done | bytes 131104 | tf_op jit(solution)/shard_map/all_to_all | solution.py:295
  149.6 9.9 %collective-permute-done.8.outer_ref = f32[9,32,1024]{2,1,0:T(8,128)} collective-permute-done((f32[9,32,1024]{2,1,0:T(8,128)}, f32[9,32,1024]{2,1,0:T(8,128)}, u32[]{:S(2)}, u32[]{:S(2)}) %collective-permute-start.8) | collective-permute-done | bytes 1179680 | tf_op jit(solution)/shard_map/ppermute | solution.py:236
  159.5 0.0 copy-start.7
  159.5 0.9 copy-done.7
  160.4 0.0 copy-start.9
  160.4 0.7 copy-done.9
  161.1 2.9 %finish.1 = f32[9,32,1024]{2,1,0:T(8,128)} custom-call(f32[32,20]{1,0:T(8,128)S(1)} %copy-done.3, f32[9,32,1024]{2,1,0:T(8,128)S(1)} %get-tuple-element.22.e_ref, f32[9,32,1024]{2,1,0:T(8,128)S(1)} %collective-permute-done.3.r_ref, f32[3,32,1024]{2,1,0:T(8,128)} %collective-permute-done.4.low_ref, f32[3,32,1024]{2,1,0:T(8,128)} %collective-permute-done.5.top_ref, ...), custom_call_target="tpu_custom_call" | custom-call | flops 1024 | bytes 1024 | tf_op jit(solution)/shard_map/finish/pallas_call | solution.py:310
  (3 shorter events, 0.0 us)
Async XLA Ops:
  0.0 10.0 %copy-start.3 = (f32[32,20]{1,0:T(8,128)S(1)}, f32[32,20]{1,0:T(8,128)}, u32[]{:S(2)}) copy-start(f32[32,20]{1,0:T(8,128)} %constant.2.clone.table_ref) | copy-start | bytes 7684
  0.0 10.0 %copy-start = (f32[9,32,1024]{2,1,0:T(8,128)S(1)}, f32[9,32,1024]{2,1,0:T(8,128)}, u32[]{:S(2)}) copy-start(f32[9,32,1024]{2,1,0:T(8,128)} %field_ref.1) | copy-start | bytes 3538948
  0.0 10.0 %copy-start.1 = (s32[32,1024]{1,0:T(8,128)S(1)}, s32[32,1024]{1,0:T(8,128)}, u32[]{:S(2)}) copy-start(s32[32,1024]{1,0:T(8,128)} %mask_ref.1) | copy-start | bytes 393220
  1.9 34.8 %copy-start.4 = (s32[32,1024]{1,0:T(8,128)S(1)}, s32[32,1024]{1,0:T(8,128)}, u32[]{:S(2)}) copy-start(s32[32,1024]{1,0:T(8,128)} %ice_ref.1) | copy-start | bytes 393220
  1.9 34.8 %copy-start.5 = (f32[32,1024]{1,0:T(8,128)S(1)}, f32[32,1024]{1,0:T(8,128)}, u32[]{:S(2)}) copy-start(f32[32,1024]{1,0:T(8,128)} %thick_ref.1) | copy-start | bytes 393220
  1.9 8.2 %collective-permute-start = (f32[40,1024]{1,0:T(8,128)}, f32[40,1024]{1,0:T(8,128)S(1)}, u32[]{:S(2)}, u32[]{:S(2)}) collective-permute-start(f32[40,1024]{1,0:T(8,128)} %edge_rows.1), channel_id=1, source_target_pairs={{0,1},{1,2},{2,3},{3,4},{4,5},{5,6},{6,7},{7,8},{8,9},{9,10},{10,1... | collective-permute-start | bytes 491528 | tf_op jit(solution)/shard_map/ppermute | solution.py:273
  14.1 36.0 %collective-permute-start.3 = (f32[9,32,1024]{2,1,0:T(8,128)S(1)}, f32[9,32,1024]{2,1,0:T(8,128)S(1)}, u32[]{:S(2)}, u32[]{:S(2)}) collective-permute-start(f32[9,32,1024]{2,1,0:T(8,128)S(1)} %get-tuple-element.22.e_ref), channel_id=1, source_target_pairs={{0,256},{1,257},{2,258},{3,259},{4,260},{5,261},{6,262},{7,263},{8... | collective-permute-start | bytes 3538952 | tf_op jit(solution)/shard_map/ppermute | solution.py:236
  25.1 10.3 %collective-permute-start.1 = (f32[3,32,1024]{2,1,0:T(8,128)S(1)}, f32[3,32,1024]{2,1,0:T(8,128)S(1)}, u32[]{:S(2)}, u32[]{:S(2)}) collective-permute-start(f32[3,32,1024]{2,1,0:T(8,128)S(1)} %get-tuple-element.23), channel_id=1, source_target_pairs={{0,32},{32,64},{64,96},{96,0},{128,160},{160,192},{192,224},{224,1... | collective-permute-start | bytes 1179656 | tf_op jit(solution)/shard_map/ppermute | solution.py:252
  27.0 9.6 %collective-permute-start.2 = (f32[3,32,1024]{2,1,0:T(8,128)S(1)}, f32[3,32,1024]{2,1,0:T(8,128)S(1)}, u32[]{:S(2)}, u32[]{:S(2)}) collective-permute-start(f32[3,32,1024]{2,1,0:T(8,128)S(1)} %get-tuple-element.24), channel_id=1, source_target_pairs={{0,96},{32,0},{64,32},{96,64},{128,224},{160,128},{192,160},{224,1... | collective-permute-start | bytes 1179656 | tf_op jit(solution)/shard_map/ppermute | solution.py:252
  38.6 0.6 copy-start.6
  50.1 76.2 %collective-permute-start.6 = (f32[9,32,1024]{2,1,0:T(8,128)}, f32[9,32,1024]{2,1,0:T(8,128)S(1)}, u32[]{:S(2)}, u32[]{:S(2)}) collective-permute-start(f32[9,32,1024]{2,1,0:T(8,128)} %get-tuple-element.35), channel_id=1, source_target_pairs={{16,272},{17,273},{18,274},{19,275},{20,276},{21,277},{22,278},{23... | collective-permute-start | bytes 3538952 | tf_op jit(solution)/shard_map/ppermute | solution.py:236
  126.3 5.6 %collective-permute-start.7 = (f32[32,128]{1,0:T(8,128)S(1)}, f32[32,128]{1,0:T(8,128)S(1)}, u32[]{:S(2)}, u32[]{:S(2)}) collective-permute-start(f32[32,128]{1,0:T(8,128)S(1)} %slice_bitcast_fusion), channel_id=1, source_target_pairs={{8,0},{9,1},{10,2},{11,3},{12,4},{13,5},{14,6},{15,7},{16,24},{17,... | collective-permute-start | bytes 49160 | tf_op jit(solution)/shard_map/ppermute | solution.py:245
  131.9 0.6 copy-start.8
  132.5 27.0 %collective-permute-start.8 = (f32[9,32,1024]{2,1,0:T(8,128)}, f32[9,32,1024]{2,1,0:T(8,128)}, u32[]{:S(2)}, u32[]{:S(2)}) collective-permute-start(f32[9,32,1024]{2,1,0:T(8,128)} %get-tuple-element.35), channel_id=1, source_target_pairs={{24,280},{25,281},{26,282},{27,283},{28,284},{29,285},{30,286},{31... | collective-permute-start | bytes 3538952 | tf_op jit(solution)/shard_map/ppermute | solution.py:236
  133.8 11.7 %collective-permute-start.4 = (f32[3,32,1024]{2,1,0:T(8,128)}, f32[3,32,1024]{2,1,0:T(8,128)}, u32[]{:S(2)}, u32[]{:S(2)}) collective-permute-start(f32[3,32,1024]{2,1,0:T(8,128)} %get-tuple-element.29), channel_id=1, source_target_pairs={{0,32},{32,64},{64,96},{96,0},{128,160},{160,192},{192,224},{224,1... | collective-permute-start | bytes 1179656 | tf_op jit(solution)/shard_map/ppermute | solution.py:252
  135.7 10.7 %collective-permute-start.5 = (f32[3,32,1024]{2,1,0:T(8,128)}, f32[3,32,1024]{2,1,0:T(8,128)}, u32[]{:S(2)}, u32[]{:S(2)}) collective-permute-start(f32[3,32,1024]{2,1,0:T(8,128)} %get-tuple-element.31), channel_id=1, source_target_pairs={{0,96},{32,0},{64,32},{96,64},{128,224},{160,128},{192,160},{224,1... | collective-permute-start | bytes 1179656 | tf_op jit(solution)/shard_map/ppermute | solution.py:252
  139.4 0.7 copy-start.2
  140.0 9.6 %all-to-all-start.2 = ((f32[8,32,128]{2,1,0:T(8,128)}), f32[8,32,128]{2,1,0:T(8,128)}, u32[]{:S(2)}, u32[]{:S(2)}) async-start(f32[8,32,128]{2,1,0:T(8,128)} %copy-done.2), calls=%async_computation.2 | async-start | bytes 262144 | tf_op jit(solution)/shard_map/all_to_all | solution.py:295
  159.5 0.9 copy-start.7
  160.4 0.7 copy-start.9

commit v4 on v3

--- a/solution.py
+++ b/solution.py
@@ -74,99 +74,132 @@
         write(first_ref, first_mask, 0)
 
 
-def propagate(table_ref, field_ref, mask_ref, halo_ref, out_ref, lo_ref, hi_ref, land, ext):
+def by_quarter(kernel):
+    for k, signs in enumerate(((True, True), (False, True), (False, False), (True, False))):
+        pl.when(quarter() == k)(functools.partial(kernel, *signs))
+
+
+def steps(table_ref, i, land, field, eastward, northward):
     p = lax.axis_index("comp")
-    q = lax.rem(p, QUARTERS)
-    rows, cols = mask_ref.shape
-    high = rows + 8
-
+    high, cols = field.shape
+    column = lax.broadcasted_iota(jnp.int32, (1, cols), 1)
+    inner = (column != (0 if eastward else cols - 1)).astype(jnp.float32)
+    ax = table_ref[p, i]
+    ay = table_ref[p, NQ + i]
+    stay = 1.0 - ax - ay
+    side = inner * ax
+    for _ in range(PSTEPS):
+        along = pltpu.roll(field, 1 if eastward else cols - 1, 1)
+        across = pltpu.roll(field, 1 if northward else high - 1, 0)
+        field = (stay * field + side * along + ay * across) * land[...]
+    return field
+
+
+def inner_rows(table_ref, field_ref, mask_ref, mid_ref, land):
     def run(eastward, northward):
-        own = 8 if northward else 0
-        halo = 8 - PSTEPS if northward else rows
-        rest = 0 if northward else rows + PSTEPS
-        zeros = jnp.zeros((8 - PSTEPS, cols), jnp.float32)
-        land[own : own + rows] = mask_ref[...].astype(jnp.float32)
-        land[halo : halo + PSTEPS] = halo_ref[PSTEPS * NQ :]
+        low = 0 if northward else 8
+        land[...] = mask_ref[low : low + 24].astype(jnp.float32)
+
+        def component(i, carry):
+            f = steps(table_ref, i, land, field_ref[i, low : low + 24] * land[...], eastward, northward)
+            mid_ref[i] = f[8 - low : 24 - low]
+            return carry
+
+        lax.fori_loop(0, NQ, component, 0)
+
+    by_quarter(run)
+
+
+def outer_rows(table_ref, field_ref, mask_ref, halo_ref, mid_ref, rim_ref, lo_ref, hi_ref, land, ext):
+    def run(eastward, northward):
+        halo = 8 - PSTEPS if northward else 24
+        rest = 0 if northward else 24 + PSTEPS
+        own = ((8, 0), (16, 16), (24, 24)) if northward else ((0, 0), (8, 8), (16, 24))
+        zeros = jnp.zeros((8 - PSTEPS, land.shape[1]), jnp.float32)
         land[rest : rest + 8 - PSTEPS] = zeros
         ext[rest : rest + 8 - PSTEPS] = zeros
-        column = lax.broadcasted_iota(jnp.int32, (1, cols), 1)
-        inner = (column != (0 if eastward else cols - 1)).astype(jnp.float32)
+        land[halo : halo + PSTEPS] = halo_ref[PSTEPS * NQ :]
+        for to, row in own:
+            land[to : to + 8] = mask_ref[row : row + 8].astype(jnp.float32)
 
         def component(i, carry):
-            ext[own : own + rows] = field_ref[i] * land[own : own + rows]
             for r in range(PSTEPS):
                 ext[halo + r : halo + r + 1] = halo_ref[pl.ds(PSTEPS * i + r, 1)]
-            ax = table_ref[p, i]
-            ay = table_ref[p, NQ + i]
-            stay = 1.0 - ax - ay
-            side = inner * ax
-            f = ext[...]
-            for _ in range(PSTEPS):
-                along = pltpu.roll(f, 1 if eastward else cols - 1, 1)
-                across = pltpu.roll(f, 1 if northward else high - 1, 0)
-                f = (stay * f + side * along + ay * across) * land[...]
-            out_ref[i] = f[own : own + rows]
-
-            @pl.when(i < EDGE)
-            def _():
-                lo_ref[i] = f[own : own + rows]
-
-            @pl.when(i >= NQ - EDGE)
-            def _():
-                hi_ref[i - (NQ - EDGE)] = f[own : own + rows]
-
+            for to, row in own:
+                ext[to : to + 8] = field_ref[i, row : row + 8] * land[to : to + 8]
+            f = steps(table_ref, i, land, ext[...], eastward, northward)
+            e0 = f[8:16] if northward else f[0:8]
+            e3 = f[24:32] if northward else f[16:24]
+            rim_ref[i, 0:8] = e0
+            rim_ref[i, 8:16] = e3
+
+            def edge(ref, k):
+                ref[k, 0:8] = e0
+                ref[k, 8:24] = mid_ref[i]
+                ref[k, 24:32] = e3
+
+            pl.when(i < EDGE)(lambda: edge(lo_ref, i))
+            pl.when(i >= NQ - EDGE)(lambda: edge(hi_ref, i - (NQ - EDGE)))
             return carry
 
         lax.fori_loop(0, NQ, component, 0)
 
-    for k, (eastward, northward) in enumerate(
-        ((True, True), (False, True), (False, False), (True, False))
-    ):
-        pl.when(q == k)(functools.partial(run, eastward, northward))
-
-
-def at(low_ref, mid_ref, top_ref, i, rows):
+    by_quarter(run)
+
+
+def part_of(mid_ref, rim_ref, t):
+    if 8 <= t < 24:
+        return mid_ref, pl.ds(t - 8, 8)
+    return rim_ref, pl.ds(0 if t < 8 else 8, 8)
+
+
+def at(low_ref, mid_ref, top_ref, i, rows, edge_rows):
     if i < 0:
-        return low_ref[i + EDGE, rows]
+        return low_ref[i + EDGE, edge_rows]
     if i >= NQ:
-        return top_ref[i - NQ, rows]
+        return top_ref[i - NQ, edge_rows]
     return mid_ref[i, rows]
 
 
-def sums(table_ref, e_ref, low_ref, top_ref, ice_ref, thick_ref, out_ref, att_ref):
+def sums(table_ref, mid_ref, rim_ref, low_ref, top_ref, ice_ref, thick_ref, out_ref, att_ref):
     fsq = table_ref[lax.axis_index("comp"), 2 * NQ]
     depth = ice_ref[...].astype(jnp.float32) * thick_ref[...]
     att_ref[...] = jnp.exp(-ice_rate * depth * fsq)
 
     def write(climbed):
         step = 3 if climbed else 1
-        for t in range(0, e_ref.shape[1], 8):
+        for t in range(0, out_ref.shape[1], 8):
             rows = pl.ds(t, 8)
-            e = lambda i: at(low_ref, e_ref, top_ref, i, rows)
+            e_ref, e_rows = part_of(mid_ref, rim_ref, t)
+            e = lambda i: at(low_ref, e_ref, top_ref, i, e_rows, rows)
             for i in range(NQ):
                 out_ref[i, rows] = e(i - step) + e(i + step)
 
     by_direction(write)
 
 
-def half_way(e_ref, low_ref, top_ref, r_ref, share_ref, prev_ref, next_ref):
-    rows, cols = e_ref.shape[1:]
+def half_way(mid_ref, rim_ref, low_ref, top_ref, r_mid_ref, r_rim_ref, share_ref, prev_ref, next_ref):
+    rows, cols = low_ref.shape[1:]
     width = cols // GROUP
     for t in range(0, rows, 8):
         there = pl.ds(t, 8)
-        e = lambda i: at(low_ref, e_ref, top_ref, i, there)
+        e_ref, e_rows = part_of(mid_ref, rim_ref, t)
+        r_ref, _ = part_of(r_mid_ref, r_rim_ref, t)
+        e = lambda i: at(low_ref, e_ref, top_ref, i, e_rows, there)
         total = jnp.zeros((8, cols), jnp.float32)
         for i in range(NQ):
             around = (e(i - 1) + e(i + 1)) + (e(i - 3) + e(i + 3))
-            crossed = 0.25 * mixing_rate * r_ref[i, there] * around
+            crossed = 0.25 * mixing_rate * r_ref[i, e_rows] * around
             total = total + (e(i) - mixing_rate * e(i) * e(i) + crossed)
         for g in range(GROUP):
             share_ref[g, there] = total[:, g * width : (g + 1) * width]
-    prev_ref[...] = r_ref[:EDGE]
-    next_ref[...] = r_ref[NQ - EDGE :]
-
-
-def total_to_all(parts_ref, out_ref):
+        for k in range(EDGE):
+            prev_ref[k, there] = r_ref[k, e_rows]
+            next_ref[k, there] = r_ref[NQ - EDGE + k, e_rows]
+
+
+def total_to_all(parts_ref, *refs):
+    out_ref = refs[-1]
     total = parts_ref[0]
     for k in range(1, parts_ref.shape[0]):
         total = total + parts_ref[k]
@@ -175,19 +208,21 @@
 
 
 def finish(
-    table_ref, e_ref, r_ref, low_ref, top_ref, inner_ref, outer_ref, energy_ref, att_ref, told_ref, out_ref
+    table_ref, mid_ref, rim_ref, r_mid_ref, r_rim_ref, low_ref, top_ref, inner_ref, outer_ref, energy_ref, att_ref, out_ref
 ):
     fsq = table_ref[lax.axis_index("comp"), 2 * NQ]
 
     def write(climbed, s_ref):
         step = 1 if climbed else 3
-        for t in range(0, e_ref.shape[1], 8):
+        for t in range(0, out_ref.shape[1], 8):
             rows = pl.ds(t, 8)
+            e_ref, e_rows = part_of(mid_ref, rim_ref, t)
+            r_ref, _ = part_of(r_mid_ref, r_rim_ref, t)
             energy = jnp.concatenate([energy_ref[g, rows] for g in range(GROUP)], axis=1) * (1.0 / (ND * NF))
             factor = att_ref[rows] / (1.0 + whitecap_rate * energy * fsq)
-            raw = lambda i: at(low_ref, r_ref, top_ref, i, rows)
+            raw = lambda i: at(low_ref, r_ref, top_ref, i, e_rows, rows)
             for i in range(NQ):
-                e = e_ref[i, rows]
+                e = e_ref[i, e_rows]
                 around = s_ref[i, rows] + (raw(i - step) + raw(i + step))
                 out_ref[i, rows] = (e + mixing_rate * e * (0.25 * around - e)) * factor
 
@@ -239,9 +274,8 @@
         pairs = []
         for p in range(n_comp):
             for s in range(n_space):
-                step = n_space // Z_LOW * (1 if place(s) == 2 else -1)
-                if place(s) in (1, 2):
-                    pairs.append((p * n_space + s, p * n_space + s + step))
+                if place(s) == 2:
+                    pairs.append((p * n_space + s, p * n_space + s + n_space // Z_LOW))
         return lax.ppermute(value, ("comp", "space"), pairs)
 
     def after(value, *others):
@@ -273,20 +307,28 @@
     halo = lax.ppermute(message, ("comp", "space"), pairs)
 
     whole = (comps, rows, cols)
+    part = (comps, 16, cols)
     edge = (EDGE, rows, cols)
-    scratch = pltpu.VMEM((rows + 8, cols), jnp.float32)
-    e, lo, hi = call(propagate, [whole, edge, edge], True, 3, [scratch, scratch])(
-        table, spectrum, sea_mask, halo
-    )
-    received = move(e, True, (0, 1, 2, 3))
+
+    def land(high):
+        return pltpu.VMEM((high, cols), jnp.float32)
+
+    (mid,) = call(inner_rows, [part], True, 2, [land(24)])(table, spectrum, sea_mask)
+    r_mid = move(mid, True, (0, 1, 2, 3))
+    rim, lo, hi = call(outer_rows, [part, edge, edge], True, 4, [land(32), land(32)])(
+        table, spectrum, sea_mask, halo, mid
+    )
+    r_rim = move(rim, True, (0, 1, 2, 3))
     top = turn(lo, -1)
     low = turn(hi, 1)
-    out, att = call(sums, [whole, (rows, cols)], True, 5)(table, e, low, top, ice_flag, thickness)
-    out, received = lax.optimization_barrier((out, received))
+    out, att = call(sums, [whole, (rows, cols)], True, 6)(
+        table, mid, rim, low, top, ice_flag, thickness
+    )
+    out, r_mid, r_rim = lax.optimization_barrier((out, r_mid, r_rim))
     inner = move(out, False, (1, 2))
 
-    share, to_prev, to_next = call(half_way, [(GROUP, rows, cols // GROUP), edge, edge], False, 4)(
-        e, low, top, received
+    share, to_prev, to_next = call(half_way, [(GROUP, rows, cols // GROUP), edge, edge], False, 6)(
+        mid, rim, low, top, r_mid, r_rim
     )
     near = [list(range(g, g + GROUP)) for g in range(0, n_comp, GROUP)]
     far = [list(range(g, n_comp, GROUP)) for g in range(GROUP)]
@@ -294,8 +336,8 @@
     def swap(value, groups):
         return lax.all_to_all(value, "comp", 0, 0, axis_index_groups=groups, tiled=True)
 
-    def spread(value, copies):
-        return call(total_to_all, [(copies,) + value.shape[1:]], False, 1)(value)[0]
+    def spread(value, copies, *others):
+        return call(total_to_all, [(copies,) + value.shape[1:]], False, 1 + len(others))(value, *others)[0]
 
     share = swap(share, near)
     top = turn(after(to_prev, share), -1)
@@ -305,10 +347,10 @@
     told = tell(share[0])
     out, share, told = lax.optimization_barrier((out, share, told))
     outer = move(out, False, (0, 3))
-    energy = swap(spread(share, GROUP), near)
-
-    (updated,) = call(finish, [whole], True, 9)(
-        table, e, received, low, top, inner, outer, energy, att, told
+    energy = swap(spread(share, GROUP, told), near)
+
+    (updated,) = call(finish, [whole], True, 10)(
+        table, mid, rim, r_mid, r_rim, low, top, inner, outer, energy, att
     )
     return updated
 

time: 166 us -> 157 us (0.946)
  waiting for transfers between devices: 41.9 us -> 24.9 us
  starting transfers between devices: 32.2 us -> 41.6 us
  Pallas kernels: 12 us -> 15.8 us
  blocking collectives: 74.2 us -> 71.8 us
    ppermute x3 -> x4, starting transfers between devices: 13 us -> 24 us  [move(): return lax.ppermute(value, ('comp', 'space'), pairs)]
    ppermute x3 -> x4, waiting for transfers between devices: 20.7 us -> 11.9 us  [move(): return lax.ppermute(value, ('comp', 'space'), pairs)]
    ppermute x1, waiting for transfers between devices: 6.74 us -> 0.01 us  [body(): halo = lax.ppermute(message, ('comp', 'space'), pairs)]
    ppermute x4, waiting for transfers between devices: 6.95 us -> 11.5 us  [turn(): return lax.ppermute(value, 'comp', pairs)]
    ppermute x1, waiting for transfers between devices: 4.33 us -> 0.01 us  [tell(): return lax.ppermute(value, ('comp', 'space'), pairs)]
    pallas_call x6 -> x7, Pallas kernels: 10.2 us -> 14 us  [the longest x1 3.79 us: body(): call(outer_rows, [part, edge, edge], True, 4, [land(32), land(32)])]
    all_to_all x2, blocking collectives: 74.2 us -> 71.8 us  [swap(): lax.all_to_all(value, 'comp', 0, 0, axis_index_groups=groups, tiled=True)]
    all_to_all x1, waiting for transfers between devices: 3.22 us -> 1.54 us  [swap(): lax.all_to_all(value, 'comp', 0, 0, axis_index_groups=groups, tiled=True)]
  transfers between devices with their start and end apart: 10 -> 11, of which waited for: 8 -> 5; matrix products, arithmetic and copies ran while one was open for 0% -> 0% of each run, Pallas kernels for 2% -> 7%
where the time goes in v4:
time: 157 us
  blocking collectives  71.8 us (46%)
  starting transfers between devices  41.6 us (26%)
  waiting for transfers between devices  24.9 us (16%)
  Pallas kernels  15.8 us (10%)
  local copies, waits for them, and re-layouts  2.34 us (1%)
    all_to_all x2, blocking collectives, swap(): lax.all_to_all(value, 'comp', 0, 0, axis_index_groups=groups, tiled=True)  71.8 us
    ppermute x4, starting transfers between devices, move(): return lax.ppermute(value, ('comp', 'space'), pairs)  24 us
    ppermute x4, waiting for transfers between devices, move(): return lax.ppermute(value, ('comp', 'space'), pairs)  11.9 us
    ppermute x4, waiting for transfers between devices, turn(): return lax.ppermute(value, 'comp', pairs)  11.5 us
    ppermute x4, starting transfers between devices, turn(): return lax.ppermute(value, 'comp', pairs)  11.1 us
    all_to_all x1, starting transfers between devices, swap(): lax.all_to_all(value, 'comp', 0, 0, axis_index_groups=groups, tiled=True)  4.51 us
    pallas_call x1, Pallas kernels, body(): call(outer_rows, [part, edge, edge], True, 4, [land(32), land(32)])  3.79 us
    pallas_call x1, Pallas kernels, body(): call(inner_rows, [part], True, 2, [land(24)])(table, spectrum, sea_mask)  3.68 us
  transfers between devices with their start and end apart: 11, of which 5 were waited for; matrix products, arithmetic and copies ran while one was open for 0% of the time, Pallas kernels for 7%

profile of v4, /device:TPU:6, one launch (start us, length us, event | category | flops | bytes accessed | tf_op | source)
XLA Modules:
  0.0 156.6 jit_solution(17553379784062564620)
XLA Ops:
  0.0 0.0 copy-start.4
  0.0 0.0 copy-start
  0.0 0.0 copy-start.1
  0.0 1.9 %edge_rows.1 = f32[40,1024]{1,0:T(8,128)} custom-call(f32[9,32,1024]{2,1,0:T(8,128)} %field_ref.3, f32[9,32,1024]{2,1,0:T(8,128)} %field_ref.3, s32[32,1024]{1,0:T(8,128)} %mask_ref.3, s32[32,1024]{1,0:T(8,128)} %mask_ref.3), custom_call_target="tpu_custom_call" | custom-call | tf_op jit(solution)/shard_map/edge_rows/pallas_call | solution.py:288
  1.9 1.3 collective-permute-start
  3.2 0.0 copy-done.4
  3.2 0.0 copy-done
  3.2 0.0 copy-done.1
  3.2 3.7 %inner_rows.1.mid_ref = f32[9,16,1024]{2,1,0:T(8,128)S(1)} custom-call(f32[32,20]{1,0:T(8,128)S(1)} %copy-done.4, f32[9,32,1024]{2,1,0:T(8,128)S(1)} %copy-done, s32[32,1024]{1,0:T(8,128)S(1)} %copy-done.1), custom_call_target="tpu_custom_call" | custom-call | flops 1024 | bytes 1024 | tf_op jit(solution)/shard_map/inner_rows/pallas_call | solution.py:316
  6.9 0.0 copy-start.5
  6.9 0.0 copy-start.6
  6.9 11.1 %collective-permute-start.3 = (f32[9,16,1024]{2,1,0:T(8,128)S(1)}, f32[9,16,1024]{2,1,0:T(8,128)S(1)}, u32[]{:S(2)}, u32[]{:S(2)}) collective-permute-start(f32[9,16,1024]{2,1,0:T(8,128)S(1)} %inner_rows.1.mid_ref), channel_id=1, source_target_pairs={{0,256},{1,257},{2,258},{3,259},{4,260},{5,261},{6,262},{7,263},{8... | collective-permute-start | bytes 1769480 | tf_op jit(solution)/shard_map/ppermute | solution.py:271
  18.0 0.0 collective-permute-done.halo_ref
  18.0 3.8 %outer_rows.1 = (f32[9,16,1024]{2,1,0:T(8,128)S(1)}, f32[3,32,1024]{2,1,0:T(8,128)S(1)}, f32[3,32,1024]{2,1,0:T(8,128)S(1)}) custom-call(f32[32,20]{1,0:T(8,128)S(1)} %copy-done.4, f32[9,32,1024]{2,1,0:T(8,128)S(1)} %copy-done, s32[32,1024]{1,0:T(8,128)S(1)} %copy-done.1, f32[40,1024]{1,0:T(8,128)S(1)} %collective-permute-done.halo_ref, ...), custom_call_target="tpu_custom_call" | custom-call | flops 1024 | bytes 1024 | tf_op jit(solution)/shard_map/outer_rows/pallas_call | solution.py:318
  21.8 10.9 %collective-permute-start.4 = (f32[9,16,1024]{2,1,0:T(8,128)S(1)}, f32[9,16,1024]{2,1,0:T(8,128)S(1)}, u32[]{:S(2)}, u32[]{:S(2)}) collective-permute-start(f32[9,16,1024]{2,1,0:T(8,128)S(1)} %get-tuple-element.23.rim_ref), channel_id=1, source_target_pairs={{0,256},{1,257},{2,258},{3,259},{4,260},{5,261},{6,262},{7,263},{8... | collective-permute-start | bytes 1769480 | tf_op jit(solution)/shard_map/ppermute | solution.py:271
  32.7 1.9 %collective-permute-start.1 = (f32[3,32,1024]{2,1,0:T(8,128)S(1)}, f32[3,32,1024]{2,1,0:T(8,128)S(1)}, u32[]{:S(2)}, u32[]{:S(2)}) collective-permute-start(f32[3,32,1024]{2,1,0:T(8,128)S(1)} %get-tuple-element.24), channel_id=1, source_target_pairs={{0,32},{32,64},{64,96},{96,0},{128,160},{160,192},{192,224},{224,1... | collective-permute-start | bytes 1179656 | tf_op jit(solution)/shard_map/ppermute | solution.py:286
  34.6 3.6 %collective-permute-start.2 = (f32[3,32,1024]{2,1,0:T(8,128)S(1)}, f32[3,32,1024]{2,1,0:T(8,128)S(1)}, u32[]{:S(2)}, u32[]{:S(2)}) collective-permute-start(f32[3,32,1024]{2,1,0:T(8,128)S(1)} %get-tuple-element.25), channel_id=1, source_target_pairs={{0,96},{32,0},{64,32},{96,64},{128,224},{160,128},{192,160},{224,1... | collective-permute-start | bytes 1179656 | tf_op jit(solution)/shard_map/ppermute | solution.py:286
  38.3 3.5 %collective-permute-done.1.low_ref = f32[3,32,1024]{2,1,0:T(8,128)S(1)} collective-permute-done((f32[3,32,1024]{2,1,0:T(8,128)S(1)}, f32[3,32,1024]{2,1,0:T(8,128)S(1)}, u32[]{:S(2)}, u32[]{:S(2)}) %collective-permute-start.1) | collective-permute-done | bytes 393248 | tf_op jit(solution)/shard_map/ppermute | solution.py:286
  41.8 5.4 %collective-permute-done.2.top_ref = f32[3,32,1024]{2,1,0:T(8,128)S(1)} collective-permute-done((f32[3,32,1024]{2,1,0:T(8,128)S(1)}, f32[3,32,1024]{2,1,0:T(8,128)S(1)}, u32[]{:S(2)}, u32[]{:S(2)}) %collective-permute-start.2) | collective-permute-done | bytes 393248 | tf_op jit(solution)/shard_map/ppermute | solution.py:286
  47.2 0.0 copy-done.5
  47.2 0.0 copy-done.6
  47.2 2.0 %sums.1 = (f32[9,32,1024]{2,1,0:T(8,128)}, f32[32,1024]{1,0:T(8,128)S(1)}) custom-call(f32[32,20]{1,0:T(8,128)S(1)} %copy-done.4, f32[9,16,1024]{2,1,0:T(8,128)S(1)} %inner_rows.1.mid_ref, f32[9,16,1024]{2,1,0:T(8,128)S(1)} %get-tuple-element.23.rim_ref, f32[3,32,1024]{2,1,0:T(8,128)S(1)} %collective-permute-done.1.low_ref, ...), custom_call_target="tpu_custom_call" | custom-call | flops 1024 | bytes 1024 | tf_op jit(solution)/shard_map/sums/pallas_call | solution.py:324
  49.2 0.0 collective-permute-done.3.r_mid_ref
  49.2 0.0 collective-permute-done.4.r_rim_ref
  49.2 0.7 collective-permute-start.7
  49.9 1.2 half_way.1
  51.2 9.8 %all_to_all.15.parts_ref = f32[8,32,128]{2,1,0:T(8,128)S(1)} all-to-all(f32[8,32,128]{2,1,0:T(8,128)S(1)} %get-tuple-element.30), channel_id=1, replica_groups={{0,32,64,96,128,160,192,224},{256,288,320,352,384,416,448,480},{512,544..., dimensions={0} | all-to-all | bytes 262144 | tf_op jit(solution)/shard_map/all_to_all | solution.py:337
  61.0 62.0 %all_to_all.16.parts_ref = f32[4,32,128]{2,1,0:T(8,128)S(1)} all-to-all(f32[4,32,128]{2,1,0:T(8,128)S(1)} %total_to_all.2), channel_id=1, replica_groups={{0,256,512,768},{32,288,544,800},{64,320,576,832},{96,352,608,864},{128..., dimensions={0} | all-to-all | bytes 131072 | tf_op jit(solution)/shard_map/all_to_all | solution.py:337
  123.0 0.0 collective-permute-done.7.inner_ref
  123.0 0.0 copy-start.2
  123.0 1.0 copy-done.2
  124.0 0.7 collective-permute-start.8
  124.7 0.0 collective-permute-done.8.refs_0_
  124.7 1.3 collective-permute-start.9
  126.0 1.9 %collective-permute-start.5 = (f32[3,32,1024]{2,1,0:T(8,128)}, f32[3,32,1024]{2,1,0:T(8,128)S(1)}, u32[]{:S(2)}, u32[]{:S(2)}) collective-permute-start(f32[3,32,1024]{2,1,0:T(8,128)} %get-tuple-element.31), channel_id=1, source_target_pairs={{0,32},{32,64},{64,96},{96,0},{128,160},{160,192},{192,224},{224,1... | collective-permute-start | bytes 1179656 | tf_op jit(solution)/shard_map/ppermute | solution.py:286
  127.9 3.6 %collective-permute-start.6 = (f32[3,32,1024]{2,1,0:T(8,128)}, f32[3,32,1024]{2,1,0:T(8,128)S(1)}, u32[]{:S(2)}, u32[]{:S(2)}) collective-permute-start(f32[3,32,1024]{2,1,0:T(8,128)} %get-tuple-element.33), channel_id=1, source_target_pairs={{0,96},{32,0},{64,32},{96,64},{128,224},{160,128},{192,160},{224,1... | collective-permute-start | bytes 1179656 | tf_op jit(solution)/shard_map/ppermute | solution.py:286
  131.6 0.7 total_to_all.3
  132.2 4.5 %all-to-all-start.2 = ((f32[8,32,128]{2,1,0:T(8,128)}), f32[8,32,128]{2,1,0:T(8,128)S(1)}, u32[]{:S(2)}, u32[]{:S(2)}) async-start(f32[8,32,128]{2,1,0:T(8,128)} %total_to_all.3), calls=%async_computation.2 | async-start | bytes 262144 | tf_op jit(solution)/shard_map/all_to_all | solution.py:337
  136.7 2.5 %collective-permute-done.5.low_ref = f32[3,32,1024]{2,1,0:T(8,128)S(1)} collective-permute-done((f32[3,32,1024]{2,1,0:T(8,128)}, f32[3,32,1024]{2,1,0:T(8,128)S(1)}, u32[]{:S(2)}, u32[]{:S(2)}) %collective-permute-start.5) | collective-permute-done | bytes 393248 | tf_op jit(solution)/shard_map/ppermute | solution.py:286
  139.3 0.0 collective-permute-done.6.top_ref
  139.3 1.5 all-to-all-done.2.energy_ref
  140.8 11.9 %collective-permute-done.9.outer_ref = f32[9,32,1024]{2,1,0:T(8,128)} collective-permute-done((f32[9,32,1024]{2,1,0:T(8,128)}, f32[9,32,1024]{2,1,0:T(8,128)}, u32[]{:S(2)}, u32[]{:S(2)}) %collective-permute-start.9) | collective-permute-done | bytes 1179680 | tf_op jit(solution)/shard_map/ppermute | solution.py:271
  152.7 0.0 copy-start.3
  152.7 1.3 copy-done.3
  154.0 2.7 %finish.1 = f32[9,32,1024]{2,1,0:T(8,128)} custom-call(f32[32,20]{1,0:T(8,128)S(1)} %copy-done.4, f32[9,16,1024]{2,1,0:T(8,128)S(1)} %inner_rows.1.mid_ref, f32[9,16,1024]{2,1,0:T(8,128)S(1)} %get-tuple-element.23.rim_ref, f32[9,16,1024]{2,1,0:T(8,128)S(1)} %collective-permute-done.3.r_mid_ref, f32[9,16,1024]{2,1,0:T(8,128)S(1)} %collective-permute-done.4.r_rim_ref, ...), custom_call_target="tpu_custom_call" | custom-call | flops 1024 | bytes 1024 | tf_op jit(solution)/shard_map/finish/pallas_call | solution.py:352
  (2 shorter events, 0.0 us)
Async XLA Ops:
  0.0 3.2 %copy-start.4 = (f32[32,20]{1,0:T(8,128)S(1)}, f32[32,20]{1,0:T(8,128)}, u32[]{:S(2)}) copy-start(f32[32,20]{1,0:T(8,128)} %constant.2.clone.table_ref) | copy-start | bytes 7684
  0.0 3.2 %copy-start = (f32[9,32,1024]{2,1,0:T(8,128)S(1)}, f32[9,32,1024]{2,1,0:T(8,128)}, u32[]{:S(2)}) copy-start(f32[9,32,1024]{2,1,0:T(8,128)} %field_ref.3) | copy-start | bytes 3538948
  0.0 3.2 %copy-start.1 = (s32[32,1024]{1,0:T(8,128)S(1)}, s32[32,1024]{1,0:T(8,128)}, u32[]{:S(2)}) copy-start(s32[32,1024]{1,0:T(8,128)} %mask_ref.3) | copy-start | bytes 393220
  1.9 16.1 %collective-permute-start = (f32[40,1024]{1,0:T(8,128)}, f32[40,1024]{1,0:T(8,128)S(1)}, u32[]{:S(2)}, u32[]{:S(2)}) collective-permute-start(f32[40,1024]{1,0:T(8,128)} %edge_rows.1), channel_id=1, source_target_pairs={{0,1},{1,2},{2,3},{3,4},{4,5},{5,6},{6,7},{7,8},{8,9},{9,10},{10,1... | collective-permute-start | bytes 491528 | tf_op jit(solution)/shard_map/ppermute | solution.py:307
  6.9 40.4 %copy-start.5 = (s32[32,1024]{1,0:T(8,128)S(1)}, s32[32,1024]{1,0:T(8,128)}, u32[]{:S(2)}) copy-start(s32[32,1024]{1,0:T(8,128)} %ice_ref.1) | copy-start | bytes 393220
  6.9 40.4 %copy-start.6 = (f32[32,1024]{1,0:T(8,128)S(1)}, f32[32,1024]{1,0:T(8,128)}, u32[]{:S(2)}) copy-start(f32[32,1024]{1,0:T(8,128)} %thick_ref.1) | copy-start | bytes 393220
  6.9 42.3 %collective-permute-start.3 = (f32[9,16,1024]{2,1,0:T(8,128)S(1)}, f32[9,16,1024]{2,1,0:T(8,128)S(1)}, u32[]{:S(2)}, u32[]{:S(2)}) collective-permute-start(f32[9,16,1024]{2,1,0:T(8,128)S(1)} %inner_rows.1.mid_ref), channel_id=1, source_target_pairs={{0,256},{1,257},{2,258},{3,259},{4,260},{5,261},{6,262},{7,263},{8... | collective-permute-start | bytes 1769480 | tf_op jit(solution)/shard_map/ppermute | solution.py:271
  21.8 27.4 %collective-permute-start.4 = (f32[9,16,1024]{2,1,0:T(8,128)S(1)}, f32[9,16,1024]{2,1,0:T(8,128)S(1)}, u32[]{:S(2)}, u32[]{:S(2)}) collective-permute-start(f32[9,16,1024]{2,1,0:T(8,128)S(1)} %get-tuple-element.23.rim_ref), channel_id=1, source_target_pairs={{0,256},{1,257},{2,258},{3,259},{4,260},{5,261},{6,262},{7,263},{8... | collective-permute-start | bytes 1769480 | tf_op jit(solution)/shard_map/ppermute | solution.py:271
  32.7 9.1 %collective-permute-start.1 = (f32[3,32,1024]{2,1,0:T(8,128)S(1)}, f32[3,32,1024]{2,1,0:T(8,128)S(1)}, u32[]{:S(2)}, u32[]{:S(2)}) collective-permute-start(f32[3,32,1024]{2,1,0:T(8,128)S(1)} %get-tuple-element.24), channel_id=1, source_target_pairs={{0,32},{32,64},{64,96},{96,0},{128,160},{160,192},{192,224},{224,1... | collective-permute-start | bytes 1179656 | tf_op jit(solution)/shard_map/ppermute | solution.py:286
  34.6 12.6 %collective-permute-start.2 = (f32[3,32,1024]{2,1,0:T(8,128)S(1)}, f32[3,32,1024]{2,1,0:T(8,128)S(1)}, u32[]{:S(2)}, u32[]{:S(2)}) collective-permute-start(f32[3,32,1024]{2,1,0:T(8,128)S(1)} %get-tuple-element.25), channel_id=1, source_target_pairs={{0,96},{32,0},{64,32},{96,64},{128,224},{160,128},{192,160},{224,1... | collective-permute-start | bytes 1179656 | tf_op jit(solution)/shard_map/ppermute | solution.py:286
  49.2 73.8 %collective-permute-start.7 = (f32[9,32,1024]{2,1,0:T(8,128)}, f32[9,32,1024]{2,1,0:T(8,128)S(1)}, u32[]{:S(2)}, u32[]{:S(2)}) collective-permute-start(f32[9,32,1024]{2,1,0:T(8,128)} %get-tuple-element.37), channel_id=1, source_target_pairs={{16,272},{17,273},{18,274},{19,275},{20,276},{21,277},{22,278},{23... | collective-permute-start | bytes 3538952 | tf_op jit(solution)/shard_map/ppermute | solution.py:271
  123.0 1.0 copy-start.2
  124.0 0.7 collective-permute-start.8
  124.7 28.0 %collective-permute-start.9 = (f32[9,32,1024]{2,1,0:T(8,128)}, f32[9,32,1024]{2,1,0:T(8,128)}, u32[]{:S(2)}, u32[]{:S(2)}) collective-permute-start(f32[9,32,1024]{2,1,0:T(8,128)} %get-tuple-element.37), channel_id=1, source_target_pairs={{24,280},{25,281},{26,282},{27,283},{28,284},{29,285},{30,286},{31... | collective-permute-start | bytes 3538952 | tf_op jit(solution)/shard_map/ppermute | solution.py:271
  126.0 13.3 %collective-permute-start.5 = (f32[3,32,1024]{2,1,0:T(8,128)}, f32[3,32,1024]{2,1,0:T(8,128)S(1)}, u32[]{:S(2)}, u32[]{:S(2)}) collective-permute-start(f32[3,32,1024]{2,1,0:T(8,128)} %get-tuple-element.31), channel_id=1, source_target_pairs={{0,32},{32,64},{64,96},{96,0},{128,160},{160,192},{192,224},{224,1... | collective-permute-start | bytes 1179656 | tf_op jit(solution)/shard_map/ppermute | solution.py:286
  127.9 11.3 %collective-permute-start.6 = (f32[3,32,1024]{2,1,0:T(8,128)}, f32[3,32,1024]{2,1,0:T(8,128)S(1)}, u32[]{:S(2)}, u32[]{:S(2)}) collective-permute-start(f32[3,32,1024]{2,1,0:T(8,128)} %get-tuple-element.33), channel_id=1, source_target_pairs={{0,96},{32,0},{64,32},{96,64},{128,224},{160,128},{192,160},{224,1... | collective-permute-start | bytes 1179656 | tf_op jit(solution)/shard_map/ppermute | solution.py:286
  132.2 8.6 %all-to-all-start.2 = ((f32[8,32,128]{2,1,0:T(8,128)}), f32[8,32,128]{2,1,0:T(8,128)S(1)}, u32[]{:S(2)}, u32[]{:S(2)}) async-start(f32[8,32,128]{2,1,0:T(8,128)} %total_to_all.3), calls=%async_computation.2 | async-start | bytes 262144 | tf_op jit(solution)/shard_map/all_to_all | solution.py:337
  152.7 1.3 copy-start.3

commit v5 on v4

--- a/solution.py
+++ b/solution.py
@@ -105,7 +105,7 @@
             mid_ref[i] = f[8 - low : 24 - low]
             return carry
 
-        lax.fori_loop(0, NQ, component, 0)
+        lax.fori_loop(0, NQ, component, 0, unroll=3)
 
     by_quarter(run)
 
@@ -142,7 +142,7 @@
             pl.when(i >= NQ - EDGE)(lambda: edge(hi_ref, i - (NQ - EDGE)))
             return carry
 
-        lax.fori_loop(0, NQ, component, 0)
+        lax.fori_loop(0, NQ, component, 0, unroll=3)
 
     by_quarter(run)
 
@@ -207,14 +207,12 @@
         out_ref[k] = total
 
 
-def finish(
-    table_ref, mid_ref, rim_ref, r_mid_ref, r_rim_ref, low_ref, top_ref, inner_ref, outer_ref, energy_ref, att_ref, out_ref
-):
+def prepare(table_ref, mid_ref, rim_ref, r_mid_ref, r_rim_ref, low_ref, top_ref, energy_ref, att_ref, base_ref, coef_ref):
     fsq = table_ref[lax.axis_index("comp"), 2 * NQ]
 
-    def write(climbed, s_ref):
+    def write(climbed):
         step = 1 if climbed else 3
-        for t in range(0, out_ref.shape[1], 8):
+        for t in range(0, base_ref.shape[1], 8):
             rows = pl.ds(t, 8)
             e_ref, e_rows = part_of(mid_ref, rim_ref, t)
             r_ref, _ = part_of(r_mid_ref, r_rim_ref, t)
@@ -223,10 +221,37 @@
             raw = lambda i: at(low_ref, r_ref, top_ref, i, e_rows, rows)
             for i in range(NQ):
                 e = e_ref[i, e_rows]
-                around = s_ref[i, rows] + (raw(i - step) + raw(i + step))
-                out_ref[i, rows] = (e + mixing_rate * e * (0.25 * around - e)) * factor
-
-    by_place(lambda k: write(k < 2, outer_ref if k in (0, 3) else inner_ref))
+                pair = raw(i - step) + raw(i + step)
+                base_ref[i, rows] = (e + mixing_rate * e * (0.25 * pair - e)) * factor
+                coef_ref[i, rows] = (0.25 * mixing_rate) * e * factor
+
+    by_direction(write)
+
+
+def finish(base_ref, coef_ref, inner_ref, outer_ref, out_ref, sums_ref, done_ref, in_sems, out_sems):
+    tiles = base_ref.shape[1] // 8
+
+    def fetch(ref, t):
+        rows = pl.ds(8 * t, 8)
+        return pltpu.make_async_copy(ref.at[:, rows], sums_ref.at[:, rows], in_sems.at[t])
+
+    def store(t):
+        rows = pl.ds(8 * t, 8)
+        return pltpu.make_async_copy(done_ref.at[:, rows], out_ref.at[:, rows], out_sems.at[t])
+
+    def start(k):
+        for t in range(tiles):
+            fetch(outer_ref if k in (0, 3) else inner_ref, t).start()
+
+    by_place(start)
+    for t in range(tiles):
+        rows = pl.ds(8 * t, 8)
+        fetch(inner_ref, t).wait()
+        for i in range(NQ):
+            done_ref[i, rows] = base_ref[i, rows] + coef_ref[i, rows] * sums_ref[i, rows]
+        store(t).start()
+    for t in range(tiles):
+        store(t).wait()
 
 
 def in_vmem(count):
@@ -349,10 +374,24 @@
     outer = move(out, False, (0, 3))
     energy = swap(spread(share, GROUP, told), near)
 
-    (updated,) = call(finish, [whole], True, 10)(
-        table, mid, rim, r_mid, r_rim, low, top, inner, outer, energy, att
+    base, coef = call(prepare, [whole, whole], True, 8)(
+        table, mid, rim, r_mid, r_rim, low, top, energy, att
     )
-    return updated
+    anywhere = pl.BlockSpec(memory_space=pl.ANY)
+    return pl.pallas_call(
+        finish,
+        out_shape=jax.ShapeDtypeStruct(whole, jnp.float32),
+        in_specs=in_vmem(2) + [anywhere, anywhere],
+        out_specs=anywhere,
+        scratch_shapes=[
+            pltpu.VMEM(whole, jnp.float32),
+            pltpu.VMEM(whole, jnp.float32),
+            pltpu.SemaphoreType.DMA((rows // 8,)),
+            pltpu.SemaphoreType.DMA((rows // 8,)),
+        ],
+        compiler_params=pltpu.CompilerParams(vmem_limit_bytes=VMEM_BYTES),
+        name="finish",
+    )(base, coef, inner, outer)
 
 
 def solution(mesh):

time: 157 us -> 154 us (0.981)
    pallas_call x1 -> x2, Pallas kernels: 2.66 us -> 3.26 us  [the longest x1 2.08 us: body(): pl.pallas_call(finish, out_shape=jax.ShapeDtypeStruct(whole, jnp.float32)...]
where the time goes in v5:
time: 154 us; the launch traced here: 153 us
  blocking collectives  71.8 us (47%)
  starting transfers between devices  41.6 us (27%)
  waiting for transfers between devices  23.6 us (15%)
  Pallas kernels  15 us (10%)
    all_to_all x2, blocking collectives, swap(): lax.all_to_all(value, 'comp', 0, 0, axis_index_groups=groups, tiled=True)  71.8 us
    ppermute x4, starting transfers between devices, move(): return lax.ppermute(value, ('comp', 'space'), pairs)  24 us
    ppermute x4, waiting for transfers between devices, turn(): return lax.ppermute(value, 'comp', pairs)  11.3 us
    ppermute x4, starting transfers between devices, turn(): return lax.ppermute(value, 'comp', pairs)  11.1 us
    ppermute x4, waiting for transfers between devices, move(): return lax.ppermute(value, ('comp', 'space'), pairs)  10.7 us
    all_to_all x1, starting transfers between devices, swap(): lax.all_to_all(value, 'comp', 0, 0, axis_index_groups=groups, tiled=True)  4.51 us
    pallas_call x1, Pallas kernels, body(): call(outer_rows, [part, edge, edge], True, 4, [land(32), land(32)])  3.76 us
  transfers between devices with their start and end apart: 11, of which 5 were waited for; matrix products, arithmetic and copies ran while one was open for 0% of the time, Pallas kernels for 7%

profile of v5, /device:TPU:6, one launch (start us, length us, event | category | flops | bytes accessed | tf_op | source)
XLA Modules:
  0.0 153.2 jit_solution(8922187882983923947)
XLA Ops:
  0.0 0.0 copy-start.4
  0.0 0.0 copy-start.1
  0.0 0.0 copy-start
  0.0 1.9 %edge_rows.1 = f32[40,1024]{1,0:T(8,128)} custom-call(f32[9,32,1024]{2,1,0:T(8,128)} %field_ref.3, f32[9,32,1024]{2,1,0:T(8,128)} %field_ref.3, s32[32,1024]{1,0:T(8,128)} %mask_ref.3, s32[32,1024]{1,0:T(8,128)} %mask_ref.3), custom_call_target="tpu_custom_call" | custom-call | tf_op jit(solution)/shard_map/edge_rows/pallas_call | solution.py:313
  1.9 1.3 collective-permute-start
  3.2 0.0 copy-done.4
  3.2 0.0 copy-done.1
  3.2 0.0 copy-done
  3.2 2.2 %inner_rows.1.mid_ref = f32[9,16,1024]{2,1,0:T(8,128)S(1)} custom-call(f32[32,20]{1,0:T(8,128)S(1)} %copy-done.4, f32[9,32,1024]{2,1,0:T(8,128)S(1)} %copy-done, s32[32,1024]{1,0:T(8,128)S(1)} %copy-done.1), custom_call_target="tpu_custom_call" | custom-call | flops 1024 | bytes 1024 | tf_op jit(solution)/shard_map/inner_rows/pallas_call | solution.py:341
  5.4 0.0 copy-start.5
  5.4 0.0 copy-start.6
  5.4 11.1 %collective-permute-start.3 = (f32[9,16,1024]{2,1,0:T(8,128)S(1)}, f32[9,16,1024]{2,1,0:T(8,128)S(1)}, u32[]{:S(2)}, u32[]{:S(2)}) collective-permute-start(f32[9,16,1024]{2,1,0:T(8,128)S(1)} %inner_rows.1.mid_ref), channel_id=1, source_target_pairs={{0,256},{1,257},{2,258},{3,259},{4,260},{5,261},{6,262},{7,263},{8... | collective-permute-start | bytes 1769480 | tf_op jit(solution)/shard_map/ppermute | solution.py:296
  16.5 0.0 collective-permute-done.halo_ref
  16.5 3.8 %outer_rows.1 = (f32[9,16,1024]{2,1,0:T(8,128)S(1)}, f32[3,32,1024]{2,1,0:T(8,128)S(1)}, f32[3,32,1024]{2,1,0:T(8,128)S(1)}) custom-call(f32[32,20]{1,0:T(8,128)S(1)} %copy-done.4, f32[9,32,1024]{2,1,0:T(8,128)S(1)} %copy-done, s32[32,1024]{1,0:T(8,128)S(1)} %copy-done.1, f32[40,1024]{1,0:T(8,128)S(1)} %collective-permute-done.halo_ref, ...), custom_call_target="tpu_custom_call" | custom-call | flops 1024 | bytes 1024 | tf_op jit(solution)/shard_map/outer_rows/pallas_call | solution.py:343
  20.3 10.9 %collective-permute-start.4 = (f32[9,16,1024]{2,1,0:T(8,128)S(1)}, f32[9,16,1024]{2,1,0:T(8,128)S(1)}, u32[]{:S(2)}, u32[]{:S(2)}) collective-permute-start(f32[9,16,1024]{2,1,0:T(8,128)S(1)} %get-tuple-element.25.rim_ref), channel_id=1, source_target_pairs={{0,256},{1,257},{2,258},{3,259},{4,260},{5,261},{6,262},{7,263},{8... | collective-permute-start | bytes 1769480 | tf_op jit(solution)/shard_map/ppermute | solution.py:296
  31.2 1.9 %collective-permute-start.1 = (f32[3,32,1024]{2,1,0:T(8,128)S(1)}, f32[3,32,1024]{2,1,0:T(8,128)S(1)}, u32[]{:S(2)}, u32[]{:S(2)}) collective-permute-start(f32[3,32,1024]{2,1,0:T(8,128)S(1)} %get-tuple-element.26), channel_id=1, source_target_pairs={{0,32},{32,64},{64,96},{96,0},{128,160},{160,192},{192,224},{224,1... | collective-permute-start | bytes 1179656 | tf_op jit(solution)/shard_map/ppermute | solution.py:311
  33.1 3.6 %collective-permute-start.2 = (f32[3,32,1024]{2,1,0:T(8,128)S(1)}, f32[3,32,1024]{2,1,0:T(8,128)S(1)}, u32[]{:S(2)}, u32[]{:S(2)}) collective-permute-start(f32[3,32,1024]{2,1,0:T(8,128)S(1)} %get-tuple-element.27), channel_id=1, source_target_pairs={{0,96},{32,0},{64,32},{96,64},{128,224},{160,128},{192,160},{224,1... | collective-permute-start | bytes 1179656 | tf_op jit(solution)/shard_map/ppermute | solution.py:311
  36.8 3.5 %collective-permute-done.1.low_ref = f32[3,32,1024]{2,1,0:T(8,128)S(1)} collective-permute-done((f32[3,32,1024]{2,1,0:T(8,128)S(1)}, f32[3,32,1024]{2,1,0:T(8,128)S(1)}, u32[]{:S(2)}, u32[]{:S(2)}) %collective-permute-start.1) | collective-permute-done | bytes 393248 | tf_op jit(solution)/shard_map/ppermute | solution.py:311
  40.3 5.3 %collective-permute-done.2.top_ref = f32[3,32,1024]{2,1,0:T(8,128)S(1)} collective-permute-done((f32[3,32,1024]{2,1,0:T(8,128)S(1)}, f32[3,32,1024]{2,1,0:T(8,128)S(1)}, u32[]{:S(2)}, u32[]{:S(2)}) %collective-permute-start.2) | collective-permute-done | bytes 393248 | tf_op jit(solution)/shard_map/ppermute | solution.py:311
  45.6 0.0 copy-done.5
  45.6 0.0 copy-done.6
  45.6 2.0 %sums.1 = (f32[9,32,1024]{2,1,0:T(8,128)}, f32[32,1024]{1,0:T(8,128)S(1)}) custom-call(f32[32,20]{1,0:T(8,128)S(1)} %copy-done.4, f32[9,16,1024]{2,1,0:T(8,128)S(1)} %inner_rows.1.mid_ref, f32[9,16,1024]{2,1,0:T(8,128)S(1)} %get-tuple-element.25.rim_ref, f32[3,32,1024]{2,1,0:T(8,128)S(1)} %collective-permute-done.1.low_ref, ...), custom_call_target="tpu_custom_call" | custom-call | flops 1024 | bytes 1024 | tf_op jit(solution)/shard_map/sums/pallas_call | solution.py:349
  47.6 0.0 collective-permute-done.3.r_mid_ref
  47.6 0.0 collective-permute-done.4.r_rim_ref
  47.6 0.7 collective-permute-start.7
  48.3 1.3 half_way.1
  49.6 9.7 %all_to_all.15.parts_ref = f32[8,32,128]{2,1,0:T(8,128)S(1)} all-to-all(f32[8,32,128]{2,1,0:T(8,128)S(1)} %get-tuple-element.32), channel_id=1, replica_groups={{0,32,64,96,128,160,192,224},{256,288,320,352,384,416,448,480},{512,544..., dimensions={0} | all-to-all | bytes 262144 | tf_op jit(solution)/shard_map/all_to_all | solution.py:362
  59.3 62.1 %all_to_all.16.parts_ref = f32[4,32,128]{2,1,0:T(8,128)S(1)} all-to-all(f32[4,32,128]{2,1,0:T(8,128)S(1)} %total_to_all.2), channel_id=1, replica_groups={{0,256,512,768},{32,288,544,800},{64,320,576,832},{96,352,608,864},{128..., dimensions={0} | all-to-all | bytes 131072 | tf_op jit(solution)/shard_map/all_to_all | solution.py:362
  121.4 0.0 collective-permute-done.7.inner_ref
  121.4 0.0 copy-start.2
  121.4 1.0 copy-done.2
  122.4 0.7 collective-permute-start.8
  123.1 0.0 collective-permute-done.8.refs_0_
  123.1 1.3 collective-permute-start.9
  124.4 1.9 %collective-permute-start.5 = (f32[3,32,1024]{2,1,0:T(8,128)}, f32[3,32,1024]{2,1,0:T(8,128)S(1)}, u32[]{:S(2)}, u32[]{:S(2)}) collective-permute-start(f32[3,32,1024]{2,1,0:T(8,128)} %get-tuple-element.33), channel_id=1, source_target_pairs={{0,32},{32,64},{64,96},{96,0},{128,160},{160,192},{192,224},{224,1... | collective-permute-start | bytes 1179656 | tf_op jit(solution)/shard_map/ppermute | solution.py:311
  126.3 3.6 %collective-permute-start.6 = (f32[3,32,1024]{2,1,0:T(8,128)}, f32[3,32,1024]{2,1,0:T(8,128)S(1)}, u32[]{:S(2)}, u32[]{:S(2)}) collective-permute-start(f32[3,32,1024]{2,1,0:T(8,128)} %get-tuple-element.35), channel_id=1, source_target_pairs={{0,96},{32,0},{64,32},{96,64},{128,224},{160,128},{192,160},{224,1... | collective-permute-start | bytes 1179656 | tf_op jit(solution)/shard_map/ppermute | solution.py:311
  130.0 0.7 total_to_all.3
  130.7 4.5 %all-to-all-start.2 = ((f32[8,32,128]{2,1,0:T(8,128)}), f32[8,32,128]{2,1,0:T(8,128)S(1)}, u32[]{:S(2)}, u32[]{:S(2)}) async-start(f32[8,32,128]{2,1,0:T(8,128)} %total_to_all.3), calls=%async_computation.2 | async-start | bytes 262144 | tf_op jit(solution)/shard_map/all_to_all | solution.py:362
  135.2 2.5 %collective-permute-done.5.low_ref = f32[3,32,1024]{2,1,0:T(8,128)S(1)} collective-permute-done((f32[3,32,1024]{2,1,0:T(8,128)}, f32[3,32,1024]{2,1,0:T(8,128)S(1)}, u32[]{:S(2)}, u32[]{:S(2)}) %collective-permute-start.5) | collective-permute-done | bytes 393248 | tf_op jit(solution)/shard_map/ppermute | solution.py:311
  137.7 0.0 collective-permute-done.6.top_ref
  137.7 1.6 %all-to-all-done.2.energy_ref = f32[8,32,128]{2,1,0:T(8,128)S(1)} async-done(((f32[8,32,128]{2,1,0:T(8,128)}), f32[8,32,128]{2,1,0:T(8,128)S(1)}, u32[]{:S(2)}, u32[]{:S(2)}) %all-to-all-start.2) | async-done | bytes 131104 | tf_op jit(solution)/shard_map/all_to_all | solution.py:362
  139.2 0.0 copy-start.3
  139.2 1.2 prepare.1
  140.4 10.7 %collective-permute-done.9.outer_ref = f32[9,32,1024]{2,1,0:T(8,128)} collective-permute-done((f32[9,32,1024]{2,1,0:T(8,128)}, f32[9,32,1024]{2,1,0:T(8,128)}, u32[]{:S(2)}, u32[]{:S(2)}) %collective-permute-start.9) | collective-permute-done | bytes 1179680 | tf_op jit(solution)/shard_map/ppermute | solution.py:296
  151.1 0.0 copy-done.3
  151.1 2.1 %finish.1 = f32[9,32,1024]{2,1,0:T(8,128)} custom-call(f32[9,32,1024]{2,1,0:T(8,128)S(1)} %get-tuple-element.41.base_ref, f32[9,32,1024]{2,1,0:T(8,128)S(1)} %get-tuple-element.42.coef_ref, f32[9,32,1024]{2,1,0:T(8,128)S(1)} %copy-done.3, f32[9,32,1024]{2,1,0:T(8,128)} %collective-permute-done.9.outer_ref), custom_call_target="tpu_custom_call" | custom-call | tf_op jit(solution)/shard_map/finish/pallas_call | solution.py:381
  (2 shorter events, 0.0 us)
Async XLA Ops:
  0.0 3.2 %copy-start.4 = (f32[32,20]{1,0:T(8,128)S(1)}, f32[32,20]{1,0:T(8,128)}, u32[]{:S(2)}) copy-start(f32[32,20]{1,0:T(8,128)} %constant.2.clone.table_ref) | copy-start | bytes 7684
  0.0 3.2 %copy-start.1 = (s32[32,1024]{1,0:T(8,128)S(1)}, s32[32,1024]{1,0:T(8,128)}, u32[]{:S(2)}) copy-start(s32[32,1024]{1,0:T(8,128)} %mask_ref.3) | copy-start | bytes 393220
  0.0 3.2 %copy-start = (f32[9,32,1024]{2,1,0:T(8,128)S(1)}, f32[9,32,1024]{2,1,0:T(8,128)}, u32[]{:S(2)}) copy-start(f32[9,32,1024]{2,1,0:T(8,128)} %field_ref.3) | copy-start | bytes 3538948
  1.9 14.6 %collective-permute-start = (f32[40,1024]{1,0:T(8,128)}, f32[40,1024]{1,0:T(8,128)S(1)}, u32[]{:S(2)}, u32[]{:S(2)}) collective-permute-start(f32[40,1024]{1,0:T(8,128)} %edge_rows.1), channel_id=1, source_target_pairs={{0,1},{1,2},{2,3},{3,4},{4,5},{5,6},{6,7},{7,8},{8,9},{9,10},{10,1... | collective-permute-start | bytes 491528 | tf_op jit(solution)/shard_map/ppermute | solution.py:332
  5.4 40.2 %copy-start.5 = (s32[32,1024]{1,0:T(8,128)S(1)}, s32[32,1024]{1,0:T(8,128)}, u32[]{:S(2)}) copy-start(s32[32,1024]{1,0:T(8,128)} %ice_ref.1) | copy-start | bytes 393220
  5.4 40.2 %copy-start.6 = (f32[32,1024]{1,0:T(8,128)S(1)}, f32[32,1024]{1,0:T(8,128)}, u32[]{:S(2)}) copy-start(f32[32,1024]{1,0:T(8,128)} %thick_ref.1) | copy-start | bytes 393220
  5.4 42.2 %collective-permute-start.3 = (f32[9,16,1024]{2,1,0:T(8,128)S(1)}, f32[9,16,1024]{2,1,0:T(8,128)S(1)}, u32[]{:S(2)}, u32[]{:S(2)}) collective-permute-start(f32[9,16,1024]{2,1,0:T(8,128)S(1)} %inner_rows.1.mid_ref), channel_id=1, source_target_pairs={{0,256},{1,257},{2,258},{3,259},{4,260},{5,261},{6,262},{7,263},{8... | collective-permute-start | bytes 1769480 | tf_op jit(solution)/shard_map/ppermute | solution.py:296
  20.3 27.3 %collective-permute-start.4 = (f32[9,16,1024]{2,1,0:T(8,128)S(1)}, f32[9,16,1024]{2,1,0:T(8,128)S(1)}, u32[]{:S(2)}, u32[]{:S(2)}) collective-permute-start(f32[9,16,1024]{2,1,0:T(8,128)S(1)} %get-tuple-element.25.rim_ref), channel_id=1, source_target_pairs={{0,256},{1,257},{2,258},{3,259},{4,260},{5,261},{6,262},{7,263},{8... | collective-permute-start | bytes 1769480 | tf_op jit(solution)/shard_map/ppermute | solution.py:296
  31.2 9.1 %collective-permute-start.1 = (f32[3,32,1024]{2,1,0:T(8,128)S(1)}, f32[3,32,1024]{2,1,0:T(8,128)S(1)}, u32[]{:S(2)}, u32[]{:S(2)}) collective-permute-start(f32[3,32,1024]{2,1,0:T(8,128)S(1)} %get-tuple-element.26), channel_id=1, source_target_pairs={{0,32},{32,64},{64,96},{96,0},{128,160},{160,192},{192,224},{224,1... | collective-permute-start | bytes 1179656 | tf_op jit(solution)/shard_map/ppermute | solution.py:311
  33.1 12.5 %collective-permute-start.2 = (f32[3,32,1024]{2,1,0:T(8,128)S(1)}, f32[3,32,1024]{2,1,0:T(8,128)S(1)}, u32[]{:S(2)}, u32[]{:S(2)}) collective-permute-start(f32[3,32,1024]{2,1,0:T(8,128)S(1)} %get-tuple-element.27), channel_id=1, source_target_pairs={{0,96},{32,0},{64,32},{96,64},{128,224},{160,128},{192,160},{224,1... | collective-permute-start | bytes 1179656 | tf_op jit(solution)/shard_map/ppermute | solution.py:311
  47.6 73.8 %collective-permute-start.7 = (f32[9,32,1024]{2,1,0:T(8,128)}, f32[9,32,1024]{2,1,0:T(8,128)S(1)}, u32[]{:S(2)}, u32[]{:S(2)}) collective-permute-start(f32[9,32,1024]{2,1,0:T(8,128)} %get-tuple-element.44), channel_id=1, source_target_pairs={{16,272},{17,273},{18,274},{19,275},{20,276},{21,277},{22,278},{23... | collective-permute-start | bytes 3538952 | tf_op jit(solution)/shard_map/ppermute | solution.py:296
  121.4 1.0 copy-start.2
  122.4 0.7 collective-permute-start.8
  123.1 28.0 %collective-permute-start.9 = (f32[9,32,1024]{2,1,0:T(8,128)}, f32[9,32,1024]{2,1,0:T(8,128)}, u32[]{:S(2)}, u32[]{:S(2)}) collective-permute-start(f32[9,32,1024]{2,1,0:T(8,128)} %get-tuple-element.44), channel_id=1, source_target_pairs={{24,280},{25,281},{26,282},{27,283},{28,284},{29,285},{30,286},{31... | collective-permute-start | bytes 3538952 | tf_op jit(solution)/shard_map/ppermute | solution.py:296
  124.4 13.2 %collective-permute-start.5 = (f32[3,32,1024]{2,1,0:T(8,128)}, f32[3,32,1024]{2,1,0:T(8,128)S(1)}, u32[]{:S(2)}, u32[]{:S(2)}) collective-permute-start(f32[3,32,1024]{2,1,0:T(8,128)} %get-tuple-element.33), channel_id=1, source_target_pairs={{0,32},{32,64},{64,96},{96,0},{128,160},{160,192},{192,224},{224,1... | collective-permute-start | bytes 1179656 | tf_op jit(solution)/shard_map/ppermute | solution.py:311
  126.3 11.3 %collective-permute-start.6 = (f32[3,32,1024]{2,1,0:T(8,128)}, f32[3,32,1024]{2,1,0:T(8,128)S(1)}, u32[]{:S(2)}, u32[]{:S(2)}) collective-permute-start(f32[3,32,1024]{2,1,0:T(8,128)} %get-tuple-element.35), channel_id=1, source_target_pairs={{0,96},{32,0},{64,32},{96,64},{128,224},{160,128},{192,160},{224,1... | collective-permute-start | bytes 1179656 | tf_op jit(solution)/shard_map/ppermute | solution.py:311
  130.7 8.6 %all-to-all-start.2 = ((f32[8,32,128]{2,1,0:T(8,128)}), f32[8,32,128]{2,1,0:T(8,128)S(1)}, u32[]{:S(2)}, u32[]{:S(2)}) async-start(f32[8,32,128]{2,1,0:T(8,128)} %total_to_all.3), calls=%async_computation.2 | async-start | bytes 262144 | tf_op jit(solution)/shard_map/all_to_all | solution.py:362
  139.2 11.9 %copy-start.3 = (f32[9,32,1024]{2,1,0:T(8,128)S(1)}, f32[9,32,1024]{2,1,0:T(8,128)}, u32[]{:S(2)}) copy-start(f32[9,32,1024]{2,1,0:T(8,128)} %copy-done.2) | copy-start | bytes 3538948

commit v6 on v5

--- a/solution.py
+++ b/solution.py
@@ -228,7 +228,7 @@
     by_direction(write)
 
 
-def finish(base_ref, coef_ref, inner_ref, outer_ref, out_ref, sums_ref, done_ref, in_sems, out_sems):
+def finish(base_ref, coef_ref, first_ref, inner_ref, last_ref, out_ref, sums_ref, done_ref, in_sems, out_sems):
     tiles = base_ref.shape[1] // 8
 
     def fetch(ref, t):
@@ -241,7 +241,7 @@
 
     def start(k):
         for t in range(tiles):
-            fetch(outer_ref if k in (0, 3) else inner_ref, t).start()
+            fetch((first_ref, inner_ref, inner_ref, last_ref)[k], t).start()
 
     by_place(start)
     for t in range(tiles):
@@ -351,6 +351,7 @@
     )
     out, r_mid, r_rim = lax.optimization_barrier((out, r_mid, r_rim))
     inner = move(out, False, (1, 2))
+    first = move(out, False, (0,))
 
     share, to_prev, to_next = call(half_way, [(GROUP, rows, cols // GROUP), edge, edge], False, 6)(
         mid, rim, low, top, r_mid, r_rim
@@ -368,10 +369,10 @@
     top = turn(after(to_prev, share), -1)
     low = turn(after(to_next, share), 1)
     share = swap(spread(share, n_comp // GROUP), far)
-    share, inner = lax.optimization_barrier((share, inner))
-    told = tell(share[0])
+    share, word = lax.optimization_barrier((share, inner[0, :8, :128]))
+    told = tell(word)
     out, share, told = lax.optimization_barrier((out, share, told))
-    outer = move(out, False, (0, 3))
+    last = move(out, False, (3,))
     energy = swap(spread(share, GROUP, told), near)
 
     base, coef = call(prepare, [whole, whole], True, 8)(
@@ -381,7 +382,7 @@
     return pl.pallas_call(
         finish,
         out_shape=jax.ShapeDtypeStruct(whole, jnp.float32),
-        in_specs=in_vmem(2) + [anywhere, anywhere],
+        in_specs=in_vmem(2) + [anywhere] * 3,
         out_specs=anywhere,
         scratch_shapes=[
             pltpu.VMEM(whole, jnp.float32),
@@ -391,7 +392,7 @@
         ],
         compiler_params=pltpu.CompilerParams(vmem_limit_bytes=VMEM_BYTES),
         name="finish",
-    )(base, coef, inner, outer)
+    )(base, coef, first, inner, last)
 
 
 def solution(mesh):

time: 154 us -> 152 us (0.987)
  blocking collectives: 71.8 us -> 9.73 us
  starting transfers between devices: 41.6 us -> 80 us
  waiting for transfers between devices: 23.6 us -> 46.2 us
    all_to_all x2 -> x1, blocking collectives: 71.8 us -> 9.73 us  [swap(): lax.all_to_all(value, 'comp', 0, 0, axis_index_groups=groups, tiled=True)]
    all_to_all x1 -> x2, starting transfers between devices: 4.51 us -> 41.5 us  [swap(): lax.all_to_all(value, 'comp', 0, 0, axis_index_groups=groups, tiled=True)]
    all_to_all x1 -> x2, waiting for transfers between devices: 1.57 us -> 27 us  [swap(): lax.all_to_all(value, 'comp', 0, 0, axis_index_groups=groups, tiled=True)]
    ppermute x4 -> x5, starting transfers between devices: 24 us -> 26.7 us  [move(): return lax.ppermute(value, ('comp', 'space'), pairs)]
    ppermute x4 -> x5, waiting for transfers between devices: 10.7 us -> 9.29 us  [move(): return lax.ppermute(value, ('comp', 'space'), pairs)]
  transfers between devices with their start and end apart: 11 -> 13, of which waited for: 5 -> 6; matrix products, arithmetic and copies ran while one was open for 0% -> 0% of each run, Pallas kernels for 7% -> 7%
where the time goes in v6:
time: 152 us
  starting transfers between devices  80 us (53%)
  waiting for transfers between devices  46.2 us (30%)
  Pallas kernels  14.7 us (10%)
  blocking collectives  9.73 us (6%)
    all_to_all x2, starting transfers between devices, swap(): lax.all_to_all(value, 'comp', 0, 0, axis_index_groups=groups, tiled=True)  41.5 us
    all_to_all x2, waiting for transfers between devices, swap(): lax.all_to_all(value, 'comp', 0, 0, axis_index_groups=groups, tiled=True)  27 us
    ppermute x5, starting transfers between devices, move(): return lax.ppermute(value, ('comp', 'space'), pairs)  26.7 us
    ppermute x4, starting transfers between devices, turn(): return lax.ppermute(value, 'comp', pairs)  9.88 us
    ppermute x4, waiting for transfers between devices, turn(): return lax.ppermute(value, 'comp', pairs)  9.86 us
    all_to_all x1, blocking collectives, swap(): lax.all_to_all(value, 'comp', 0, 0, axis_index_groups=groups, tiled=True)  9.73 us
    ppermute x5, waiting for transfers between devices, move(): return lax.ppermute(value, ('comp', 'space'), pairs)  9.29 us
    pallas_call x1, Pallas kernels, body(): call(outer_rows, [part, edge, edge], True, 4, [land(32), land(32)])  3.76 us
  transfers between devices with their start and end apart: 13, of which 6 were waited for; matrix products, arithmetic and copies ran while one was open for 0% of the time, Pallas kernels for 7%

profile of v6, /device:TPU:6, one launch (start us, length us, event | category | flops | bytes accessed | tf_op | source)
XLA Modules:
  0.0 151.6 jit_solution(844291230452336195)
XLA Ops:
  0.0 1.9 %edge_rows.1 = f32[40,1024]{1,0:T(8,128)} custom-call(f32[9,32,1024]{2,1,0:T(8,128)} %field_ref.3, f32[9,32,1024]{2,1,0:T(8,128)} %field_ref.3, s32[32,1024]{1,0:T(8,128)} %mask_ref.3, s32[32,1024]{1,0:T(8,128)} %mask_ref.3), custom_call_target="tpu_custom_call" | custom-call | tf_op jit(solution)/shard_map/edge_rows/pallas_call | solution.py:313
  1.9 1.3 collective-permute-start
  3.2 0.0 copy-done.2
  3.2 0.0 copy-done
  3.2 0.0 copy-done.1
  3.2 2.2 %inner_rows.1.mid_ref = f32[9,16,1024]{2,1,0:T(8,128)S(1)} custom-call(f32[32,20]{1,0:T(8,128)S(1)} %copy-done.2, f32[9,32,1024]{2,1,0:T(8,128)S(1)} %copy-done, s32[32,1024]{1,0:T(8,128)S(1)} %copy-done.1), custom_call_target="tpu_custom_call" | custom-call | flops 1024 | bytes 1024 | tf_op jit(solution)/shard_map/inner_rows/pallas_call | solution.py:341
  5.4 0.0 copy-start.3
  5.4 0.0 copy-start.4
  5.4 11.1 %collective-permute-start.3 = (f32[9,16,1024]{2,1,0:T(8,128)S(1)}, f32[9,16,1024]{2,1,0:T(8,128)S(1)}, u32[]{:S(2)}, u32[]{:S(2)}) collective-permute-start(f32[9,16,1024]{2,1,0:T(8,128)S(1)} %inner_rows.1.mid_ref), channel_id=1, source_target_pairs={{0,256},{1,257},{2,258},{3,259},{4,260},{5,261},{6,262},{7,263},{8... | collective-permute-start | bytes 1769480 | tf_op jit(solution)/shard_map/ppermute | solution.py:296
  16.5 0.0 collective-permute-done.halo_ref
  16.5 3.8 %outer_rows.1 = (f32[9,16,1024]{2,1,0:T(8,128)S(1)}, f32[3,32,1024]{2,1,0:T(8,128)S(1)}, f32[3,32,1024]{2,1,0:T(8,128)S(1)}) custom-call(f32[32,20]{1,0:T(8,128)S(1)} %copy-done.2, f32[9,32,1024]{2,1,0:T(8,128)S(1)} %copy-done, s32[32,1024]{1,0:T(8,128)S(1)} %copy-done.1, f32[40,1024]{1,0:T(8,128)S(1)} %collective-permute-done.halo_ref, ...), custom_call_target="tpu_custom_call" | custom-call | flops 1024 | bytes 1024 | tf_op jit(solution)/shard_map/outer_rows/pallas_call | solution.py:343
  20.3 10.9 %collective-permute-start.4 = (f32[9,16,1024]{2,1,0:T(8,128)S(1)}, f32[9,16,1024]{2,1,0:T(8,128)S(1)}, u32[]{:S(2)}, u32[]{:S(2)}) collective-permute-start(f32[9,16,1024]{2,1,0:T(8,128)S(1)} %get-tuple-element.25.rim_ref), channel_id=1, source_target_pairs={{0,256},{1,257},{2,258},{3,259},{4,260},{5,261},{6,262},{7,263},{8... | collective-permute-start | bytes 1769480 | tf_op jit(solution)/shard_map/ppermute | solution.py:296
  31.2 1.9 %collective-permute-start.1 = (f32[3,32,1024]{2,1,0:T(8,128)S(1)}, f32[3,32,1024]{2,1,0:T(8,128)S(1)}, u32[]{:S(2)}, u32[]{:S(2)}) collective-permute-start(f32[3,32,1024]{2,1,0:T(8,128)S(1)} %get-tuple-element.26), channel_id=1, source_target_pairs={{0,32},{32,64},{64,96},{96,0},{128,160},{160,192},{192,224},{224,1... | collective-permute-start | bytes 1179656 | tf_op jit(solution)/shard_map/ppermute | solution.py:311
  33.1 3.6 %collective-permute-start.2 = (f32[3,32,1024]{2,1,0:T(8,128)S(1)}, f32[3,32,1024]{2,1,0:T(8,128)S(1)}, u32[]{:S(2)}, u32[]{:S(2)}) collective-permute-start(f32[3,32,1024]{2,1,0:T(8,128)S(1)} %get-tuple-element.27), channel_id=1, source_target_pairs={{0,96},{32,0},{64,32},{96,64},{128,224},{160,128},{192,160},{224,1... | collective-permute-start | bytes 1179656 | tf_op jit(solution)/shard_map/ppermute | solution.py:311
  36.8 3.5 %collective-permute-done.1.low_ref = f32[3,32,1024]{2,1,0:T(8,128)S(1)} collective-permute-done((f32[3,32,1024]{2,1,0:T(8,128)S(1)}, f32[3,32,1024]{2,1,0:T(8,128)S(1)}, u32[]{:S(2)}, u32[]{:S(2)}) %collective-permute-start.1) | collective-permute-done | bytes 393248 | tf_op jit(solution)/shard_map/ppermute | solution.py:311
  40.3 5.3 %collective-permute-done.2.top_ref = f32[3,32,1024]{2,1,0:T(8,128)S(1)} collective-permute-done((f32[3,32,1024]{2,1,0:T(8,128)S(1)}, f32[3,32,1024]{2,1,0:T(8,128)S(1)}, u32[]{:S(2)}, u32[]{:S(2)}) %collective-permute-start.2) | collective-permute-done | bytes 393248 | tf_op jit(solution)/shard_map/ppermute | solution.py:311
  45.6 0.0 copy-done.3
  45.6 0.0 copy-done.4
  45.6 2.0 %sums.1 = (f32[9,32,1024]{2,1,0:T(8,128)}, f32[32,1024]{1,0:T(8,128)S(1)}) custom-call(f32[32,20]{1,0:T(8,128)S(1)} %copy-done.2, f32[9,16,1024]{2,1,0:T(8,128)S(1)} %inner_rows.1.mid_ref, f32[9,16,1024]{2,1,0:T(8,128)S(1)} %get-tuple-element.25.rim_ref, f32[3,32,1024]{2,1,0:T(8,128)S(1)} %collective-permute-done.1.low_ref, ...), custom_call_target="tpu_custom_call" | custom-call | flops 1024 | bytes 1024 | tf_op jit(solution)/shard_map/sums/pallas_call | solution.py:349
  47.6 0.0 collective-permute-done.3.r_mid_ref
  47.6 0.0 collective-permute-done.4.r_rim_ref
  47.6 1.7 %collective-permute-start.7 = (f32[9,32,1024]{2,1,0:T(8,128)}, f32[9,32,1024]{2,1,0:T(8,128)}, u32[]{:S(2)}, u32[]{:S(2)}) collective-permute-start(f32[9,32,1024]{2,1,0:T(8,128)} %get-tuple-element.44), channel_id=1, source_target_pairs={{16,272},{17,273},{18,274},{19,275},{20,276},{21,277},{22,278},{23... | collective-permute-start | bytes 3538952 | tf_op jit(solution)/shard_map/ppermute | solution.py:296
  49.3 0.4 half_way.1
  49.7 0.0 copy-start.6
  49.7 0.0 copy-start.5
  49.7 9.7 %all_to_all.15.parts_ref = f32[8,32,128]{2,1,0:T(8,128)S(1)} all-to-all(f32[8,32,128]{2,1,0:T(8,128)S(1)} %get-tuple-element.32), channel_id=1, replica_groups={{0,32,64,96,128,160,192,224},{256,288,320,352,384,416,448,480},{512,544..., dimensions={0} | all-to-all | bytes 262144 | tf_op jit(solution)/shard_map/all_to_all | solution.py:363
  59.4 0.0 copy-done.6
  59.4 0.6 total_to_all.2
  60.1 36.4 %all-to-all-start.1 = ((f32[4,32,128]{2,1,0:T(8,128)}), f32[4,32,128]{2,1,0:T(8,128)S(1)}, u32[]{:S(2)}, u32[]{:S(2)}) async-start(f32[4,32,128]{2,1,0:T(8,128)} %total_to_all.2), calls=%async_computation.1 | async-start | bytes 131072 | tf_op jit(solution)/shard_map/all_to_all | solution.py:363
  96.4 0.0 collective-permute-done.7.inner_ref
  96.4 0.7 slice_bitcast_fusion
  97.1 23.4 %all-to-all-done.1.parts_ref = f32[4,32,128]{2,1,0:T(8,128)S(1)} async-done(((f32[4,32,128]{2,1,0:T(8,128)}), f32[4,32,128]{2,1,0:T(8,128)S(1)}, u32[]{:S(2)}, u32[]{:S(2)}) %all-to-all-start.1) | async-done | bytes 65568 | tf_op jit(solution)/shard_map/all_to_all | solution.py:363
  120.5 0.7 collective-permute-start.8
  121.1 1.3 collective-permute-start.9
  122.4 0.0 collective-permute-done.8.refs_0_
  122.4 1.7 %collective-permute-start.10 = (f32[9,32,1024]{2,1,0:T(8,128)}, f32[9,32,1024]{2,1,0:T(8,128)}, u32[]{:S(2)}, u32[]{:S(2)}) collective-permute-start(f32[9,32,1024]{2,1,0:T(8,128)} %get-tuple-element.44), channel_id=1, source_target_pairs={{24,280},{25,281},{26,282},{27,283},{28,284},{29,285},{30,286},{31... | collective-permute-start | bytes 3538952 | tf_op jit(solution)/shard_map/ppermute | solution.py:296
  124.1 1.9 %collective-permute-start.6 = (f32[3,32,1024]{2,1,0:T(8,128)}, f32[3,32,1024]{2,1,0:T(8,128)S(1)}, u32[]{:S(2)}, u32[]{:S(2)}) collective-permute-start(f32[3,32,1024]{2,1,0:T(8,128)} %copy-done.6), channel_id=1, source_target_pairs={{0,96},{32,0},{64,32},{96,64},{128,224},{160,128},{192,160},{224,1... | collective-permute-start | bytes 1179656 | tf_op jit(solution)/shard_map/ppermute | solution.py:311
  126.0 0.0 copy-done.5
  126.1 2.4 %collective-permute-start.5 = (f32[3,32,1024]{2,1,0:T(8,128)}, f32[3,32,1024]{2,1,0:T(8,128)S(1)}, u32[]{:S(2)}, u32[]{:S(2)}) collective-permute-start(f32[3,32,1024]{2,1,0:T(8,128)} %copy-done.5), channel_id=1, source_target_pairs={{0,32},{32,64},{64,96},{96,0},{128,160},{160,192},{192,224},{224,1... | collective-permute-start | bytes 1179656 | tf_op jit(solution)/shard_map/ppermute | solution.py:311
  128.5 0.7 total_to_all.3
  129.1 5.2 %all-to-all-start.2 = ((f32[8,32,128]{2,1,0:T(8,128)}), f32[8,32,128]{2,1,0:T(8,128)S(1)}, u32[]{:S(2)}, u32[]{:S(2)}) async-start(f32[8,32,128]{2,1,0:T(8,128)} %total_to_all.3), calls=%async_computation.2 | async-start | bytes 262144 | tf_op jit(solution)/shard_map/all_to_all | solution.py:363
  134.3 0.0 collective-permute-done.6.top_ref
  134.3 1.0 collective-permute-done.5.low_ref
  135.4 3.6 %all-to-all-done.2.energy_ref = f32[8,32,128]{2,1,0:T(8,128)S(1)} async-done(((f32[8,32,128]{2,1,0:T(8,128)}), f32[8,32,128]{2,1,0:T(8,128)S(1)}, u32[]{:S(2)}, u32[]{:S(2)}) %all-to-all-start.2) | async-done | bytes 131104 | tf_op jit(solution)/shard_map/all_to_all | solution.py:363
  139.0 1.2 prepare.1
  140.2 9.3 %collective-permute-done.9.first_ref = f32[9,32,1024]{2,1,0:T(8,128)} collective-permute-done((f32[9,32,1024]{2,1,0:T(8,128)}, f32[9,32,1024]{2,1,0:T(8,128)}, u32[]{:S(2)}, u32[]{:S(2)}) %collective-permute-start.9) | collective-permute-done | bytes 1179680 | tf_op jit(solution)/shard_map/ppermute | solution.py:296
  149.5 0.0 collective-permute-done.10.last_ref
  149.5 2.1 %finish.1 = f32[9,32,1024]{2,1,0:T(8,128)} custom-call(f32[9,32,1024]{2,1,0:T(8,128)S(1)} %get-tuple-element.42.base_ref, f32[9,32,1024]{2,1,0:T(8,128)S(1)} %get-tuple-element.43.coef_ref, f32[9,32,1024]{2,1,0:T(8,128)} %collective-permute-done.9.first_ref, f32[9,32,1024]{2,1,0:T(8,128)} %collective-permute-done.7.inner_ref, ...), custom_call_target="tpu_custom_call" | custom-call | tf_op jit(solution)/shard_map/finish/pallas_call | solution.py:382
  (3 shorter events, 0.0 us)
Async XLA Ops:
  0.0 3.2 %copy-start.2 = (f32[32,20]{1,0:T(8,128)S(1)}, f32[32,20]{1,0:T(8,128)}, u32[]{:S(2)}) copy-start(f32[32,20]{1,0:T(8,128)} %constant.2.clone.table_ref) | copy-start | bytes 7684
  0.0 3.2 %copy-start = (f32[9,32,1024]{2,1,0:T(8,128)S(1)}, f32[9,32,1024]{2,1,0:T(8,128)}, u32[]{:S(2)}) copy-start(f32[9,32,1024]{2,1,0:T(8,128)} %field_ref.3) | copy-start | bytes 3538948
  0.0 3.2 %copy-start.1 = (s32[32,1024]{1,0:T(8,128)S(1)}, s32[32,1024]{1,0:T(8,128)}, u32[]{:S(2)}) copy-start(s32[32,1024]{1,0:T(8,128)} %mask_ref.3) | copy-start | bytes 393220
  1.9 14.6 %collective-permute-start = (f32[40,1024]{1,0:T(8,128)}, f32[40,1024]{1,0:T(8,128)S(1)}, u32[]{:S(2)}, u32[]{:S(2)}) collective-permute-start(f32[40,1024]{1,0:T(8,128)} %edge_rows.1), channel_id=1, source_target_pairs={{0,1},{1,2},{2,3},{3,4},{4,5},{5,6},{6,7},{7,8},{8,9},{9,10},{10,1... | collective-permute-start | bytes 491528 | tf_op jit(solution)/shard_map/ppermute | solution.py:332
  5.4 40.2 %copy-start.3 = (s32[32,1024]{1,0:T(8,128)S(1)}, s32[32,1024]{1,0:T(8,128)}, u32[]{:S(2)}) copy-start(s32[32,1024]{1,0:T(8,128)} %ice_ref.1) | copy-start | bytes 393220
  5.4 40.2 %copy-start.4 = (f32[32,1024]{1,0:T(8,128)S(1)}, f32[32,1024]{1,0:T(8,128)}, u32[]{:S(2)}) copy-start(f32[32,1024]{1,0:T(8,128)} %thick_ref.1) | copy-start | bytes 393220
  5.4 42.2 %collective-permute-start.3 = (f32[9,16,1024]{2,1,0:T(8,128)S(1)}, f32[9,16,1024]{2,1,0:T(8,128)S(1)}, u32[]{:S(2)}, u32[]{:S(2)}) collective-permute-start(f32[9,16,1024]{2,1,0:T(8,128)S(1)} %inner_rows.1.mid_ref), channel_id=1, source_target_pairs={{0,256},{1,257},{2,258},{3,259},{4,260},{5,261},{6,262},{7,263},{8... | collective-permute-start | bytes 1769480 | tf_op jit(solution)/shard_map/ppermute | solution.py:296
  20.3 27.3 %collective-permute-start.4 = (f32[9,16,1024]{2,1,0:T(8,128)S(1)}, f32[9,16,1024]{2,1,0:T(8,128)S(1)}, u32[]{:S(2)}, u32[]{:S(2)}) collective-permute-start(f32[9,16,1024]{2,1,0:T(8,128)S(1)} %get-tuple-element.25.rim_ref), channel_id=1, source_target_pairs={{0,256},{1,257},{2,258},{3,259},{4,260},{5,261},{6,262},{7,263},{8... | collective-permute-start | bytes 1769480 | tf_op jit(solution)/shard_map/ppermute | solution.py:296
  31.2 9.1 %collective-permute-start.1 = (f32[3,32,1024]{2,1,0:T(8,128)S(1)}, f32[3,32,1024]{2,1,0:T(8,128)S(1)}, u32[]{:S(2)}, u32[]{:S(2)}) collective-permute-start(f32[3,32,1024]{2,1,0:T(8,128)S(1)} %get-tuple-element.26), channel_id=1, source_target_pairs={{0,32},{32,64},{64,96},{96,0},{128,160},{160,192},{192,224},{224,1... | collective-permute-start | bytes 1179656 | tf_op jit(solution)/shard_map/ppermute | solution.py:311
  33.1 12.5 %collective-permute-start.2 = (f32[3,32,1024]{2,1,0:T(8,128)S(1)}, f32[3,32,1024]{2,1,0:T(8,128)S(1)}, u32[]{:S(2)}, u32[]{:S(2)}) collective-permute-start(f32[3,32,1024]{2,1,0:T(8,128)S(1)} %get-tuple-element.27), channel_id=1, source_target_pairs={{0,96},{32,0},{64,32},{96,64},{128,224},{160,128},{192,160},{224,1... | collective-permute-start | bytes 1179656 | tf_op jit(solution)/shard_map/ppermute | solution.py:311
  47.6 48.8 %collective-permute-start.7 = (f32[9,32,1024]{2,1,0:T(8,128)}, f32[9,32,1024]{2,1,0:T(8,128)}, u32[]{:S(2)}, u32[]{:S(2)}) collective-permute-start(f32[9,32,1024]{2,1,0:T(8,128)} %get-tuple-element.44), channel_id=1, source_target_pairs={{16,272},{17,273},{18,274},{19,275},{20,276},{21,277},{22,278},{23... | collective-permute-start | bytes 3538952 | tf_op jit(solution)/shard_map/ppermute | solution.py:296
  49.7 9.8 %copy-start.6 = (f32[3,32,1024]{2,1,0:T(8,128)}, f32[3,32,1024]{2,1,0:T(8,128)S(1)}, u32[]{:S(2)}) copy-start(f32[3,32,1024]{2,1,0:T(8,128)S(1)} %get-tuple-element.35) | copy-start | bytes 1179652
  49.7 76.4 %copy-start.5 = (f32[3,32,1024]{2,1,0:T(8,128)}, f32[3,32,1024]{2,1,0:T(8,128)S(1)}, u32[]{:S(2)}) copy-start(f32[3,32,1024]{2,1,0:T(8,128)S(1)} %get-tuple-element.33) | copy-start | bytes 1179652
  60.1 60.4 %all-to-all-start.1 = ((f32[4,32,128]{2,1,0:T(8,128)}), f32[4,32,128]{2,1,0:T(8,128)S(1)}, u32[]{:S(2)}, u32[]{:S(2)}) async-start(f32[4,32,128]{2,1,0:T(8,128)} %total_to_all.2), calls=%async_computation.1 | async-start | bytes 131072 | tf_op jit(solution)/shard_map/all_to_all | solution.py:363
  120.5 2.0 %collective-permute-start.8 = (f32[8,128]{1,0:T(8,128)S(1)}, f32[8,128]{1,0:T(8,128)S(1)}, u32[]{:S(2)}, u32[]{:S(2)}) collective-permute-start(f32[8,128]{1,0:T(8,128)S(1)} %slice_bitcast_fusion), channel_id=1, source_target_pairs={{16,24},{17,25},{18,26},{19,27},{20,28},{21,29},{22,30},{23,31},{4... | collective-permute-start | bytes 12296 | tf_op jit(solution)/shard_map/ppermute | solution.py:304
  121.1 28.4 %collective-permute-start.9 = (f32[9,32,1024]{2,1,0:T(8,128)}, f32[9,32,1024]{2,1,0:T(8,128)}, u32[]{:S(2)}, u32[]{:S(2)}) collective-permute-start(f32[9,32,1024]{2,1,0:T(8,128)} %get-tuple-element.44), channel_id=1, source_target_pairs={{256,0},{257,1},{258,2},{259,3},{260,4},{261,5},{262,6},{263,7},{2... | collective-permute-start | bytes 3538952 | tf_op jit(solution)/shard_map/ppermute | solution.py:296
  122.4 27.0 %collective-permute-start.10 = (f32[9,32,1024]{2,1,0:T(8,128)}, f32[9,32,1024]{2,1,0:T(8,128)}, u32[]{:S(2)}, u32[]{:S(2)}) collective-permute-start(f32[9,32,1024]{2,1,0:T(8,128)} %get-tuple-element.44), channel_id=1, source_target_pairs={{24,280},{25,281},{26,282},{27,283},{28,284},{29,285},{30,286},{31... | collective-permute-start | bytes 3538952 | tf_op jit(solution)/shard_map/ppermute | solution.py:296
  124.1 10.2 %collective-permute-start.6 = (f32[3,32,1024]{2,1,0:T(8,128)}, f32[3,32,1024]{2,1,0:T(8,128)S(1)}, u32[]{:S(2)}, u32[]{:S(2)}) collective-permute-start(f32[3,32,1024]{2,1,0:T(8,128)} %copy-done.6), channel_id=1, source_target_pairs={{0,96},{32,0},{64,32},{96,64},{128,224},{160,128},{192,160},{224,1... | collective-permute-start | bytes 1179656 | tf_op jit(solution)/shard_map/ppermute | solution.py:311
  126.1 9.3 %collective-permute-start.5 = (f32[3,32,1024]{2,1,0:T(8,128)}, f32[3,32,1024]{2,1,0:T(8,128)S(1)}, u32[]{:S(2)}, u32[]{:S(2)}) collective-permute-start(f32[3,32,1024]{2,1,0:T(8,128)} %copy-done.5), channel_id=1, source_target_pairs={{0,32},{32,64},{64,96},{96,0},{128,160},{160,192},{192,224},{224,1... | collective-permute-start | bytes 1179656 | tf_op jit(solution)/shard_map/ppermute | solution.py:311
  129.1 9.9 %all-to-all-start.2 = ((f32[8,32,128]{2,1,0:T(8,128)}), f32[8,32,128]{2,1,0:T(8,128)S(1)}, u32[]{:S(2)}, u32[]{:S(2)}) async-start(f32[8,32,128]{2,1,0:T(8,128)} %total_to_all.3), calls=%async_computation.2 | async-start | bytes 262144 | tf_op jit(solution)/shard_map/all_to_all | solution.py:363

commit v7 on v6

--- a/solution.py
+++ b/solution.py
@@ -58,20 +58,23 @@
         pl.when(place == k)(functools.partial(kernel, k))
 
 
-def edge_rows(first_ref, last_ref, first_mask, last_mask, out_ref):
-    def write(field_ref, mask_ref, low):
-        land = mask_ref[low : low + PSTEPS].astype(jnp.float32)
+def edge_rows(field_ref, mask_ref, out_ref, field, mask, sems):
+    def write(start, low):
+        copies = [
+            pltpu.make_async_copy(field_ref.at[:, pl.ds(start, 8)], field, sems.at[0]),
+            pltpu.make_async_copy(mask_ref.at[pl.ds(start, 8)], mask, sems.at[1]),
+        ]
+        for copy in copies:
+            copy.start()
+        for copy in copies:
+            copy.wait()
+        land = mask[low : low + PSTEPS].astype(jnp.float32)
         for i in range(NQ):
-            out_ref[PSTEPS * i : PSTEPS * (i + 1)] = field_ref[i, low : low + PSTEPS] * land
+            out_ref[PSTEPS * i : PSTEPS * (i + 1)] = field[i, low : low + PSTEPS] * land
         out_ref[PSTEPS * NQ :] = land
 
-    @pl.when(quarter() < 2)
-    def _():
-        write(last_ref, last_mask, 8 - PSTEPS)
-
-    @pl.when(quarter() >= 2)
-    def _():
-        write(first_ref, first_mask, 0)
+    pl.when(quarter() < 2)(lambda: write(field_ref.shape[1] - 8, 8 - PSTEPS))
+    pl.when(quarter() >= 2)(lambda: write(0, 0))
 
 
 def by_quarter(kernel):
@@ -312,17 +315,17 @@
 
     message = pl.pallas_call(
         edge_rows,
-        grid=(1,),
         out_shape=jax.ShapeDtypeStruct((PSTEPS * (comps + 1), cols), jnp.float32),
-        in_specs=[
-            pl.BlockSpec((comps, 8, cols), lambda g: (0, 0, 0)),
-            pl.BlockSpec((comps, 8, cols), lambda g: (0, rows // 8 - 1, 0)),
-            pl.BlockSpec((8, cols), lambda g: (0, 0)),
-            pl.BlockSpec((8, cols), lambda g: (rows // 8 - 1, 0)),
+        in_specs=[pl.BlockSpec(memory_space=pl.ANY)] * 2,
+        out_specs=pl.BlockSpec(memory_space=pltpu.VMEM),
+        scratch_shapes=[
+            pltpu.VMEM((comps, 8, cols), jnp.float32),
+            pltpu.VMEM((8, cols), jnp.int32),
+            pltpu.SemaphoreType.DMA((2,)),
         ],
-        out_specs=pl.BlockSpec((PSTEPS * (comps + 1), cols), lambda g: (0, 0)),
+        compiler_params=pltpu.CompilerParams(vmem_limit_bytes=VMEM_BYTES),
         name="edge_rows",
-    )(spectrum, spectrum, sea_mask, sea_mask)
+    )(spectrum, sea_mask)
     pairs = []
     for p in range(n_comp):
         step = 1 if p % QUARTERS < 2 else -1

time: 152 us -> 153 us (level)
  local copies, waits for them, and re-layouts: 0.72 us -> 7.12 us
  waiting for transfers between devices: 46.2 us -> 43.7 us
  Pallas kernels: 14.7 us -> 12.9 us
    unnamed x14 -> x24, local copies, waits for them, and re-layouts: 0.03 us -> 6.53 us
    pallas_call x1, Pallas kernels: 1.86 us -> 0.11 us  [body(): pl.pallas_call(edge_rows, out_shape=jax.ShapeDtypeStruct((PSTEPS * (comps...]
    ppermute x5, waiting for transfers between devices: 9.29 us -> 7.71 us  [move(): return lax.ppermute(value, ('comp', 'space'), pairs)]
where the time goes in v7:
time: 153 us; the launch traced here: 152 us
  starting transfers between devices  78.5 us (51%)
  waiting for transfers between devices  43.7 us (29%)
  Pallas kernels  12.9 us (8%)
  blocking collectives  9.72 us (6%)
  local copies, waits for them, and re-layouts  7.12 us (5%)
    all_to_all x2, starting transfers between devices, swap(): lax.all_to_all(value, 'comp', 0, 0, axis_index_groups=groups, tiled=True)  40.9 us
    all_to_all x2, waiting for transfers between devices, swap(): lax.all_to_all(value, 'comp', 0, 0, axis_index_groups=groups, tiled=True)  26.9 us
    ppermute x5, starting transfers between devices, move(): return lax.ppermute(value, ('comp', 'space'), pairs)  25.7 us
    ppermute x4, starting transfers between devices, turn(): return lax.ppermute(value, 'comp', pairs)  9.88 us
    all_to_all x1, blocking collectives, swap(): lax.all_to_all(value, 'comp', 0, 0, axis_index_groups=groups, tiled=True)  9.72 us
    ppermute x4, waiting for transfers between devices, turn(): return lax.ppermute(value, 'comp', pairs)  9.12 us
    ppermute x5, waiting for transfers between devices, move(): return lax.ppermute(value, ('comp', 'space'), pairs)  7.71 us
    unnamed x24, local copies, waits for them, and re-layouts  6.53 us
  transfers between devices with their start and end apart: 13, of which 6 were waited for; matrix products, arithmetic and copies ran while one was open for 0% of the time, Pallas kernels for 7%

profile of v7, /device:TPU:6, one launch (start us, length us, event | category | flops | bytes accessed | tf_op | source)
XLA Modules:
  0.0 152.2 jit_solution(16390803911967532569)
XLA Ops:
  0.0 1.3 copy-done
  1.3 0.9 copy-done.2
  2.2 0.1 edge_rows.1
  2.3 1.4 collective-permute-start
  3.7 0.0 copy-done.1
  3.8 2.2 %inner_rows.1.mid_ref = f32[9,16,1024]{2,1,0:T(8,128)S(1)} custom-call(f32[32,20]{1,0:T(8,128)S(1)} %copy-done.4, f32[9,32,1024]{2,1,0:T(8,128)S(1)} %copy-done.1, s32[32,1024]{1,0:T(8,128)S(1)} %copy-done.2), custom_call_target="tpu_custom_call" | custom-call | flops 1024 | bytes 1024 | tf_op jit(solution)/shard_map/inner_rows/pallas_call | solution.py:344
  6.0 0.0 copy-start.6
  6.0 0.0 copy-start.7
  6.0 11.1 %collective-permute-start.3 = (f32[9,16,1024]{2,1,0:T(8,128)S(1)}, f32[9,16,1024]{2,1,0:T(8,128)S(1)}, u32[]{:S(2)}, u32[]{:S(2)}) collective-permute-start(f32[9,16,1024]{2,1,0:T(8,128)S(1)} %inner_rows.1.mid_ref), channel_id=1, source_target_pairs={{0,256},{1,257},{2,258},{3,259},{4,260},{5,261},{6,262},{7,263},{8... | collective-permute-start | bytes 1769480 | tf_op jit(solution)/shard_map/ppermute | solution.py:299
  17.1 0.0 collective-permute-done.halo_ref
  17.1 3.8 %outer_rows.1 = (f32[9,16,1024]{2,1,0:T(8,128)S(1)}, f32[3,32,1024]{2,1,0:T(8,128)S(1)}, f32[3,32,1024]{2,1,0:T(8,128)S(1)}) custom-call(f32[32,20]{1,0:T(8,128)S(1)} %copy-done.4, f32[9,32,1024]{2,1,0:T(8,128)S(1)} %copy-done.1, s32[32,1024]{1,0:T(8,128)S(1)} %copy-done.2, f32[40,1024]{1,0:T(8,128)S(1)} %collective-permute-done.halo_ref, ...), custom_call_target="tpu_custom_call" | custom-call | flops 1024 | bytes 1024 | tf_op jit(solution)/shard_map/outer_rows/pallas_call | solution.py:346
  20.9 10.9 %collective-permute-start.4 = (f32[9,16,1024]{2,1,0:T(8,128)S(1)}, f32[9,16,1024]{2,1,0:T(8,128)S(1)}, u32[]{:S(2)}, u32[]{:S(2)}) collective-permute-start(f32[9,16,1024]{2,1,0:T(8,128)S(1)} %get-tuple-element.25.rim_ref), channel_id=1, source_target_pairs={{0,256},{1,257},{2,258},{3,259},{4,260},{5,261},{6,262},{7,263},{8... | collective-permute-start | bytes 1769480 | tf_op jit(solution)/shard_map/ppermute | solution.py:299
  31.8 1.9 %collective-permute-start.1 = (f32[3,32,1024]{2,1,0:T(8,128)S(1)}, f32[3,32,1024]{2,1,0:T(8,128)S(1)}, u32[]{:S(2)}, u32[]{:S(2)}) collective-permute-start(f32[3,32,1024]{2,1,0:T(8,128)S(1)} %get-tuple-element.26), channel_id=1, source_target_pairs={{0,32},{32,64},{64,96},{96,0},{128,160},{160,192},{192,224},{224,1... | collective-permute-start | bytes 1179656 | tf_op jit(solution)/shard_map/ppermute | solution.py:314
  33.7 3.6 %collective-permute-start.2 = (f32[3,32,1024]{2,1,0:T(8,128)S(1)}, f32[3,32,1024]{2,1,0:T(8,128)S(1)}, u32[]{:S(2)}, u32[]{:S(2)}) collective-permute-start(f32[3,32,1024]{2,1,0:T(8,128)S(1)} %get-tuple-element.27), channel_id=1, source_target_pairs={{0,96},{32,0},{64,32},{96,64},{128,224},{160,128},{192,160},{224,1... | collective-permute-start | bytes 1179656 | tf_op jit(solution)/shard_map/ppermute | solution.py:314
  37.4 3.5 %collective-permute-done.1.low_ref = f32[3,32,1024]{2,1,0:T(8,128)S(1)} collective-permute-done((f32[3,32,1024]{2,1,0:T(8,128)S(1)}, f32[3,32,1024]{2,1,0:T(8,128)S(1)}, u32[]{:S(2)}, u32[]{:S(2)}) %collective-permute-start.1) | collective-permute-done | bytes 393248 | tf_op jit(solution)/shard_map/ppermute | solution.py:314
  40.9 5.3 %collective-permute-done.2.top_ref = f32[3,32,1024]{2,1,0:T(8,128)S(1)} collective-permute-done((f32[3,32,1024]{2,1,0:T(8,128)S(1)}, f32[3,32,1024]{2,1,0:T(8,128)S(1)}, u32[]{:S(2)}, u32[]{:S(2)}) %collective-permute-start.2) | collective-permute-done | bytes 393248 | tf_op jit(solution)/shard_map/ppermute | solution.py:314
  46.2 2.0 %sums.1 = (f32[9,32,1024]{2,1,0:T(8,128)}, f32[32,1024]{1,0:T(8,128)S(1)}) custom-call(f32[32,20]{1,0:T(8,128)S(1)} %copy-done.4, f32[9,16,1024]{2,1,0:T(8,128)S(1)} %inner_rows.1.mid_ref, f32[9,16,1024]{2,1,0:T(8,128)S(1)} %get-tuple-element.25.rim_ref, f32[3,32,1024]{2,1,0:T(8,128)S(1)} %collective-permute-done.1.low_ref, ...), custom_call_target="tpu_custom_call" | custom-call | flops 1024 | bytes 1024 | tf_op jit(solution)/shard_map/sums/pallas_call | solution.py:352
  48.2 0.7 copy-done.8
  48.8 0.0 collective-permute-done.3.r_mid_ref
  48.8 0.0 collective-permute-done.4.r_rim_ref
  48.8 0.7 collective-permute-start.7
  49.5 0.4 half_way.1
  49.9 0.0 copy-start.10
  50.0 0.8 copy-done.10
  50.7 0.7 copy-done.11
  51.4 9.7 %all_to_all.15.parts_ref = f32[8,32,128]{2,1,0:T(8,128)S(1)} all-to-all(f32[8,32,128]{2,1,0:T(8,128)S(1)} %get-tuple-element.32), channel_id=1, replica_groups={{0,32,64,96,128,160,192,224},{256,288,320,352,384,416,448,480},{512,544..., dimensions={0} | all-to-all | bytes 262144 | tf_op jit(solution)/shard_map/all_to_all | solution.py:366
  61.2 0.6 copy-done.5
  61.8 35.7 %all-to-all-start.1 = ((f32[4,32,128]{2,1,0:T(8,128)}), f32[4,32,128]{2,1,0:T(8,128)}, u32[]{:S(2)}, u32[]{:S(2)}) async-start(f32[4,32,128]{2,1,0:T(8,128)} %copy-done.5), calls=%async_computation.1 | async-start | bytes 131072 | tf_op jit(solution)/shard_map/all_to_all | solution.py:366
  97.5 0.0 collective-permute-done.7.inner_ref
  97.5 0.6 slice_bitcast_fusion
  98.1 23.0 %all-to-all-done.1.parts_ref = f32[4,32,128]{2,1,0:T(8,128)} async-done(((f32[4,32,128]{2,1,0:T(8,128)}), f32[4,32,128]{2,1,0:T(8,128)}, u32[]{:S(2)}, u32[]{:S(2)}) %all-to-all-start.1) | async-done | bytes 65568 | tf_op jit(solution)/shard_map/all_to_all | solution.py:366
  121.1 0.7 collective-permute-start.8
  121.8 1.3 collective-permute-start.9
  123.1 0.0 collective-permute-done.8.refs_0_
  123.1 1.7 %collective-permute-start.10 = (f32[9,32,1024]{2,1,0:T(8,128)}, f32[9,32,1024]{2,1,0:T(8,128)}, u32[]{:S(2)}, u32[]{:S(2)}) collective-permute-start(f32[9,32,1024]{2,1,0:T(8,128)} %get-tuple-element.44), channel_id=1, source_target_pairs={{24,280},{25,281},{26,282},{27,283},{28,284},{29,285},{30,286},{31... | collective-permute-start | bytes 3538952 | tf_op jit(solution)/shard_map/ppermute | solution.py:299
  124.8 1.9 %collective-permute-start.6 = (f32[3,32,1024]{2,1,0:T(8,128)}, f32[3,32,1024]{2,1,0:T(8,128)}, u32[]{:S(2)}, u32[]{:S(2)}) collective-permute-start(f32[3,32,1024]{2,1,0:T(8,128)} %copy-done.11), channel_id=1, source_target_pairs={{0,96},{32,0},{64,32},{96,64},{128,224},{160,128},{192,160},{224,1... | collective-permute-start | bytes 1179656 | tf_op jit(solution)/shard_map/ppermute | solution.py:314
  126.7 2.4 %collective-permute-start.5 = (f32[3,32,1024]{2,1,0:T(8,128)}, f32[3,32,1024]{2,1,0:T(8,128)}, u32[]{:S(2)}, u32[]{:S(2)}) collective-permute-start(f32[3,32,1024]{2,1,0:T(8,128)} %copy-done.10), channel_id=1, source_target_pairs={{0,32},{32,64},{64,96},{96,0},{128,160},{160,192},{192,224},{224,1... | collective-permute-start | bytes 1179656 | tf_op jit(solution)/shard_map/ppermute | solution.py:314
  129.1 0.9 total_to_all.3
  130.0 0.7 copy-done.3
  130.6 5.2 %all-to-all-start.2 = ((f32[8,32,128]{2,1,0:T(8,128)}), f32[8,32,128]{2,1,0:T(8,128)}, u32[]{:S(2)}, u32[]{:S(2)}) async-start(f32[8,32,128]{2,1,0:T(8,128)} %copy-done.3), calls=%async_computation.2 | async-start | bytes 262144 | tf_op jit(solution)/shard_map/all_to_all | solution.py:366
  135.8 0.0 collective-permute-done.6.top_ref
  135.8 0.3 collective-permute-done.5.low_ref
  136.1 3.9 %all-to-all-done.2.energy_ref = f32[8,32,128]{2,1,0:T(8,128)} async-done(((f32[8,32,128]{2,1,0:T(8,128)}), f32[8,32,128]{2,1,0:T(8,128)}, u32[]{:S(2)}, u32[]{:S(2)}) %all-to-all-start.2) | async-done | bytes 131104 | tf_op jit(solution)/shard_map/all_to_all | solution.py:366
  140.0 0.9 copy-done.9
  140.9 1.5 %prepare.1 = (f32[9,32,1024]{2,1,0:T(8,128)S(1)}, f32[9,32,1024]{2,1,0:T(8,128)S(1)}) custom-call(f32[32,20]{1,0:T(8,128)S(1)} %copy-done.4, f32[9,16,1024]{2,1,0:T(8,128)S(1)} %inner_rows.1.mid_ref, f32[9,16,1024]{2,1,0:T(8,128)S(1)} %get-tuple-element.25.rim_ref, f32[9,16,1024]{2,1,0:T(8,128)S(1)} %collective-permute-done.3.r_mid_ref, ...), custom_call_target="tpu_custom_call" | custom-call | flops 1024 | bytes 1024 | tf_op jit(solution)/shard_map/prepare/pallas_call | solution.py:381
  142.5 7.7 %collective-permute-done.9.first_ref = f32[9,32,1024]{2,1,0:T(8,128)} collective-permute-done((f32[9,32,1024]{2,1,0:T(8,128)}, f32[9,32,1024]{2,1,0:T(8,128)}, u32[]{:S(2)}, u32[]{:S(2)}) %collective-permute-start.9) | collective-permute-done | bytes 1179680 | tf_op jit(solution)/shard_map/ppermute | solution.py:299
  150.2 0.0 collective-permute-done.10.last_ref
  150.2 2.1 %finish.1 = f32[9,32,1024]{2,1,0:T(8,128)} custom-call(f32[9,32,1024]{2,1,0:T(8,128)S(1)} %get-tuple-element.42.base_ref, f32[9,32,1024]{2,1,0:T(8,128)S(1)} %get-tuple-element.43.coef_ref, f32[9,32,1024]{2,1,0:T(8,128)} %collective-permute-done.9.first_ref, f32[9,32,1024]{2,1,0:T(8,128)S(1)} %collective-permute-done.7.inner_ref, ...), custom_call_target="tpu_custom_call" | custom-call | tf_op jit(solution)/shard_map/finish/pallas_call | solution.py:385
  (13 shorter events, 0.0 us)
Async XLA Ops:
  0.0 1.3 copy-start
  1.3 0.9 copy-start.2
  2.2 1.6 %copy-start.1 = (f32[9,32,1024]{2,1,0:T(8,128)S(1)}, f32[9,32,1024]{2,1,0:T(8,128)}, u32[]{:S(2)}) copy-start(f32[9,32,1024]{2,1,0:T(8,128)} %field_ref.5) | copy-start | bytes 3538948
  2.2 1.6 %copy-start.4 = (f32[32,20]{1,0:T(8,128)S(1)}, f32[32,20]{1,0:T(8,128)}, u32[]{:S(2)}) copy-start(f32[32,20]{1,0:T(8,128)} %constant.2.clone.table_ref) | copy-start | bytes 7684
  2.3 14.8 %collective-permute-start = (f32[40,1024]{1,0:T(8,128)S(1)}, f32[40,1024]{1,0:T(8,128)S(1)}, u32[]{:S(2)}, u32[]{:S(2)}) collective-permute-start(f32[40,1024]{1,0:T(8,128)S(1)} %edge_rows.1), channel_id=1, source_target_pairs={{0,1},{1,2},{2,3},{3,4},{4,5},{5,6},{6,7},{7,8},{8,9},{9,10},{10,1... | collective-permute-start | bytes 491528 | tf_op jit(solution)/shard_map/ppermute | solution.py:335
  6.0 40.2 %copy-start.6 = (s32[32,1024]{1,0:T(8,128)S(1)}, s32[32,1024]{1,0:T(8,128)}, u32[]{:S(2)}) copy-start(s32[32,1024]{1,0:T(8,128)} %ice_ref.1) | copy-start | bytes 393220
  6.0 40.2 %copy-start.7 = (f32[32,1024]{1,0:T(8,128)S(1)}, f32[32,1024]{1,0:T(8,128)}, u32[]{:S(2)}) copy-start(f32[32,1024]{1,0:T(8,128)} %thick_ref.1) | copy-start | bytes 393220
  6.0 42.8 %collective-permute-start.3 = (f32[9,16,1024]{2,1,0:T(8,128)S(1)}, f32[9,16,1024]{2,1,0:T(8,128)S(1)}, u32[]{:S(2)}, u32[]{:S(2)}) collective-permute-start(f32[9,16,1024]{2,1,0:T(8,128)S(1)} %inner_rows.1.mid_ref), channel_id=1, source_target_pairs={{0,256},{1,257},{2,258},{3,259},{4,260},{5,261},{6,262},{7,263},{8... | collective-permute-start | bytes 1769480 | tf_op jit(solution)/shard_map/ppermute | solution.py:299
  20.9 28.0 %collective-permute-start.4 = (f32[9,16,1024]{2,1,0:T(8,128)S(1)}, f32[9,16,1024]{2,1,0:T(8,128)S(1)}, u32[]{:S(2)}, u32[]{:S(2)}) collective-permute-start(f32[9,16,1024]{2,1,0:T(8,128)S(1)} %get-tuple-element.25.rim_ref), channel_id=1, source_target_pairs={{0,256},{1,257},{2,258},{3,259},{4,260},{5,261},{6,262},{7,263},{8... | collective-permute-start | bytes 1769480 | tf_op jit(solution)/shard_map/ppermute | solution.py:299
  31.8 9.1 %collective-permute-start.1 = (f32[3,32,1024]{2,1,0:T(8,128)S(1)}, f32[3,32,1024]{2,1,0:T(8,128)S(1)}, u32[]{:S(2)}, u32[]{:S(2)}) collective-permute-start(f32[3,32,1024]{2,1,0:T(8,128)S(1)} %get-tuple-element.26), channel_id=1, source_target_pairs={{0,32},{32,64},{64,96},{96,0},{128,160},{160,192},{192,224},{224,1... | collective-permute-start | bytes 1179656 | tf_op jit(solution)/shard_map/ppermute | solution.py:314
  33.7 12.5 %collective-permute-start.2 = (f32[3,32,1024]{2,1,0:T(8,128)S(1)}, f32[3,32,1024]{2,1,0:T(8,128)S(1)}, u32[]{:S(2)}, u32[]{:S(2)}) collective-permute-start(f32[3,32,1024]{2,1,0:T(8,128)S(1)} %get-tuple-element.27), channel_id=1, source_target_pairs={{0,96},{32,0},{64,32},{96,64},{128,224},{160,128},{192,160},{224,1... | collective-permute-start | bytes 1179656 | tf_op jit(solution)/shard_map/ppermute | solution.py:314
  48.2 0.7 copy-start.8
  48.8 48.7 %collective-permute-start.7 = (f32[9,32,1024]{2,1,0:T(8,128)}, f32[9,32,1024]{2,1,0:T(8,128)S(1)}, u32[]{:S(2)}, u32[]{:S(2)}) collective-permute-start(f32[9,32,1024]{2,1,0:T(8,128)} %get-tuple-element.44), channel_id=1, source_target_pairs={{16,272},{17,273},{18,274},{19,275},{20,276},{21,277},{22,278},{23... | collective-permute-start | bytes 3538952 | tf_op jit(solution)/shard_map/ppermute | solution.py:299
  49.9 0.8 copy-start.10
  50.7 0.7 copy-start.11
  61.2 0.6 copy-start.5
  61.8 59.3 %all-to-all-start.1 = ((f32[4,32,128]{2,1,0:T(8,128)}), f32[4,32,128]{2,1,0:T(8,128)}, u32[]{:S(2)}, u32[]{:S(2)}) async-start(f32[4,32,128]{2,1,0:T(8,128)} %copy-done.5), calls=%async_computation.1 | async-start | bytes 131072 | tf_op jit(solution)/shard_map/all_to_all | solution.py:366
  121.1 2.0 %collective-permute-start.8 = (f32[8,128]{1,0:T(8,128)}, f32[8,128]{1,0:T(8,128)S(1)}, u32[]{:S(2)}, u32[]{:S(2)}) collective-permute-start(f32[8,128]{1,0:T(8,128)} %slice_bitcast_fusion), channel_id=1, source_target_pairs={{16,24},{17,25},{18,26},{19,27},{20,28},{21,29},{22,30},{23,31},{4... | collective-permute-start | bytes 12296 | tf_op jit(solution)/shard_map/ppermute | solution.py:307
  121.8 28.4 %collective-permute-start.9 = (f32[9,32,1024]{2,1,0:T(8,128)}, f32[9,32,1024]{2,1,0:T(8,128)}, u32[]{:S(2)}, u32[]{:S(2)}) collective-permute-start(f32[9,32,1024]{2,1,0:T(8,128)} %get-tuple-element.44), channel_id=1, source_target_pairs={{256,0},{257,1},{258,2},{259,3},{260,4},{261,5},{262,6},{263,7},{2... | collective-permute-start | bytes 3538952 | tf_op jit(solution)/shard_map/ppermute | solution.py:299
  123.1 27.1 %collective-permute-start.10 = (f32[9,32,1024]{2,1,0:T(8,128)}, f32[9,32,1024]{2,1,0:T(8,128)}, u32[]{:S(2)}, u32[]{:S(2)}) collective-permute-start(f32[9,32,1024]{2,1,0:T(8,128)} %get-tuple-element.44), channel_id=1, source_target_pairs={{24,280},{25,281},{26,282},{27,283},{28,284},{29,285},{30,286},{31... | collective-permute-start | bytes 3538952 | tf_op jit(solution)/shard_map/ppermute | solution.py:299
  124.8 11.1 %collective-permute-start.6 = (f32[3,32,1024]{2,1,0:T(8,128)}, f32[3,32,1024]{2,1,0:T(8,128)}, u32[]{:S(2)}, u32[]{:S(2)}) collective-permute-start(f32[3,32,1024]{2,1,0:T(8,128)} %copy-done.11), channel_id=1, source_target_pairs={{0,96},{32,0},{64,32},{96,64},{128,224},{160,128},{192,160},{224,1... | collective-permute-start | bytes 1179656 | tf_op jit(solution)/shard_map/ppermute | solution.py:314
  126.7 9.4 %collective-permute-start.5 = (f32[3,32,1024]{2,1,0:T(8,128)}, f32[3,32,1024]{2,1,0:T(8,128)}, u32[]{:S(2)}, u32[]{:S(2)}) collective-permute-start(f32[3,32,1024]{2,1,0:T(8,128)} %copy-done.10), channel_id=1, source_target_pairs={{0,32},{32,64},{64,96},{96,0},{128,160},{160,192},{192,224},{224,1... | collective-permute-start | bytes 1179656 | tf_op jit(solution)/shard_map/ppermute | solution.py:314
  130.0 0.7 copy-start.3
  130.6 9.4 %all-to-all-start.2 = ((f32[8,32,128]{2,1,0:T(8,128)}), f32[8,32,128]{2,1,0:T(8,128)}, u32[]{:S(2)}, u32[]{:S(2)}) async-start(f32[8,32,128]{2,1,0:T(8,128)} %copy-done.3), calls=%async_computation.2 | async-start | bytes 262144 | tf_op jit(solution)/shard_map/all_to_all | solution.py:366
  140.0 0.9 copy-start.9
